TPU v7x, 32 devices: a whole 2x2x4 slice. The times are simulated.
32 devices in a mesh: rep: 16 (over z, y, x), tp: 2 (over core).
Axes of the slice: x: 2, y: 2, z: 4, core: 2. Of those that a mesh axis runs over, the one named last changes fastest.
Arguments:
- hidden_input: bfloat16 [16384, 8192], P('rep', 'tp'), may hold values from -6 to 6
- query_weight: bfloat16 [8192, 4096], P('tp'), may hold values from -0.0625 to 0.0625
- slot_down_weight: bfloat16 [64, 8192, 64], P('rep', 'tp'), may hold values from -0.0625 to 0.0625
- slot_up_weight: bfloat16 [64, 64, 4096], P('rep', None, 'tp'), may hold values from -0.75 to 0.75
- request_adapter: int32 [16384, 1], P('rep'), may hold values from 0 to 63; in each aligned block of 1024 rows (0 to 1023, 1024 to 2047, ...) at most 16 rows name the same one
- adapter_slot: int32 [64], replicated, may hold values from 0 to 63, each once
Outputs:
- queries: bfloat16 [16384, 4096], P('rep', 'tp')
Inputs may be any that keep to these rules, and one draw needn't show every extreme that they name: `request_adapter`: within the requests of one index of rep no adapter is named more than 16 times. `adapter_slot`: each slot once; slot s is stored by index s // 4 of rep, at position s % 4.
All inputs are finite; a program needn't handle non-finite values.
Results may differ from a plain program's by a relative error of at most 0.012.
Values may be sent and summed in bfloat16 or wider, within the bound.
No kernel may reach another device: no remote copies, remote signals or barrier semaphores. Data moves between devices by JAX's collectives and lax.ppermute only.
A program may use at most 256 MiB of HBM per device.

v0:
```python
import jax
import jax.numpy as jnp
from jax import lax
from jax.sharding import PartitionSpec as P

MOST = 16


def shards(
    hidden_input, query_weight, slot_down_weight, slot_up_weight, request_adapter, adapter_slot
):
    rows = hidden_input.shape[0]
    local_width = hidden_input.shape[1]
    owned_adapters = slot_down_weight.shape[0]
    output_width = slot_up_weight.shape[2]
    groups = lax.axis_size("rep")
    total = owned_adapters * groups
    limit = MOST
    base_sum = lax.psum_scatter(
        lax.dot_general(
            query_weight, hidden_input, (((0,), (1,)), ((), ())), preferred_element_type=jnp.float32
        ).astype(jnp.bfloat16),
        "tp",
        scatter_dimension=0,
        tiled=True,
    ).astype(jnp.float32)
    ids = request_adapter[:, 0]
    names = lax.broadcasted_iota(jnp.int32, (rows, total), 1)
    slots = jnp.sum(jnp.where(ids[:, None] == names, adapter_slot[None, :], 0), axis=1)
    onehot = (slots[:, None] == names).astype(jnp.bfloat16)
    row_iota = lax.broadcasted_iota(jnp.int32, (rows, rows), 0)
    col_iota = lax.broadcasted_iota(jnp.int32, (rows, rows), 1)
    earlier = (row_iota > col_iota).astype(jnp.bfloat16)
    counts = jnp.dot(earlier, onehot, preferred_element_type=jnp.float32)
    position = jnp.sum(counts * onehot.astype(jnp.float32), axis=1).astype(jnp.int32)
    target = slots * limit + position
    buffer = jnp.zeros((total * limit, local_width), jnp.bfloat16).at[target].set(hidden_input)
    slot_rows = buffer.reshape(total, limit, local_width)
    block = slot_rows
    term = jnp.einsum(
        "amd,adr->amr",
        block,
        lax.all_gather(slot_down_weight, "rep", axis=0, tiled=True),
        preferred_element_type=jnp.float32,
    )
    lowered = term
    lowered = lax.psum(lowered.astype(jnp.bfloat16), "tp")
    block = lowered
    term = jnp.einsum(
        "amr,are->ame",
        block,
        lax.all_gather(slot_up_weight, "rep", axis=0, tiled=True),
        preferred_element_type=jnp.float32,
    )
    lifted = term
    lifted = lifted.astype(jnp.bfloat16).reshape(total * limit, output_width)
    lift_rows = lifted[target]
    return (base_sum.T + lift_rows.astype(jnp.float32)).astype(jnp.bfloat16)


def solution(mesh):
    in_specs = (
        P("rep", "tp"),
        P("tp", None),
        P("rep", "tp", None),
        P("rep", None, "tp"),
        P("rep", None),
        P(),
    )
    out_specs = P("rep", "tp")
    return jax.shard_map(shards, mesh=mesh, in_specs=in_specs, out_specs=out_specs, check_vma=False)
```

profile of v0, /device:TPU:0, one launch (start us, length us, event | category | flops | bytes accessed | tf_op | source)
XLA Modules:
  0.0 624.6 jit_solution(4963572074226123929)
XLA Ops:
  6.5 0.0 all-gather.3.cloned.1.call-start
  6.5 0.7 all-gather.3.cloned.1.call-update
  7.3 0.0 all-gather.5.cloned.1.call-start
  7.3 0.7 all-gather.5.cloned.1.call-update
  8.0 0.0 all-reduce.2.cloned.1.call-start
  8.1 0.8 select_reduce_fusion
  8.9 0.6 fusion.5
  9.5 17.7 %scatter_custom_fusion = bf16[1024,4096]{1,0:T(8,128)(2,1)} fusion(s32[1024]{0:T(1024)S(1)} %bitcast.18, bf16[1024,4096]{1,0:T(8,128)(2,1)} %param.6, bf16[]{:T(256)} %constant.5.clone.1), kind=kCustom, calls=%fused_computation.6 | custom fusion | bytes 8389120 | tf_op jit(solution)/shard_map/scatter | solution.py:37
  27.2 336.5 %all-gather.3.cloned.1.call-done = bf16[64,4096,64]{1,2,0:T(8,128)(2,1)} async-done(((bf16[4,4096,64]{1,2,0:T(8,128)(2,1)}), bf16[64,4096,64]{1,2,0:T(8,128)(2,1)}) %all-gather.3.cloned.1.call-update) | async-done | bytes 33554448 | tf_op jit(solution)/shard_map/all_gather | solution.py:43
  363.7 18.4 %convolution_convert_fusion.2 = bf16[64,16,64]{2,1,0:T(8,128)(2,1)} fusion(bf16[64,16,4096]{2,1,0:T(8,128)(2,1)} %bitcast.16, bf16[64,4096,64]{1,2,0:T(8,128)(2,1)} %all-gather.3.cloned.1.call-done), kind=kOutput, calls=%fused_computation.10 | convolution fusion | flops 536936448 | bytes 42074112 | tf_op jit(solution)/shard_map/amd,adr->amr/dot_general | solution.py:40
  382.2 0.0 all-reduce.2.cloned.1.call-update
  382.2 0.2 reduce-scatter.2.cloned.1.call-start
  382.4 42.7 %convolution_convert_fusion = bf16[4096,1024]{1,0:T(8,128)(2,1)} fusion(bf16[4096,4096]{1,0:T(8,128)(2,1)} %param.7, bf16[1024,4096]{1,0:T(8,128)(2,1)} %param.6), kind=kOutput, calls=%fused_computation.4 | convolution fusion | flops 34363932672 | bytes 50331648 | tf_op jit(solution)/shard_map/dot_general | solution.py:20
  425.1 0.0 reduce-scatter.2.cloned.1.call-update
  425.2 131.2 %all-gather.5.cloned.1.call-done = bf16[64,64,2048]{2,1,0:T(8,128)(2,1)} async-done(((bf16[4,64,2048]{2,1,0:T(8,128)(2,1)}), bf16[64,64,2048]{2,1,0:T(8,128)(2,1)}) %all-gather.5.cloned.1.call-update) | async-done | bytes 16777232 | tf_op jit(solution)/shard_map/all_gather | solution.py:52
  556.3 18.8 %all-reduce.2.cloned.1.call-done = bf16[64,16,64]{2,1,0:T(8,128)(2,1)} async-done(((bf16[64,16,64]{2,1,0:T(8,128)(2,1)}), bf16[64,16,64]{2,1,0:T(8,128)(2,1)}) %all-reduce.2.cloned.1.call-update) | async-done | bytes 131088 | tf_op jit(solution)/shard_map/psum | solution.py:47
  575.1 10.3 %convolution_convert_fusion.1 = bf16[64,16,2048]{2,1,0:T(8,128)(2,1)} fusion(bf16[64,16,64]{2,1,0:T(8,128)(2,1)} %all-reduce.2.cloned.1.call-done, bf16[64,64,2048]{2,1,0:T(8,128)(2,1)} %all-gather.5.cloned.1.call-done), kind=kOutput, calls=%fused_computation.9 | convolution fusion | flops 270532608 | bytes 21102592 | tf_op jit(solution)/shard_map/amr,are->ame/dot_general | solution.py:49
  585.4 12.4 %gather_fusion = bf16[1024,2048]{1,0:T(8,128)(2,1)} fusion(bf16[1024,2048]{1,0:T(8,128)(2,1)} %bitcast.15, s32[1024]{0:T(1024)S(1)} %broadcast_clamp_fusion), kind=kCustom, calls=%fused_computation | custom fusion | bytes 8392704 | tf_op jit(solution)/shard_map/gather | solution.py:57
  597.8 6.4 %copy.13 = bf16[1024,2048]{0,1:T(8,128)(2,1)} copy(bf16[1024,2048]{1,0:T(8,128)(2,1)} %gather_fusion) | data formatting | bytes 8388608 | tf_op jit(solution)/shard_map/gather | solution.py:57
  604.2 0.0 reduce-scatter.2.cloned.1.call-done
  604.2 7.5 %fusion = bf16[1024,2048]{0,1:T(8,128)(2,1)} fusion(bf16[2048,1024]{1,0:T(8,128)(2,1)} %reduce-scatter.2.cloned.1.call-done, bf16[1024,2048]{0,1:T(8,128)(2,1)} %copy.13), kind=kLoop, calls=%fused_computation.3 | loop fusion | flops 8388608 | bytes 12582912 | tf_op jit(solution)/shard_map/convert_element_type | solution.py:58
  611.7 6.4 %copy.14 = bf16[1024,2048]{1,0:T(8,128)(2,1)} copy(bf16[1024,2048]{0,1:T(8,128)(2,1)} %fusion) | data formatting | bytes 8388608 | tf_op jit(solution)/shard_map/convert_element_type | solution.py:58
  (3 shorter events, 0.0 us)
Async XLA Ops:
  6.5 357.2 %all-gather.3.cloned.1.call-start = ((), (), s32[]{:S(2)}) async-start(), calls=%async_computation.2 | async-start | bytes 35651584 | tf_op jit(solution)/shard_map/all_gather | solution.py:43
  7.3 549.1 %all-gather.5.cloned.1.call-start = ((), (), s32[]{:S(2)}) async-start(), calls=%async_computation.4 | async-start | bytes 17825792 | tf_op jit(solution)/shard_map/all_gather | solution.py:52
  8.0 567.1 %all-reduce.2.cloned.1.call-start = ((), (), s32[]{:S(2)}) async-start(), calls=%async_computation.3 | async-start | bytes 524288 | tf_op jit(solution)/shard_map/psum | solution.py:47
  382.2 222.0 %reduce-scatter.2.cloned.1.call-start = ((), (), s32[]{:S(2)}) async-start(), calls=%async_computation.1 | async-start | bytes 12582912 | tf_op jit(solution)/shard_map/reduce_scatter | solution.py:19
Sparse Core Ops, SparseCore 0:
  10.1 353.5 all-gather.2
  366.5 189.7 all-gather.4
  558.7 16.4 all-reduce.1
  577.4 17.9 reduce-scatter.1
where the time goes:
time: 625 us
  waiting for transfers between devices  488 us (78%)
  matrix products  72 us (12%)
  local copies, waits for them, and re-layouts  42.9 us (7%)
  between operations  13.2 us (2%)
  other arithmetic  8.33 us (1%)
    all_gather x1, waiting for transfers between devices, shards(): lax.all_gather(slot_down_weight, 'rep', axis=0, tiled=True)  337 us
    all_gather x1, waiting for transfers between devices, shards(): lax.all_gather(slot_up_weight, 'rep', axis=0, tiled=True)  131 us
    dot_general x1, matrix products, shards(): lax.dot_general(query_weight, hidden_input, (((0,), (1,)), ((), ())), pre...  42.7 us
    psum x1, waiting for transfers between devices, shards(): lowered = lax.psum(lowered.astype(jnp.bfloat16), 'tp')  18.8 us
    gather x2, local copies, waits for them, and re-layouts, shards(): lift_rows = lifted[target]  18.8 us
    dot_general x1, matrix products, shards(): jnp.einsum('amd,adr->amr', block, lax.all_gather(slot_down_weight, 'rep',...  18.4 us
    scatter x1, local copies, waits for them, and re-layouts, shards(): jnp.zeros((total * limit, local_width), jnp.bfloat16).at[target]  17.7 us
  transfers between devices with their start and end apart: 4, of which 3 were waited for; matrix products, arithmetic and copies ran while one was open for 18% of the time, Pallas kernels for 0%

commit v1 on v0

v1 whole, which is shorter than its diff:
```python
import functools

import jax
import jax.numpy as jnp
from jax import lax
from jax.experimental import pallas as pl
from jax.experimental.pallas import tpu as pltpu
from jax.sharding import PartitionSpec as P

MOST = 16
COLUMNS = 4
PLANES = 4
SWAP = [(0, 1), (1, 0)]
LIMIT = 56 * 1024 * 1024
NT = (((1,), (1,)), ((), ()))


def params(steps=1):
    return pltpu.CompilerParams(dimension_semantics=("arbitrary",) * steps, vmem_limit_bytes=LIMIT)


def cost(flops, size):
    return pl.CostEstimate(flops=flops, bytes_accessed=size, transcendentals=0)


def pack_kernel(target_ref, x_ref, *rest):
    outs, onehot = rest[:-1], rest[-1]
    size = onehot.shape[0]

    @pl.when(pl.program_id(0) == 0)
    def _():
        place = lax.broadcasted_iota(jnp.int32, onehot.shape, 0)
        onehot[...] = (place == target_ref[...]).astype(jnp.bfloat16)

    packed = jnp.dot(onehot[...], x_ref[...], preferred_element_type=jnp.float32).astype(jnp.bfloat16)
    part = size // len(outs)
    for k, out in enumerate(outs):
        out[...] = packed[k * part : (k + 1) * part]


def pack(target, x, parts):
    rows, width = x.shape
    tile = 512
    part = rows // parts
    return pl.pallas_call(
        pack_kernel,
        grid=(width // tile,),
        in_specs=[pl.BlockSpec((1, rows), lambda i: (0, 0)), pl.BlockSpec((rows, tile), lambda i: (0, i))],
        out_specs=[pl.BlockSpec((part, tile), lambda i: (0, i))] * parts,
        out_shape=[jax.ShapeDtypeStruct((part, width), x.dtype)] * parts,
        scratch_shapes=[pltpu.VMEM((rows, rows), jnp.bfloat16)],
        compiler_params=params(),
        cost_estimate=cost(2 * rows * rows * width, 4 * rows * width),
        name="pack_rows",
    )(target, x)


def project_kernel(place_ref, x_ref, w_ref, o_ref):
    o_ref[...] = jnp.dot(x_ref[...], w_ref[...], preferred_element_type=jnp.float32).astype(o_ref.dtype)


def project(half, x, w):
    rows, width = x.shape
    columns = w.shape[1] // 2
    tile = 256
    steps = columns // tile
    return pl.pallas_call(
        project_kernel,
        grid_spec=pltpu.PrefetchScalarGridSpec(
            num_scalar_prefetch=1,
            grid=(steps,),
            in_specs=[
                pl.BlockSpec((rows, width), lambda i, place: (0, 0)),
                pl.BlockSpec((width, tile), lambda i, place: (0, place[0] * steps + i)),
            ],
            out_specs=pl.BlockSpec((rows, tile), lambda i, place: (0, i)),
        ),
        out_shape=jax.ShapeDtypeStruct((rows, columns), jnp.bfloat16),
        compiler_params=params(),
        cost_estimate=cost(2 * rows * width * columns, 2 * (rows * width + columns * width + rows * columns)),
        name="project_half",
    )(half.reshape(1), x, w)


def down_kernel(*refs):
    xs, w_ref, o_ref = refs[:-2], refs[-2], refs[-1]
    rows = jnp.concatenate([x[...] for x in xs], axis=0)
    o_ref[...] = lax.dot_general(rows, w_ref[...], NT, preferred_element_type=jnp.float32)


def down(xs, w, start):
    adapters, rank, width = w.shape
    return pl.pallas_call(
        down_kernel,
        grid=(adapters,),
        in_specs=[pl.BlockSpec((MOST, width), lambda i: (start + i, 0))] * len(xs)
        + [pl.BlockSpec((None, rank, width), lambda i: (i, 0, 0))],
        out_specs=pl.BlockSpec((None, len(xs) * MOST, rank), lambda i: (i, 0, 0)),
        out_shape=jax.ShapeDtypeStruct((adapters, len(xs) * MOST, rank), jnp.float32),
        compiler_params=params(),
        cost_estimate=cost(
            2 * adapters * len(xs) * MOST * rank * width, 2 * adapters * width * (rank + len(xs) * MOST)
        ),
        name="down_rows",
    )(*xs, w)


def lift_kernel(y_ref, u_ref, *outs):
    rows = jnp.dot(y_ref[...], u_ref[...], preferred_element_type=jnp.float32).astype(jnp.bfloat16)
    for k, out in enumerate(outs):
        out[...] = rows[k * MOST : (k + 1) * MOST]


def lift(y, u):
    adapters, rank, columns = u.shape
    rows = y.shape[1]
    parts = rows // MOST
    return pl.pallas_call(
        lift_kernel,
        grid=(adapters,),
        in_specs=[
            pl.BlockSpec((None, rows, rank), lambda i: (i, 0, 0)),
            pl.BlockSpec((None, rank, columns), lambda i: (i, 0, 0)),
        ],
        out_specs=[pl.BlockSpec((MOST, columns), lambda i: (i, 0))] * parts,
        out_shape=[jax.ShapeDtypeStruct((adapters * MOST, columns), jnp.bfloat16)] * parts,
        compiler_params=params(),
        cost_estimate=cost(2 * adapters * rows * rank * columns, 2 * adapters * columns * (rank + rows)),
        name="lift_rows",
    )(y, u)


def finish_kernel(target_ref, own_ref, other_ref, *rest):
    pieces, o_ref, onehot = rest[:-2], rest[-2], rest[-1]

    @pl.when(pl.program_id(0) == 0)
    def _():
        place = lax.broadcasted_iota(jnp.int32, onehot.shape, 1)
        onehot[...] = (place == target_ref[...]).astype(jnp.bfloat16)

    lifted = jnp.concatenate([piece[...] for piece in pieces], axis=0)
    total = jnp.dot(onehot[...], lifted, preferred_element_type=jnp.float32)
    base = own_ref[...].astype(jnp.float32) + other_ref[...].astype(jnp.float32)
    o_ref[...] = (base + total).astype(o_ref.dtype)


def finish(target, own, other, pieces):
    rows, columns = own.shape
    tile = 512
    places = sum(piece.shape[0] for piece in pieces)
    return pl.pallas_call(
        finish_kernel,
        grid=(columns // tile,),
        in_specs=[pl.BlockSpec((rows, 1), lambda i: (0, 0))]
        + [pl.BlockSpec((rows, tile), lambda i: (0, i))] * 2
        + [pl.BlockSpec((piece.shape[0], tile), lambda i: (0, i)) for piece in pieces],
        out_specs=pl.BlockSpec((rows, tile), lambda i: (0, i)),
        out_shape=jax.ShapeDtypeStruct((rows, columns), jnp.bfloat16),
        scratch_shapes=[pltpu.VMEM((rows, places), jnp.bfloat16)],
        compiler_params=params(),
        cost_estimate=cost(2 * rows * places * columns, 8 * rows * columns),
        name="finish_rows",
    )(target, own, other, *pieces)


def places(request_adapter, adapter_slot, total):
    rows = request_adapter.shape[0]
    ids = request_adapter[:, 0]
    names = lax.broadcasted_iota(jnp.int32, (rows, total), 1)
    slots = jnp.sum(jnp.where(ids[:, None] == names, adapter_slot[None, :], 0), axis=1)
    onehot = (slots[:, None] == names).astype(jnp.bfloat16)
    row_iota = lax.broadcasted_iota(jnp.int32, (rows, rows), 0)
    col_iota = lax.broadcasted_iota(jnp.int32, (rows, rows), 1)
    earlier = (row_iota > col_iota).astype(jnp.bfloat16)
    counts = jnp.dot(earlier, onehot, preferred_element_type=jnp.float32)
    position = jnp.sum(counts * onehot.astype(jnp.float32), axis=1).astype(jnp.int32)
    return slots, position


def by_planes(hidden_input, query_weight, slot_down_weight, slot_up_weight, request_adapter, adapter_slot):
    owned = slot_down_weight.shape[0]
    group = owned * MOST
    me = lax.axis_index("rep")
    plane, column = me // COLUMNS, me % COLUMNS
    inner = (plane == 1) | (plane == 2)
    every = range(COLUMNS * PLANES)
    inside = [r for r in every if r // COLUMNS in (1, 2)]
    outside = [r for r in every if r // COLUMNS in (0, 3)]

    def send(x, pairs):
        return lax.ppermute(x, "rep", pairs)

    pair = [(r, r ^ 4) for r in every]
    across = [(r, r ^ 12) for r in inside]
    outward = [(r, r ^ 4) for r in inside]
    turn = [[(r, r ^ d) for r in every] for d in range(COLUMNS)]
    turn_inside = [[(r, r ^ d) for r in inside] for d in range(COLUMNS)]
    turn_inward = [[(r, r ^ 4 ^ d) for r in outside] for d in range(COLUMNS)]

    down_own = jnp.swapaxes(slot_down_weight, 1, 2)
    up_own = slot_up_weight
    down_pair = send(down_own, pair)
    down_near = send(down_own, across)

    slots, position = places(request_adapter, adapter_slot, owned * COLUMNS * PLANES)
    slot_plane = slots // (owned * COLUMNS)
    slot_column = slots // owned % COLUMNS
    far = slot_plane // 2 != plane // 2
    second = jnp.where(far, (slot_plane == 0) | (slot_plane == 3), slot_plane != plane).astype(jnp.int32)
    order = (far.astype(jnp.int32) * COLUMNS + (slot_column ^ column)) * 2 + second
    target = order * group + slots % owned * MOST + position

    packed = pack(target[None, :], hidden_input, 2 * COLUMNS)
    home, away = packed[:COLUMNS], packed[COLUMNS:]
    inward = [send(away[d], turn_inward[d]) for d in range(COLUMNS)]
    beside = [away[0]] + [send(away[d], turn_inside[d]) for d in range(1, COLUMNS)]
    local = [home[0]] + [send(home[d], turn[d]) for d in range(1, COLUMNS)]
    down_far = send(down_pair, across)

    up_pair = send(up_own, pair)
    up_near = send(up_own, across)
    up_far = send(up_pair, across)
    up_near_out = send(up_near, outward)
    up_far_out = send(up_far, outward)
    up_near = jnp.where(inner, up_near, up_near_out)
    up_far = jnp.where(inner, up_far, up_far_out)

    tp = lax.axis_index("tp")
    given = project(1 - tp, hidden_input, query_weight)
    base_other = lax.ppermute(given, "tp", SWAP)
    base_own = project(tp, hidden_input, query_weight)

    def both(y):
        return (y + lax.ppermute(y, "tp", SWAP)).astype(jnp.bfloat16)

    half = COLUMNS * MOST
    lowered = [both(down(local, down_own, 0)), both(down(local, down_pair, owned))]
    for weight, start in ((down_near, 0), (down_far, owned)):
        y = both(down(beside + inward, weight, start))
        lowered.append(jnp.where(inner, y[:, :half], send(y[:, half:], outward)))
    lifted = []
    for y, u in zip(lowered, (up_own, up_pair, up_near, up_far)):
        rows = lift(y, u)
        lifted.append([rows[0]] + [send(rows[d], turn[d]) for d in range(1, COLUMNS)])
    pieces = [lifted[2 * f + s][d] for f in range(2) for d in range(COLUMNS) for s in range(2)]
    return finish(target[:, None], base_own, base_other, pieces)


def by_gather(hidden_input, query_weight, slot_down_weight, slot_up_weight, request_adapter, adapter_slot):
    local_width = hidden_input.shape[1]
    output_width = slot_up_weight.shape[2]
    total = slot_down_weight.shape[0] * lax.axis_size("rep")
    base_sum = lax.psum_scatter(
        lax.dot_general(
            query_weight, hidden_input, (((0,), (1,)), ((), ())), preferred_element_type=jnp.float32
        ).astype(jnp.bfloat16),
        "tp",
        scatter_dimension=0,
        tiled=True,
    ).astype(jnp.float32)
    slots, position = places(request_adapter, adapter_slot, total)
    target = slots * MOST + position
    buffer = jnp.zeros((total * MOST, local_width), jnp.bfloat16).at[target].set(hidden_input)
    slot_rows = buffer.reshape(total, MOST, local_width)
    lowered = jnp.einsum(
        "amd,adr->amr",
        slot_rows,
        lax.all_gather(slot_down_weight, "rep", axis=0, tiled=True),
        preferred_element_type=jnp.float32,
    )
    lowered = lax.psum(lowered.astype(jnp.bfloat16), "tp")
    lifted = jnp.einsum(
        "amr,are->ame",
        lowered,
        lax.all_gather(slot_up_weight, "rep", axis=0, tiled=True),
        preferred_element_type=jnp.float32,
    )
    lift_rows = lifted.astype(jnp.bfloat16).reshape(total * MOST, output_width)[target]
    return (base_sum.T + lift_rows.astype(jnp.float32)).astype(jnp.bfloat16)


def solution(mesh):
    in_specs = (
        P("rep", "tp"),
        P("tp", None),
        P("rep", "tp", None),
        P("rep", None, "tp"),
        P("rep", None),
        P(),
    )
    out_specs = P("rep", "tp")
    planes = mesh.shape["rep"] == COLUMNS * PLANES and mesh.shape["tp"] == 2
    shards = by_planes if planes else by_gather
    return jax.shard_map(shards, mesh=mesh, in_specs=in_specs, out_specs=out_specs, check_vma=False)
```

time: 625 us -> 387 us (0.62)
  waiting for transfers between devices: 488 us -> 104 us
  starting transfers between devices: 0.3 us -> 164 us
  Pallas kernels: 0 us -> 104 us
  matrix products: 72 us -> 0.59 us
  local copies, waits for them, and re-layouts: 42.9 us -> 2.34 us
  between operations: 13.2 us -> 0.64 us
    all_gather x2 -> x0, waiting for transfers between devices: 468 us -> none  [the longest x1 337 us: shards(): lax.all_gather(slot_down_weight, 'rep', axis=0, tiled=True)]
    ppermute x0 -> x37, starting transfers between devices: none -> 164 us  [the longest x32 162 us: send(): return lax.ppermute(x, 'rep', pairs)]
    ppermute x0 -> x37, waiting for transfers between devices: none -> 104 us  [the longest x32 104 us: send(): return lax.ppermute(x, 'rep', pairs)]
    pallas_call x0 -> x12, Pallas kernels: none -> 104 us  [the longest x2 47.3 us: project(): pl.pallas_call(project_kernel, grid_spec=pltpu.PrefetchScalarGridSpec(num...]
    dot_general x4 -> x1, matrix products: 72 us -> 0.59 us  [places(): counts = jnp.dot(earlier, onehot, preferred_element_type=jnp.float32)]
    psum x1 -> x0, waiting for transfers between devices: 18.8 us -> none  [shards(): lowered = lax.psum(lowered.astype(jnp.bfloat16), 'tp')]
    gather x2 -> x0, local copies, waits for them, and re-layouts: 18.8 us -> none  [shards(): lift_rows = lifted[target]]
    scatter x1 -> x0, local copies, waits for them, and re-layouts: 17.7 us -> none  [shards(): jnp.zeros((total * limit, local_width), jnp.bfloat16).at[target]]
  transfers between devices with their start and end apart: 4 -> 37, of which waited for: 3 -> 9; matrix products, arithmetic and copies ran while one was open for 18% -> 2% of each run, Pallas kernels for 0% -> 21%
where the time goes in v1:
time: 387 us; the launch traced here: 386 us
  starting transfers between devices  164 us (42%)
  Pallas kernels  104 us (27%)
  waiting for transfers between devices  104 us (27%)
  other arithmetic  10.6 us (3%)
    ppermute x32, starting transfers between devices, send(): return lax.ppermute(x, 'rep', pairs)  162 us
    ppermute x32, waiting for transfers between devices, send(): return lax.ppermute(x, 'rep', pairs)  104 us
    pallas_call x2, Pallas kernels, project(): pl.pallas_call(project_kernel, grid_spec=pltpu.PrefetchScalarGridSpec(num...  47.3 us
    pallas_call x4, Pallas kernels, down(): pl.pallas_call(down_kernel, grid=(adapters,), in_specs=[pl.BlockSpec((MOS...  18.9 us
    pallas_call x4, Pallas kernels, lift(): pl.pallas_call(lift_kernel, grid=(adapters,), in_specs=[pl.BlockSpec((Non...  15 us
    pallas_call x1, Pallas kernels, pack(): pl.pallas_call(pack_kernel, grid=(width // tile,), in_specs=[pl.BlockSpec...  13 us
    pallas_call x1, Pallas kernels, finish(): pl.pallas_call(finish_kernel, grid=(columns // tile,), in_specs=[pl.Block...  9.67 us
  transfers between devices with their start and end apart: 37, of which 9 were waited for; matrix products, arithmetic and copies ran while one was open for 2% of the time, Pallas kernels for 21%

profile of v1, /device:TPU:0, one launch (start us, length us, event | category | flops | bytes accessed | tf_op | source)
XLA Modules:
  0.0 385.7 jit_solution(5557267619531606306)
XLA Ops:
  0.0 0.8 select_reduce_fusion
  2.1 13.0 %pack_rows.1 = (bf16[128,4096]{1,0:T(8,128)(2,1)}, bf16[128,4096]{1,0:T(8,128)(2,1)}, bf16[128,4096]{1,0:T(8,128)(2,1)}, bf16[128,4096]{1,0:T(8,128)(2,1)}, bf16...) custom-call(s32[1,1024]{1,0:T(1,128)} %fusion.25.target_ref, ...), custom_call_target="tpu_custom_call" | custom-call | flops 8589934592 | bytes 16777216 | tf_op jit(solution)/shard_map/pack_rows/pallas_call | solution.py:45
  16.6 3.0 collective-permute-start.1
  19.6 1.5 collective-permute-start.2
  21.1 1.7 collective-permute-start.16
  22.8 30.8 %collective-permute-start.17 = (bf16[128,4096]{1,0:T(8,128)(2,1)}, bf16[128,4096]{1,0:T(8,128)(2,1)}, u32[]{:S(2)}, u32[]{:S(2)}) collective-permute-start(bf16[128,4096]{1,0:T(8,128)(2,1)} %get-tuple-element.41.refs_0_), channel_id=1, source_target_pairs={{0,8},{2,10},{4,12},{6,14},{24,16},{26,18},{28,20},{30,22},{1,9},{... | collective-permute-start | bytes 3145736 | tf_op jit(solution)/shard_map/ppermute | solution.py:191
  53.6 19.0 %collective-permute-start.18 = (bf16[128,4096]{1,0:T(8,128)(2,1)}, bf16[128,4096]{1,0:T(8,128)(2,1)}, u32[]{:S(2)}, u32[]{:S(2)}) collective-permute-start(bf16[128,4096]{1,0:T(8,128)(2,1)} %get-tuple-element.42), channel_id=1, source_target_pairs={{0,10},{2,8},{4,14},{6,12},{24,18},{26,16},{28,22},{30,20},{1,11},... | collective-permute-start | bytes 3145736 | tf_op jit(solution)/shard_map/ppermute | solution.py:191
  72.6 9.8 %collective-permute-start.19 = (bf16[128,4096]{1,0:T(8,128)(2,1)}, bf16[128,4096]{1,0:T(8,128)(2,1)}, u32[]{:S(2)}, u32[]{:S(2)}) collective-permute-start(bf16[128,4096]{1,0:T(8,128)(2,1)} %get-tuple-element.43), channel_id=1, source_target_pairs={{0,12},{2,14},{4,8},{6,10},{24,20},{26,22},{28,16},{30,18},{1,13},... | collective-permute-start | bytes 3145736 | tf_op jit(solution)/shard_map/ppermute | solution.py:191
  82.4 47.3 %collective-permute-start.5 = (bf16[4,64,4096]{2,1,0:T(8,128)(2,1)}, bf16[4,64,4096]{2,1,0:T(8,128)(2,1)}, u32[]{:S(2)}, u32[]{:S(2)}) collective-permute-start(bf16[4,64,4096]{2,1,0:T(8,128)(2,1)} %bitcast.7.refs_4_), channel_id=1, source_target_pairs={{0,8},{2,10},{4,12},{6,14},{8,0},{10,2},{12,4},{14,6},{16,24},{18,... | collective-permute-start | bytes 6291464 | tf_op jit(solution)/shard_map/ppermute | solution.py:191
  129.7 4.5 %down_rows.4 = f32[4,64,64]{2,1,0:T(8,128)} custom-call(bf16[128,4096]{1,0:T(8,128)(2,1)} %get-tuple-element.29.refs_0_, bf16[128,4096]{1,0:T(8,128)(2,1)} %copy-done, bf16[128,4096]{1,0:T(8,128)(2,1)} %copy-done.1, bf16[128,4096]{1,0:T(8,128)(2,1)} %copy-done.2, bf16[4,64,4096]{2,1,0:T(8,128)(2,1)} %bitcast.7.refs_4_), custom_call_target="tpu_custom_call" | custom-call | flops 134217728 | bytes 4194304 | tf_op jit(solution)/shard_map/down_rows/pallas_call | solution.py:93
  134.2 23.7 %collective-permute-start.20 = (bf16[128,4096]{1,0:T(8,128)(2,1)S(1)}, bf16[128,4096]{1,0:T(8,128)(2,1)S(1)}, u32[]{:S(2)}, u32[]{:S(2)}) collective-permute-start(bf16[128,4096]{1,0:T(8,128)(2,1)S(1)} %copy-done.23), channel_id=1, source_target_pairs={{0,14},{2,12},{4,10},{6,8},{24,22},{26,20},{28,18},{30,16},{1,15},... | collective-permute-start | bytes 3145736 | tf_op jit(solution)/shard_map/ppermute | solution.py:191
  158.1 1.7 collective-permute-start.24
  159.7 23.6 %project_half.3 = bf16[1024,2048]{1,0:T(8,128)(2,1)} custom-call(s32[1]{0:T(128)} %bitcast.4.place_ref, bf16[1024,4096]{1,0:T(8,128)(2,1)} %x_ref.5, bf16[4096,4096]{1,0:T(8,128)(2,1)} %w_ref.3), custom_call_target="tpu_custom_call" | custom-call | flops 17179869184 | bytes 29360128 | tf_op jit(solution)/shard_map/project_half/pallas_call | solution.py:67
  183.3 20.4 %collective-permute-done.20.refs_7_ = bf16[128,4096]{1,0:T(8,128)(2,1)S(1)} collective-permute-done((bf16[128,4096]{1,0:T(8,128)(2,1)S(1)}, bf16[128,4096]{1,0:T(8,128)(2,1)S(1)}, u32[]{:S(2)}, u32[]{:S(2)}) %collective-permute-start.20) | collective-permute-done | bytes 1048608 | tf_op jit(solution)/shard_map/ppermute | solution.py:191
  203.8 2.1 collective-permute-start.21
  205.8 17.4 %collective-permute-done.7.u_ref = bf16[4,64,2048]{2,1,0:T(8,128)(2,1)} collective-permute-done((bf16[4,64,2048]{2,1,0:T(8,128)(2,1)S(1)}, bf16[4,64,2048]{2,1,0:T(8,128)(2,1)}, u32[]{:S(2)}, u32[]{:S(2)}) %collective-permute-start.7) | collective-permute-done | bytes 1048608 | tf_op jit(solution)/shard_map/ppermute | solution.py:191
  223.2 1.6 collective-permute-start.29
  224.9 1.3 collective-permute-start.25
  227.0 23.7 %project_half.2.own_ref = bf16[1024,2048]{1,0:T(8,128)(2,1)} custom-call(s32[1]{0:T(128)} %bitcast.3.place_ref, bf16[1024,4096]{1,0:T(8,128)(2,1)} %x_ref.5, bf16[4096,4096]{1,0:T(8,128)(2,1)} %w_ref.3), custom_call_target="tpu_custom_call" | custom-call | flops 17179869184 | bytes 29360128 | tf_op jit(solution)/shard_map/project_half/pallas_call | solution.py:67
  251.8 3.8 lift_rows.4
  255.6 4.4 %down_rows.5 = f32[4,64,64]{2,1,0:T(8,128)} custom-call(bf16[128,4096]{1,0:T(8,128)(2,1)} %get-tuple-element.29.refs_0_, bf16[128,4096]{1,0:T(8,128)(2,1)} %copy-done, bf16[128,4096]{1,0:T(8,128)(2,1)} %copy-done.1, bf16[128,4096]{1,0:T(8,128)(2,1)} %copy-done.2, bf16[4,64,4096]{2,1,0:T(8,128)(2,1)} %collective-permute-done.5.refs_4_), custom_call_target="tpu_custom_call" | custom-call | flops 134217728 | bytes 4194304 | tf_op jit(solution)/shard_map/down_rows/pallas_call | solution.py:93
  260.5 1.3 collective-permute-start.30
  261.8 2.3 broadcast_select_fusion.1.u_ref
  264.1 2.6 collective-permute-start.10
  266.7 5.0 %down_rows.6 = f32[4,128,64]{2,1,0:T(8,128)} custom-call(bf16[128,4096]{1,0:T(8,128)(2,1)} %get-tuple-element.41.refs_0_, bf16[128,4096]{1,0:T(8,128)(2,1)} %copy-done.3, bf16[128,4096]{1,0:T(8,128)(2,1)} %copy-done.4, bf16[128,4096]{1,0:T(8,128)(2,1)} %collective-permute-done.16.refs_3_, bf16[128,4096]{1,0:T(8,128)(2,1)} %collective-permute-done.17.refs_4_, ...), custom_call_target="tpu_custom_call" | custom-call | flops 268435456 | bytes 6291456 | tf_op jit(solution)/shard_map/down_rows/pallas_call | solution.py:93
  272.5 3.7 lift_rows.5
  276.4 1.2 copy-done.6
  277.5 5.0 %down_rows.7 = f32[4,128,64]{2,1,0:T(8,128)} custom-call(bf16[128,4096]{1,0:T(8,128)(2,1)} %get-tuple-element.41.refs_0_, bf16[128,4096]{1,0:T(8,128)(2,1)} %copy-done.3, bf16[128,4096]{1,0:T(8,128)(2,1)} %copy-done.4, bf16[128,4096]{1,0:T(8,128)(2,1)} %collective-permute-done.16.refs_3_, bf16[128,4096]{1,0:T(8,128)(2,1)} %collective-permute-done.17.refs_4_, ...), custom_call_target="tpu_custom_call" | custom-call | flops 268435456 | bytes 6291456 | tf_op jit(solution)/shard_map/down_rows/pallas_call | solution.py:93
  283.5 2.4 collective-permute-done.12.rest_6_
  286.0 1.3 collective-permute-start.23
  287.3 1.0 add_convert_fusion
  288.3 44.2 %collective-permute-done.23 = bf16[4,64,64]{2,1,0:T(8,128)(2,1)S(1)} collective-permute-done((bf16[4,64,64]{2,1,0:T(8,128)(2,1)S(1)}, bf16[4,64,64]{2,1,0:T(8,128)(2,1)S(1)}, u32[]{:S(2)}, u32[]{:S(2)}) %collective-permute-start.23) | collective-permute-done | bytes 32800 | tf_op jit(solution)/shard_map/ppermute | solution.py:191
  332.5 1.5 collective-permute-start.28
  334.6 3.8 lift_rows.6
  338.4 1.7 collective-permute-start.13
  340.2 1.3 collective-permute-start.9
  342.3 1.6 collective-permute-start.33
  343.8 1.1 broadcast_select_fusion.u_ref
  345.5 3.7 lift_rows.7
  349.3 1.3 collective-permute-start.35
  350.5 3.8 collective-permute-done.9.rest_3_
  355.0 4.9 %collective-permute-done.31.rest_10_ = bf16[64,2048]{1,0:T(8,128)(2,1)S(1)} collective-permute-done((bf16[64,2048]{1,0:T(8,128)(2,1)}, bf16[64,2048]{1,0:T(8,128)(2,1)S(1)}, u32[]{:S(2)}, u32[]{:S(2)}) %collective-permute-start.31) | collective-permute-done | bytes 262176 | tf_op jit(solution)/shard_map/ppermute | solution.py:191
  360.5 1.6 collective-permute-start.36
  362.1 2.2 fusion.13.target_ref
  364.3 1.3 collective-permute-done.35.rest_14_
  365.6 5.6 %collective-permute-done.32.rest_11_ = bf16[64,2048]{1,0:T(8,128)(2,1)S(1)} collective-permute-done((bf16[64,2048]{1,0:T(8,128)(2,1)}, bf16[64,2048]{1,0:T(8,128)(2,1)S(1)}, u32[]{:S(2)}, u32[]{:S(2)}) %collective-permute-start.32) | collective-permute-done | bytes 262176 | tf_op jit(solution)/shard_map/ppermute | solution.py:191
  371.2 4.0 %collective-permute-done.36.rest_15_ = bf16[64,2048]{1,0:T(8,128)(2,1)S(1)} collective-permute-done((bf16[64,2048]{1,0:T(8,128)(2,1)}, bf16[64,2048]{1,0:T(8,128)(2,1)S(1)}, u32[]{:S(2)}, u32[]{:S(2)}) %collective-permute-start.36) | collective-permute-done | bytes 262176 | tf_op jit(solution)/shard_map/ppermute | solution.py:191
  375.9 9.7 %finish_rows.1 = bf16[1024,2048]{1,0:T(8,128)(2,1)} custom-call(s32[1024,1]{1,0:T(8,128)} %fusion.13.target_ref, bf16[1024,2048]{1,0:T(8,128)(2,1)} %project_half.2.own_ref, bf16[1024,2048]{1,0:T(8,128)(2,1)} %collective-permute-done.other_ref, bf16[64,2048]{1,0:T(8,128)(2,1)} %get-tuple-element.33.rest_0_, bf16[64,2048]{1,0:T(8,128)(2,1)} %get-tuple-element.34.rest_1_, ...), custom_call_target="tpu_custom_call" | custom-call | flops 4294967296 | bytes 16777216 | tf_op jit(solution)/shard_map/finish_rows/pallas_call | solution.py:151
  (117 shorter events, 11.1 us)
Async XLA Ops:
  15.1 6.0 %collective-permute-start.14 = (bf16[128,4096]{1,0:T(8,128)(2,1)}, bf16[128,4096]{1,0:T(8,128)(2,1)S(1)}, u32[]{:S(2)}, u32[]{:S(2)}) collective-permute-start(bf16[128,4096]{1,0:T(8,128)(2,1)} %get-tuple-element.42), channel_id=1, source_target_pairs={{8,10},{10,8},{12,14},{14,12},{16,18},{18,16},{20,22},{22,20},{9,1... | collective-permute-start | bytes 3145736 | tf_op jit(solution)/shard_map/ppermute | solution.py:191
  15.8 7.0 %collective-permute-start.15 = (bf16[128,4096]{1,0:T(8,128)(2,1)}, bf16[128,4096]{1,0:T(8,128)(2,1)S(1)}, u32[]{:S(2)}, u32[]{:S(2)}) collective-permute-start(bf16[128,4096]{1,0:T(8,128)(2,1)} %get-tuple-element.43), channel_id=1, source_target_pairs={{8,12},{10,14},{12,8},{14,10},{16,20},{18,22},{20,16},{22,18},{9,1... | collective-permute-start | bytes 3145736 | tf_op jit(solution)/shard_map/ppermute | solution.py:191
  16.6 37.0 %collective-permute-start.1 = (bf16[128,4096]{1,0:T(8,128)(2,1)}, bf16[128,4096]{1,0:T(8,128)(2,1)S(1)}, u32[]{:S(2)}, u32[]{:S(2)}) collective-permute-start(bf16[128,4096]{1,0:T(8,128)(2,1)} %get-tuple-element.30), channel_id=1, source_target_pairs={{0,2},{2,0},{4,6},{6,4},{8,10},{10,8},{12,14},{14,12},{16,18},{18,... | collective-permute-start | bytes 3145736 | tf_op jit(solution)/shard_map/ppermute | solution.py:191
  19.6 53.0 %collective-permute-start.2 = (bf16[128,4096]{1,0:T(8,128)(2,1)}, bf16[128,4096]{1,0:T(8,128)(2,1)S(1)}, u32[]{:S(2)}, u32[]{:S(2)}) collective-permute-start(bf16[128,4096]{1,0:T(8,128)(2,1)} %get-tuple-element.31), channel_id=1, source_target_pairs={{0,4},{2,6},{4,0},{6,2},{8,12},{10,14},{12,8},{14,10},{16,20},{18,... | collective-permute-start | bytes 3145736 | tf_op jit(solution)/shard_map/ppermute | solution.py:191
  21.1 61.3 %collective-permute-start.3 = (bf16[128,4096]{1,0:T(8,128)(2,1)}, bf16[128,4096]{1,0:T(8,128)(2,1)S(1)}, u32[]{:S(2)}, u32[]{:S(2)}) collective-permute-start(bf16[128,4096]{1,0:T(8,128)(2,1)} %get-tuple-element.32), channel_id=1, source_target_pairs={{0,6},{2,4},{4,2},{6,0},{8,14},{10,12},{12,10},{14,8},{16,22},{18,... | collective-permute-start | bytes 3145736 | tf_op jit(solution)/shard_map/ppermute | solution.py:191
  21.1 61.2 %copy-start.3 = (bf16[128,4096]{1,0:T(8,128)(2,1)}, bf16[128,4096]{1,0:T(8,128)(2,1)S(1)}, u32[]{:S(2)}) copy-start(bf16[128,4096]{1,0:T(8,128)(2,1)S(1)} %collective-permute-done.14.refs_1_) | copy-start | bytes 3145732
  21.1 113.1 %collective-permute-start.16 = (bf16[128,4096]{1,0:T(8,128)(2,1)}, bf16[128,4096]{1,0:T(8,128)(2,1)}, u32[]{:S(2)}, u32[]{:S(2)}) collective-permute-start(bf16[128,4096]{1,0:T(8,128)(2,1)} %get-tuple-element.44), channel_id=1, source_target_pairs={{8,14},{10,12},{12,10},{14,8},{16,22},{18,20},{20,18},{22,16},{9,1... | collective-permute-start | bytes 3145736 | tf_op jit(solution)/shard_map/ppermute | solution.py:191
  22.8 59.6 %copy-start.4 = (bf16[128,4096]{1,0:T(8,128)(2,1)}, bf16[128,4096]{1,0:T(8,128)(2,1)S(1)}, u32[]{:S(2)}) copy-start(bf16[128,4096]{1,0:T(8,128)(2,1)S(1)} %collective-permute-done.15.refs_2_) | copy-start | bytes 3145732
  22.8 135.2 %collective-permute-start.17 = (bf16[128,4096]{1,0:T(8,128)(2,1)}, bf16[128,4096]{1,0:T(8,128)(2,1)}, u32[]{:S(2)}, u32[]{:S(2)}) collective-permute-start(bf16[128,4096]{1,0:T(8,128)(2,1)} %get-tuple-element.41.refs_0_), channel_id=1, source_target_pairs={{0,8},{2,10},{4,12},{6,14},{24,16},{26,18},{28,20},{30,22},{1,9},{... | collective-permute-start | bytes 3145736 | tf_op jit(solution)/shard_map/ppermute | solution.py:191
  53.6 76.1 %copy-start = (bf16[128,4096]{1,0:T(8,128)(2,1)}, bf16[128,4096]{1,0:T(8,128)(2,1)S(1)}, u32[]{:S(2)}) copy-start(bf16[128,4096]{1,0:T(8,128)(2,1)S(1)} %collective-permute-done.1.refs_1_) | copy-start | bytes 3145732
  53.6 104.5 %collective-permute-start.18 = (bf16[128,4096]{1,0:T(8,128)(2,1)}, bf16[128,4096]{1,0:T(8,128)(2,1)}, u32[]{:S(2)}, u32[]{:S(2)}) collective-permute-start(bf16[128,4096]{1,0:T(8,128)(2,1)} %get-tuple-element.42), channel_id=1, source_target_pairs={{0,10},{2,8},{4,14},{6,12},{24,18},{26,16},{28,22},{30,20},{1,11},... | collective-permute-start | bytes 3145736 | tf_op jit(solution)/shard_map/ppermute | solution.py:191
  72.6 57.1 %copy-start.1 = (bf16[128,4096]{1,0:T(8,128)(2,1)}, bf16[128,4096]{1,0:T(8,128)(2,1)S(1)}, u32[]{:S(2)}) copy-start(bf16[128,4096]{1,0:T(8,128)(2,1)S(1)} %collective-permute-done.2.refs_2_) | copy-start | bytes 3145732
  72.6 87.1 %collective-permute-start.19 = (bf16[128,4096]{1,0:T(8,128)(2,1)}, bf16[128,4096]{1,0:T(8,128)(2,1)}, u32[]{:S(2)}, u32[]{:S(2)}) collective-permute-start(bf16[128,4096]{1,0:T(8,128)(2,1)} %get-tuple-element.43), channel_id=1, source_target_pairs={{0,12},{2,14},{4,8},{6,10},{24,20},{26,22},{28,16},{30,18},{1,13},... | collective-permute-start | bytes 3145736 | tf_op jit(solution)/shard_map/ppermute | solution.py:191
  82.4 47.3 %copy-start.2 = (bf16[128,4096]{1,0:T(8,128)(2,1)}, bf16[128,4096]{1,0:T(8,128)(2,1)S(1)}, u32[]{:S(2)}) copy-start(bf16[128,4096]{1,0:T(8,128)(2,1)S(1)} %collective-permute-done.3.refs_3_) | copy-start | bytes 3145732
  82.4 143.8 %collective-permute-start.5 = (bf16[4,64,4096]{2,1,0:T(8,128)(2,1)}, bf16[4,64,4096]{2,1,0:T(8,128)(2,1)}, u32[]{:S(2)}, u32[]{:S(2)}) collective-permute-start(bf16[4,64,4096]{2,1,0:T(8,128)(2,1)} %bitcast.7.refs_4_), channel_id=1, source_target_pairs={{0,8},{2,10},{4,12},{6,14},{8,0},{10,2},{12,4},{14,6},{16,24},{18,... | collective-permute-start | bytes 6291464 | tf_op jit(solution)/shard_map/ppermute | solution.py:191
  134.2 69.5 %collective-permute-start.20 = (bf16[128,4096]{1,0:T(8,128)(2,1)S(1)}, bf16[128,4096]{1,0:T(8,128)(2,1)S(1)}, u32[]{:S(2)}, u32[]{:S(2)}) collective-permute-start(bf16[128,4096]{1,0:T(8,128)(2,1)S(1)} %copy-done.23), channel_id=1, source_target_pairs={{0,14},{2,12},{4,10},{6,8},{24,22},{26,20},{28,18},{30,16},{1,15},... | collective-permute-start | bytes 3145736 | tf_op jit(solution)/shard_map/ppermute | solution.py:191
  158.0 65.2 %collective-permute-start.7 = (bf16[4,64,2048]{2,1,0:T(8,128)(2,1)S(1)}, bf16[4,64,2048]{2,1,0:T(8,128)(2,1)}, u32[]{:S(2)}, u32[]{:S(2)}) collective-permute-start(bf16[4,64,2048]{2,1,0:T(8,128)(2,1)S(1)} %copy-done.7), channel_id=1, source_target_pairs={{0,8},{2,10},{4,12},{6,14},{8,0},{10,2},{12,4},{14,6},{16,24},{18,... | collective-permute-start | bytes 3145736 | tf_op jit(solution)/shard_map/ppermute | solution.py:191
  158.1 65.2 %collective-permute-start.24 = (bf16[4,64,2048]{2,1,0:T(8,128)(2,1)S(1)}, bf16[4,64,2048]{2,1,0:T(8,128)(2,1)}, u32[]{:S(2)}, u32[]{:S(2)}) collective-permute-start(bf16[4,64,2048]{2,1,0:T(8,128)(2,1)S(1)} %copy-done.7), channel_id=1, source_target_pairs={{8,16},{10,18},{12,20},{14,22},{16,8},{18,10},{20,12},{22,14},{9,1... | collective-permute-start | bytes 3145736 | tf_op jit(solution)/shard_map/ppermute | solution.py:191
  159.7 65.1 %collective-permute-start.4 = (f32[4,64,64]{2,1,0:T(8,128)}, f32[4,64,64]{2,1,0:T(8,128)S(1)}, u32[]{:S(2)}, u32[]{:S(2)}) collective-permute-start(f32[4,64,64]{2,1,0:T(8,128)} %down_rows.4), channel_id=1, source_target_pairs={{0,1},{1,0},{2,3},{3,2},{4,5},{5,4},{6,7},{7,6},{8,9},{9,8},{10,11... | collective-permute-start | bytes 196616 | tf_op jit(solution)/shard_map/ppermute | solution.py:234
  203.8 46.9 %copy-start.5 = (bf16[128,4096]{1,0:T(8,128)(2,1)}, bf16[128,4096]{1,0:T(8,128)(2,1)S(1)}, u32[]{:S(2)}) copy-start(bf16[128,4096]{1,0:T(8,128)(2,1)S(1)} %collective-permute-done.20.refs_7_) | copy-start | bytes 3145732
  203.8 60.4 %collective-permute-start.21 = (bf16[4,64,4096]{2,1,0:T(8,128)(2,1)}, bf16[4,64,4096]{2,1,0:T(8,128)(2,1)}, u32[]{:S(2)}, u32[]{:S(2)}) collective-permute-start(bf16[4,64,4096]{2,1,0:T(8,128)(2,1)} %bitcast.7.refs_4_), channel_id=1, source_target_pairs={{8,16},{10,18},{12,20},{14,22},{16,8},{18,10},{20,12},{22,14},{9,1... | collective-permute-start | bytes 6291464 | tf_op jit(solution)/shard_map/ppermute | solution.py:191
  223.2 142.3 %collective-permute-start = (bf16[1024,2048]{1,0:T(8,128)(2,1)}, bf16[1024,2048]{1,0:T(8,128)(2,1)}, u32[]{:S(2)}, u32[]{:S(2)}) collective-permute-start(bf16[1024,2048]{1,0:T(8,128)(2,1)} %project_half.3), channel_id=1, source_target_pairs={{0,1},{1,0},{2,3},{3,2},{4,5},{5,4},{6,7},{7,6},{8,9},{9,8},{10,11... | collective-permute-start | bytes 12582920 | tf_op jit(solution)/shard_map/ppermute | solution.py:230
  223.2 36.7 %collective-permute-start.29 = (bf16[4,64,2048]{2,1,0:T(8,128)(2,1)}, bf16[4,64,2048]{2,1,0:T(8,128)(2,1)}, u32[]{:S(2)}, u32[]{:S(2)}) collective-permute-start(bf16[4,64,2048]{2,1,0:T(8,128)(2,1)} %collective-permute-done.7.u_ref), channel_id=1, source_target_pairs={{8,16},{10,18},{12,20},{14,22},{16,8},{18,10},{20,12},{22,14},{9,1... | collective-permute-start | bytes 3145736 | tf_op jit(solution)/shard_map/ppermute | solution.py:191
  224.9 35.6 %collective-permute-start.25 = (bf16[4,64,2048]{2,1,0:T(8,128)(2,1)}, bf16[4,64,2048]{2,1,0:T(8,128)(2,1)}, u32[]{:S(2)}, u32[]{:S(2)}) collective-permute-start(bf16[4,64,2048]{2,1,0:T(8,128)(2,1)} %collective-permute-done.24), channel_id=1, source_target_pairs={{8,0},{10,2},{12,4},{14,6},{16,24},{18,26},{20,28},{22,30},{9,1},{... | collective-permute-start | bytes 3145736 | tf_op jit(solution)/shard_map/ppermute | solution.py:191
  226.2 50.0 %collective-permute-start.26 = (bf16[4,64,4096]{2,1,0:T(8,128)(2,1)}, bf16[4,64,4096]{2,1,0:T(8,128)(2,1)S(1)}, u32[]{:S(2)}, u32[]{:S(2)}) collective-permute-start(bf16[4,64,4096]{2,1,0:T(8,128)(2,1)} %collective-permute-done.5.refs_4_), channel_id=1, source_target_pairs={{8,16},{10,18},{12,20},{14,22},{16,8},{18,10},{20,12},{22,14},{9,1... | collective-permute-start | bytes 6291464 | tf_op jit(solution)/shard_map/ppermute | solution.py:191
  260.0 11.8 %collective-permute-start.6 = (f32[4,64,64]{2,1,0:T(8,128)}, f32[4,64,64]{2,1,0:T(8,128)S(1)}, u32[]{:S(2)}, u32[]{:S(2)}) collective-permute-start(f32[4,64,64]{2,1,0:T(8,128)} %down_rows.5), channel_id=1, source_target_pairs={{0,1},{1,0},{2,3},{3,2},{4,5},{5,4},{6,7},{7,6},{8,9},{9,8},{10,11... | collective-permute-start | bytes 196616 | tf_op jit(solution)/shard_map/ppermute | solution.py:234
  260.5 81.0 %collective-permute-start.30 = (bf16[4,64,2048]{2,1,0:T(8,128)(2,1)}, bf16[4,64,2048]{2,1,0:T(8,128)(2,1)S(1)}, u32[]{:S(2)}, u32[]{:S(2)}) collective-permute-start(bf16[4,64,2048]{2,1,0:T(8,128)(2,1)} %collective-permute-done.29), channel_id=1, source_target_pairs={{8,0},{10,2},{12,4},{14,6},{16,24},{18,26},{20,28},{22,30},{9,1},{... | collective-permute-start | bytes 3145736 | tf_op jit(solution)/shard_map/ppermute | solution.py:191
  264.1 19.0 %collective-permute-start.10 = (bf16[64,2048]{1,0:T(8,128)(2,1)S(1)}, bf16[64,2048]{1,0:T(8,128)(2,1)S(1)}, u32[]{:S(2)}, u32[]{:S(2)}) collective-permute-start(bf16[64,2048]{1,0:T(8,128)(2,1)S(1)} %copy-done.30), channel_id=1, source_target_pairs={{0,4},{2,6},{4,0},{6,2},{8,12},{10,14},{12,8},{14,10},{16,20},{18,... | collective-permute-start | bytes 786440 | tf_op jit(solution)/shard_map/ppermute | solution.py:191
  271.7 10.8 %collective-permute-start.22 = (f32[4,128,64]{2,1,0:T(8,128)}, f32[4,128,64]{2,1,0:T(8,128)S(1)}, u32[]{:S(2)}, u32[]{:S(2)}) collective-permute-start(f32[4,128,64]{2,1,0:T(8,128)} %down_rows.6), channel_id=1, source_target_pairs={{0,1},{1,0},{2,3},{3,2},{4,5},{5,4},{6,7},{7,6},{8,9},{9,8},{10,11... | collective-permute-start | bytes 393224 | tf_op jit(solution)/shard_map/ppermute | solution.py:234
  276.3 62.1 %copy-start.26 = (bf16[64,2048]{1,0:T(8,128)(2,1)S(1)}, bf16[64,2048]{1,0:T(8,128)(2,1)}, u32[]{:S(2)}) copy-start(bf16[64,2048]{1,0:T(8,128)(2,1)} %get-tuple-element.40) | copy-start | bytes 786436
  276.3 63.9 %copy-start.24 = (bf16[64,2048]{1,0:T(8,128)(2,1)S(1)}, bf16[64,2048]{1,0:T(8,128)(2,1)}, u32[]{:S(2)}) copy-start(bf16[64,2048]{1,0:T(8,128)(2,1)} %get-tuple-element.36) | copy-start | bytes 786436
  276.3 9.7 %collective-permute-start.12 = (bf16[64,2048]{1,0:T(8,128)(2,1)S(1)}, bf16[64,2048]{1,0:T(8,128)(2,1)S(1)}, u32[]{:S(2)}, u32[]{:S(2)}) collective-permute-start(bf16[64,2048]{1,0:T(8,128)(2,1)S(1)} %copy-done.27), channel_id=1, source_target_pairs={{0,6},{2,4},{4,2},{6,0},{8,14},{10,12},{12,10},{14,8},{16,22},{18,... | collective-permute-start | bytes 786440 | tf_op jit(solution)/shard_map/ppermute | solution.py:191
  282.5 3.5 collective-permute-start.27
  283.1 92.1 %copy-start.11 = (bf16[64,2048]{1,0:T(8,128)(2,1)}, bf16[64,2048]{1,0:T(8,128)(2,1)S(1)}, u32[]{:S(2)}) copy-start(bf16[64,2048]{1,0:T(8,128)(2,1)S(1)} %collective-permute-done.10.rest_4_) | copy-start | bytes 786436
  283.2 55.2 %collective-permute-start.8 = (bf16[64,2048]{1,0:T(8,128)(2,1)S(1)}, bf16[64,2048]{1,0:T(8,128)(2,1)S(1)}, u32[]{:S(2)}, u32[]{:S(2)}) collective-permute-start(bf16[64,2048]{1,0:T(8,128)(2,1)S(1)} %copy-done.25), channel_id=1, source_target_pairs={{0,2},{2,0},{4,6},{6,4},{8,10},{10,8},{12,14},{14,12},{16,18},{18,... | collective-permute-start | bytes 786440 | tf_op jit(solution)/shard_map/ppermute | solution.py:191
  285.9 89.3 %copy-start.12 = (bf16[64,2048]{1,0:T(8,128)(2,1)}, bf16[64,2048]{1,0:T(8,128)(2,1)S(1)}, u32[]{:S(2)}) copy-start(bf16[64,2048]{1,0:T(8,128)(2,1)S(1)} %collective-permute-done.12.rest_6_) | copy-start | bytes 786436
  285.9 54.2 %collective-permute-start.11 = (bf16[64,2048]{1,0:T(8,128)(2,1)S(1)}, bf16[64,2048]{1,0:T(8,128)(2,1)S(1)}, u32[]{:S(2)}, u32[]{:S(2)}) collective-permute-start(bf16[64,2048]{1,0:T(8,128)(2,1)S(1)} %copy-done.28), channel_id=1, source_target_pairs={{0,4},{2,6},{4,0},{6,2},{8,12},{10,14},{12,8},{14,10},{16,20},{18,... | collective-permute-start | bytes 786440 | tf_op jit(solution)/shard_map/ppermute | solution.py:191
  286.0 46.5 %collective-permute-start.23 = (bf16[4,64,64]{2,1,0:T(8,128)(2,1)S(1)}, bf16[4,64,64]{2,1,0:T(8,128)(2,1)S(1)}, u32[]{:S(2)}, u32[]{:S(2)}) collective-permute-start(bf16[4,64,64]{2,1,0:T(8,128)(2,1)S(1)} %slice.17), channel_id=1, source_target_pairs={{8,0},{10,2},{12,4},{14,6},{16,24},{18,26},{20,28},{22,30},{9,1},{... | collective-permute-start | bytes 98312 | tf_op jit(solution)/shard_map/ppermute | solution.py:191
  332.5 9.8 %collective-permute-start.28 = (bf16[4,64,64]{2,1,0:T(8,128)(2,1)S(1)}, bf16[4,64,64]{2,1,0:T(8,128)(2,1)S(1)}, u32[]{:S(2)}, u32[]{:S(2)}) collective-permute-start(bf16[4,64,64]{2,1,0:T(8,128)(2,1)S(1)} %slice.19), channel_id=1, source_target_pairs={{8,0},{10,2},{12,4},{14,6},{16,24},{18,26},{20,28},{22,30},{9,1},{... | collective-permute-start | bytes 98312 | tf_op jit(solution)/shard_map/ppermute | solution.py:191
  338.4 36.8 %copy-start.13 = (bf16[64,2048]{1,0:T(8,128)(2,1)}, bf16[64,2048]{1,0:T(8,128)(2,1)S(1)}, u32[]{:S(2)}) copy-start(bf16[64,2048]{1,0:T(8,128)(2,1)S(1)} %collective-permute-done.8.rest_2_) | copy-start | bytes 786436
  338.4 10.8 %collective-permute-start.13 = (bf16[64,2048]{1,0:T(8,128)(2,1)S(1)}, bf16[64,2048]{1,0:T(8,128)(2,1)S(1)}, u32[]{:S(2)}, u32[]{:S(2)}) collective-permute-start(bf16[64,2048]{1,0:T(8,128)(2,1)S(1)} %copy-done.26), channel_id=1, source_target_pairs={{0,6},{2,4},{4,2},{6,0},{8,14},{10,12},{12,10},{14,8},{16,22},{18,... | collective-permute-start | bytes 786440 | tf_op jit(solution)/shard_map/ppermute | solution.py:191
  340.2 14.1 %collective-permute-start.9 = (bf16[64,2048]{1,0:T(8,128)(2,1)S(1)}, bf16[64,2048]{1,0:T(8,128)(2,1)S(1)}, u32[]{:S(2)}, u32[]{:S(2)}) collective-permute-start(bf16[64,2048]{1,0:T(8,128)(2,1)S(1)} %copy-done.24), channel_id=1, source_target_pairs={{0,2},{2,0},{4,6},{6,4},{8,10},{10,8},{12,14},{14,12},{16,18},{18,... | collective-permute-start | bytes 786440 | tf_op jit(solution)/shard_map/ppermute | solution.py:191
  341.5 18.4 %collective-permute-start.31 = (bf16[64,2048]{1,0:T(8,128)(2,1)}, bf16[64,2048]{1,0:T(8,128)(2,1)S(1)}, u32[]{:S(2)}, u32[]{:S(2)}) collective-permute-start(bf16[64,2048]{1,0:T(8,128)(2,1)} %get-tuple-element.47), channel_id=1, source_target_pairs={{0,2},{2,0},{4,6},{6,4},{8,10},{10,8},{12,14},{14,12},{16,18},{18,... | collective-permute-start | bytes 786440 | tf_op jit(solution)/shard_map/ppermute | solution.py:191
  342.3 18.2 %collective-permute-start.33 = (bf16[64,2048]{1,0:T(8,128)(2,1)}, bf16[64,2048]{1,0:T(8,128)(2,1)S(1)}, u32[]{:S(2)}, u32[]{:S(2)}) collective-permute-start(bf16[64,2048]{1,0:T(8,128)(2,1)} %get-tuple-element.49), channel_id=1, source_target_pairs={{0,4},{2,6},{4,0},{6,2},{8,12},{10,14},{12,8},{14,10},{16,20},{18,... | collective-permute-start | bytes 786440 | tf_op jit(solution)/shard_map/ppermute | solution.py:191
  349.3 16.3 %collective-permute-start.35 = (bf16[64,2048]{1,0:T(8,128)(2,1)S(1)}, bf16[64,2048]{1,0:T(8,128)(2,1)S(1)}, u32[]{:S(2)}, u32[]{:S(2)}) collective-permute-start(bf16[64,2048]{1,0:T(8,128)(2,1)S(1)} %copy-done.29), channel_id=1, source_target_pairs={{0,6},{2,4},{4,2},{6,0},{8,14},{10,12},{12,10},{14,8},{16,22},{18,... | collective-permute-start | bytes 786440 | tf_op jit(solution)/shard_map/ppermute | solution.py:191
  354.3 16.9 %collective-permute-start.32 = (bf16[64,2048]{1,0:T(8,128)(2,1)}, bf16[64,2048]{1,0:T(8,128)(2,1)S(1)}, u32[]{:S(2)}, u32[]{:S(2)}) collective-permute-start(bf16[64,2048]{1,0:T(8,128)(2,1)} %get-tuple-element.48), channel_id=1, source_target_pairs={{0,2},{2,0},{4,6},{6,4},{8,10},{10,8},{12,14},{14,12},{16,18},{18,... | collective-permute-start | bytes 786440 | tf_op jit(solution)/shard_map/ppermute | solution.py:191
  359.9 11.3 %collective-permute-start.34 = (bf16[64,2048]{1,0:T(8,128)(2,1)}, bf16[64,2048]{1,0:T(8,128)(2,1)S(1)}, u32[]{:S(2)}, u32[]{:S(2)}) collective-permute-start(bf16[64,2048]{1,0:T(8,128)(2,1)} %get-tuple-element.50), channel_id=1, source_target_pairs={{0,4},{2,6},{4,0},{6,2},{8,12},{10,14},{12,8},{14,10},{16,20},{18,... | collective-permute-start | bytes 786440 | tf_op jit(solution)/shard_map/ppermute | solution.py:191
  360.5 14.7 %collective-permute-start.36 = (bf16[64,2048]{1,0:T(8,128)(2,1)}, bf16[64,2048]{1,0:T(8,128)(2,1)S(1)}, u32[]{:S(2)}, u32[]{:S(2)}) collective-permute-start(bf16[64,2048]{1,0:T(8,128)(2,1)} %get-tuple-element.52), channel_id=1, source_target_pairs={{0,6},{2,4},{4,2},{6,0},{8,14},{10,12},{12,10},{14,8},{16,22},{18,... | collective-permute-start | bytes 786440 | tf_op jit(solution)/shard_map/ppermute | solution.py:191
  (20 other events, 252.0 us)

commit v2 on v1

--- a/solution.py
+++ b/solution.py
@@ -23,34 +23,32 @@
     return pl.CostEstimate(flops=flops, bytes_accessed=size, transcendentals=0)
 
 
-def pack_kernel(target_ref, x_ref, *rest):
+def pack_kernel(first, target_ref, x_ref, *rest):
     outs, onehot = rest[:-1], rest[-1]
-    size = onehot.shape[0]
 
     @pl.when(pl.program_id(0) == 0)
     def _():
-        place = lax.broadcasted_iota(jnp.int32, onehot.shape, 0)
+        place = lax.broadcasted_iota(jnp.int32, onehot.shape, 0) + first
         onehot[...] = (place == target_ref[...]).astype(jnp.bfloat16)
 
     packed = jnp.dot(onehot[...], x_ref[...], preferred_element_type=jnp.float32).astype(jnp.bfloat16)
-    part = size // len(outs)
+    part = onehot.shape[0] // len(outs)
     for k, out in enumerate(outs):
         out[...] = packed[k * part : (k + 1) * part]
 
 
-def pack(target, x, parts):
+def pack(target, x, first, part, parts):
     rows, width = x.shape
     tile = 512
-    part = rows // parts
-    return pl.pallas_call(
-        pack_kernel,
+    return pl.pallas_call(
+        functools.partial(pack_kernel, first),
         grid=(width // tile,),
         in_specs=[pl.BlockSpec((1, rows), lambda i: (0, 0)), pl.BlockSpec((rows, tile), lambda i: (0, i))],
         out_specs=[pl.BlockSpec((part, tile), lambda i: (0, i))] * parts,
         out_shape=[jax.ShapeDtypeStruct((part, width), x.dtype)] * parts,
-        scratch_shapes=[pltpu.VMEM((rows, rows), jnp.bfloat16)],
-        compiler_params=params(),
-        cost_estimate=cost(2 * rows * rows * width, 4 * rows * width),
+        scratch_shapes=[pltpu.VMEM((part * parts, rows), jnp.bfloat16)],
+        compiler_params=params(),
+        cost_estimate=cost(2 * part * parts * rows * width, 2 * (rows + part * parts) * width),
         name="pack_rows",
     )(target, x)
 
@@ -82,52 +80,74 @@
     )(half.reshape(1), x, w)
 
 
-def down_kernel(*refs):
-    xs, w_ref, o_ref = refs[:-2], refs[-2], refs[-1]
+def spans(arrays):
+    ends, start = [], 0
+    for array in arrays:
+        ends.append((start, start + array.shape[0]))
+        start += array.shape[0]
+    return ends
+
+
+def picked(start, end):
+    return lambda i: (jnp.clip(i - start, 0, end - start - 1), 0, 0)
+
+
+def down_kernel(ranges, *refs):
+    xs, ws, o_ref = refs[: -1 - len(ranges)], refs[-1 - len(ranges) : -1], refs[-1]
+    step = pl.program_id(0)
     rows = jnp.concatenate([x[...] for x in xs], axis=0)
-    o_ref[...] = lax.dot_general(rows, w_ref[...], NT, preferred_element_type=jnp.float32)
-
-
-def down(xs, w, start):
-    adapters, rank, width = w.shape
-    return pl.pallas_call(
-        down_kernel,
+    for w_ref, (start, end) in zip(ws, ranges):
+
+        @pl.when((step >= start) & (step < end))
+        def _():
+            o_ref[...] = lax.dot_general(rows, w_ref[...], NT, preferred_element_type=jnp.float32)
+
+
+def down(xs, ws):
+    ranges = spans(ws)
+    adapters, (_, rank, width) = ranges[-1][1], ws[0].shape
+    rows = len(xs) * MOST
+    return pl.pallas_call(
+        functools.partial(down_kernel, ranges),
         grid=(adapters,),
-        in_specs=[pl.BlockSpec((MOST, width), lambda i: (start + i, 0))] * len(xs)
-        + [pl.BlockSpec((None, rank, width), lambda i: (i, 0, 0))],
-        out_specs=pl.BlockSpec((None, len(xs) * MOST, rank), lambda i: (i, 0, 0)),
-        out_shape=jax.ShapeDtypeStruct((adapters, len(xs) * MOST, rank), jnp.float32),
-        compiler_params=params(),
-        cost_estimate=cost(
-            2 * adapters * len(xs) * MOST * rank * width, 2 * adapters * width * (rank + len(xs) * MOST)
-        ),
+        in_specs=[pl.BlockSpec((MOST, width), lambda i: (i, 0))] * len(xs)
+        + [pl.BlockSpec((None, rank, width), picked(*span)) for span in ranges],
+        out_specs=pl.BlockSpec((None, rows, rank), lambda i: (i, 0, 0)),
+        out_shape=jax.ShapeDtypeStruct((adapters, rows, rank), jnp.float32),
+        compiler_params=params(),
+        cost_estimate=cost(2 * adapters * rows * rank * width, 2 * adapters * width * (rank + rows)),
         name="down_rows",
-    )(*xs, w)
-
-
-def lift_kernel(y_ref, u_ref, *outs):
-    rows = jnp.dot(y_ref[...], u_ref[...], preferred_element_type=jnp.float32).astype(jnp.bfloat16)
-    for k, out in enumerate(outs):
-        out[...] = rows[k * MOST : (k + 1) * MOST]
-
-
-def lift(y, u):
-    adapters, rank, columns = u.shape
-    rows = y.shape[1]
+    )(*xs, *ws)
+
+
+def lift_kernel(ranges, y_ref, *refs):
+    us, outs = refs[: len(ranges)], refs[len(ranges) :]
+    step = pl.program_id(0)
+    for u_ref, (start, end) in zip(us, ranges):
+
+        @pl.when((step >= start) & (step < end))
+        def _():
+            rows = jnp.dot(y_ref[...], u_ref[...], preferred_element_type=jnp.float32).astype(jnp.bfloat16)
+            for k, out in enumerate(outs):
+                out[...] = rows[k * MOST : (k + 1) * MOST]
+
+
+def lift(y, us):
+    ranges = spans(us)
+    adapters, rows, rank = y.shape
+    columns = us[0].shape[2]
     parts = rows // MOST
     return pl.pallas_call(
-        lift_kernel,
+        functools.partial(lift_kernel, ranges),
         grid=(adapters,),
-        in_specs=[
-            pl.BlockSpec((None, rows, rank), lambda i: (i, 0, 0)),
-            pl.BlockSpec((None, rank, columns), lambda i: (i, 0, 0)),
-        ],
+        in_specs=[pl.BlockSpec((None, rows, rank), lambda i: (i, 0, 0))]
+        + [pl.BlockSpec((None, rank, columns), picked(*span)) for span in ranges],
         out_specs=[pl.BlockSpec((MOST, columns), lambda i: (i, 0))] * parts,
         out_shape=[jax.ShapeDtypeStruct((adapters * MOST, columns), jnp.bfloat16)] * parts,
         compiler_params=params(),
         cost_estimate=cost(2 * adapters * rows * rank * columns, 2 * adapters * columns * (rank + rows)),
         name="lift_rows",
-    )(y, u)
+    )(y, *us)
 
 
 def finish_kernel(target_ref, own_ref, other_ref, *rest):
@@ -177,9 +197,15 @@
     return slots, position
 
 
+def after(x, *earlier):
+    return lax.optimization_barrier((x, *earlier))[0]
+
+
 def by_planes(hidden_input, query_weight, slot_down_weight, slot_up_weight, request_adapter, adapter_slot):
     owned = slot_down_weight.shape[0]
-    group = owned * MOST
+    cut = owned // 2
+    served = 2 * owned + cut
+    rest = 4 * owned - served
     me = lax.axis_index("rep")
     plane, column = me // COLUMNS, me % COLUMNS
     inner = (plane == 1) | (plane == 2)
@@ -187,41 +213,50 @@
     inside = [r for r in every if r // COLUMNS in (1, 2)]
     outside = [r for r in every if r // COLUMNS in (0, 3)]
 
-    def send(x, pairs):
-        return lax.ppermute(x, "rep", pairs)
+    def send(x, pairs, *earlier):
+        return lax.ppermute(after(x, *earlier) if earlier else x, "rep", pairs)
 
     pair = [(r, r ^ 4) for r in every]
     across = [(r, r ^ 12) for r in inside]
     outward = [(r, r ^ 4) for r in inside]
+    inward = [(r, r ^ 4) for r in outside]
     turn = [[(r, r ^ d) for r in every] for d in range(COLUMNS)]
-    turn_inside = [[(r, r ^ d) for r in inside] for d in range(COLUMNS)]
-    turn_inward = [[(r, r ^ 4 ^ d) for r in outside] for d in range(COLUMNS)]
+
+    slots, position = places(request_adapter, adapter_slot, owned * COLUMNS * PLANES)
+    slot_plane = slots // (owned * COLUMNS)
+    slot_column = slots // owned % COLUMNS
+    other = slot_plane // 2 != plane // 2
+    second = jnp.where(other, (slot_plane == 0) | (slot_plane == 3), slot_plane != plane)
+    number = (2 * other.astype(jnp.int32) + second.astype(jnp.int32)) * owned + slots % owned
+    turned = slot_column ^ column
+    there = (turned * rest + number - served) * MOST
+    here = (COLUMNS * rest + turned * served + number) * MOST
+    target = jnp.where(number < served, here, there) + position
 
     down_own = jnp.swapaxes(slot_down_weight, 1, 2)
     up_own = slot_up_weight
     down_pair = send(down_own, pair)
     down_near = send(down_own, across)
 
-    slots, position = places(request_adapter, adapter_slot, owned * COLUMNS * PLANES)
-    slot_plane = slots // (owned * COLUMNS)
-    slot_column = slots // owned % COLUMNS
-    far = slot_plane // 2 != plane // 2
-    second = jnp.where(far, (slot_plane == 0) | (slot_plane == 3), slot_plane != plane).astype(jnp.int32)
-    order = (far.astype(jnp.int32) * COLUMNS + (slot_column ^ column)) * 2 + second
-    target = order * group + slots % owned * MOST + position
-
-    packed = pack(target[None, :], hidden_input, 2 * COLUMNS)
-    home, away = packed[:COLUMNS], packed[COLUMNS:]
-    inward = [send(away[d], turn_inward[d]) for d in range(COLUMNS)]
-    beside = [away[0]] + [send(away[d], turn_inside[d]) for d in range(1, COLUMNS)]
-    local = [home[0]] + [send(home[d], turn[d]) for d in range(1, COLUMNS)]
-    down_far = send(down_pair, across)
-
-    up_pair = send(up_own, pair)
-    up_near = send(up_own, across)
-    up_far = send(up_pair, across)
-    up_near_out = send(up_near, outward)
-    up_far_out = send(up_far, outward)
+    away = pack(target[None, :], hidden_input, 0, rest * MOST, COLUMNS)
+    home = pack(target[None, :], hidden_input, COLUMNS * rest * MOST, served * MOST, COLUMNS)
+    away = [away[0]] + [send(away[d], turn[d]) for d in range(1, COLUMNS)]
+
+    up_pair = send(up_own, pair, down_pair)
+    up_near = send(up_own, across, down_near)
+    beside = [home[0]] + [send(home[d], turn[d], away[1], away[2]) for d in (1, 2)]
+    beside.append(send(home[3], turn[3], away[3], beside[1]))
+
+    down_out = send(down_near[:cut], outward, up_pair)
+    up_far = send(up_pair, across, up_near)
+    moved, last = [], up_pair
+    for rows in away:
+        last = send(rows, inward, last)
+        moved.append(last)
+    down_far = send(down_pair, across, up_far)
+    up_near_out = send(up_near, outward, down_out)
+    up_far_out = send(up_far, outward, up_near_out)
+    down_part = jnp.where(inner, down_near[:cut], down_out)
     up_near = jnp.where(inner, up_near, up_near_out)
     up_far = jnp.where(inner, up_far, up_far_out)
 
@@ -233,17 +268,16 @@
     def both(y):
         return (y + lax.ppermute(y, "tp", SWAP)).astype(jnp.bfloat16)
 
+    low = both(down(beside, [down_own, down_pair, down_part]))
+    rows = lift(low, [up_own, up_pair, up_near[:cut]])
+    lifted = [rows[0]] + [send(rows[d], turn[d]) for d in range(1, COLUMNS)]
+
     half = COLUMNS * MOST
-    lowered = [both(down(local, down_own, 0)), both(down(local, down_pair, owned))]
-    for weight, start in ((down_near, 0), (down_far, owned)):
-        y = both(down(beside + inward, weight, start))
-        lowered.append(jnp.where(inner, y[:, :half], send(y[:, half:], outward)))
-    lifted = []
-    for y, u in zip(lowered, (up_own, up_pair, up_near, up_far)):
-        rows = lift(y, u)
-        lifted.append([rows[0]] + [send(rows[d], turn[d]) for d in range(1, COLUMNS)])
-    pieces = [lifted[2 * f + s][d] for f in range(2) for d in range(COLUMNS) for s in range(2)]
-    return finish(target[:, None], base_own, base_other, pieces)
+    low = both(down(away + moved, [down_near[cut:], down_far]))
+    low = jnp.where(inner, low[:, :half], send(low[:, half:], outward))
+    rows = lift(low, [up_near[cut:], up_far])
+    lifted = [rows[0]] + [send(rows[d], turn[d]) for d in range(1, COLUMNS)] + lifted
+    return finish(target[:, None], base_own, base_other, lifted)
 
 
 def by_gather(hidden_input, query_weight, slot_down_weight, slot_up_weight, request_adapter, adapter_slot):

time: 387 us -> 293 us (0.76)
  the two profiles are of different devices: /device:TPU:0 before, /device:TPU:20 now
where the time goes in v2:
time: 293 us; the launch traced here: 291 us
  waiting for transfers between devices  119 us (41%)
  Pallas kernels  107 us (37%)
  starting transfers between devices  47.7 us (16%)
  other arithmetic  11.4 us (4%)
  local copies, waits for them, and re-layouts  4.9 us (2%)
    ppermute x26, waiting for transfers between devices, send(): return lax.ppermute(after(x, *earlier) if earlier else x, 'rep', pairs)  119 us
    ppermute x26, starting transfers between devices, send(): return lax.ppermute(after(x, *earlier) if earlier else x, 'rep', pairs)  47.6 us
    pallas_call x2, Pallas kernels, project(): pl.pallas_call(project_kernel, grid_spec=pltpu.PrefetchScalarGridSpec(num...  47.3 us
    pallas_call x2, Pallas kernels, pack(): pl.pallas_call(functools.partial(pack_kernel, first), grid=(width // tile...  20 us
    pallas_call x2, Pallas kernels, down(): pl.pallas_call(functools.partial(down_kernel, ranges), grid=(adapters,),...  16.8 us
    pallas_call x2, Pallas kernels, lift(): pl.pallas_call(functools.partial(lift_kernel, ranges), grid=(adapters,),...  12.9 us
    pallas_call x1, Pallas kernels, finish(): pl.pallas_call(finish_kernel, grid=(columns // tile,), in_specs=[pl.Block...  10.1 us
  transfers between devices with their start and end apart: 29, of which 9 were waited for; matrix products, arithmetic and copies ran while one was open for 5% of the time, Pallas kernels for 33%

profile of v2, /device:TPU:20, one launch (start us, length us, event | category | flops | bytes accessed | tf_op | source)
XLA Modules:
  0.0 291.1 jit_solution(17964099677401835057)
XLA Ops:
  0.0 1.6 collective-permute-start.4
  1.6 1.9 collective-permute-start.10
  5.7 9.1 %pack_rows.2 = (bf16[96,4096]{1,0:T(8,128)(2,1)}, bf16[96,4096]{1,0:T(8,128)(2,1)}, bf16[96,4096]{1,0:T(8,128)(2,1)}, bf16[96,4096]{1,0:T(8,128)(2,1)}) custom-call(s32[1,1024]{1,0:T(1,128)} %fusion.16.target_ref, bf16[1024,4096]{1,0:T(8,128)(2,1)} %x_ref.7), custom_call_target="tpu_custom_call" | custom-call | flops 3221225472 | bytes 11534336 | tf_op jit(solution)/shard_map/pack_rows/pallas_call | solution.py:43
  14.8 1.5 collective-permute-start.1
  16.8 30.9 %collective-permute-done.4.refs_5_ = bf16[4,64,4096]{2,1,0:T(8,128)(2,1)} collective-permute-done((bf16[4,64,4096]{2,1,0:T(8,128)(2,1)}, bf16[4,64,4096]{2,1,0:T(8,128)(2,1)}, u32[]{:S(2)}, u32[]{:S(2)}) %collective-permute-start.4) | collective-permute-done | bytes 2097184 | tf_op jit(solution)/shard_map/ppermute | solution.py:217
  47.7 1.6 collective-permute-start.5
  49.3 10.9 %pack_rows.3 = (bf16[160,4096]{1,0:T(8,128)(2,1)}, bf16[160,4096]{1,0:T(8,128)(2,1)}, bf16[160,4096]{1,0:T(8,128)(2,1)}, bf16[160,4096]{1,0:T(8,128)(2,1)}) custom-call(s32[1,1024]{1,0:T(1,128)} %fusion.16.target_ref, bf16[1024,4096]{1,0:T(8,128)(2,1)} %x_ref.7), custom_call_target="tpu_custom_call" | custom-call | flops 5368709120 | bytes 13631488 | tf_op jit(solution)/shard_map/pack_rows/pallas_call | solution.py:43
  60.1 1.6 collective-permute-start.22
  61.7 1.9 collective-permute-start.11
  63.6 0.8 collective-permute-start.3
  64.5 7.6 %collective-permute-done.5.refs_1_ = bf16[4,64,2048]{2,1,0:T(8,128)(2,1)} collective-permute-done((bf16[4,64,2048]{2,1,0:T(8,128)(2,1)}, bf16[4,64,2048]{2,1,0:T(8,128)(2,1)}, u32[]{:S(2)}, u32[]{:S(2)}) %collective-permute-start.5) | collective-permute-done | bytes 1048608 | tf_op jit(solution)/shard_map/ppermute | solution.py:217
  72.0 1.3 collective-permute-start.6
  73.9 32.9 %collective-permute-done.3.refs_3_ = bf16[96,4096]{1,0:T(8,128)(2,1)} collective-permute-done((bf16[96,4096]{1,0:T(8,128)(2,1)}, bf16[96,4096]{1,0:T(8,128)(2,1)}, u32[]{:S(2)}, u32[]{:S(2)}) %collective-permute-start.3) | collective-permute-done | bytes 786464 | tf_op jit(solution)/shard_map/ppermute | solution.py:217
  106.8 2.4 collective-permute-start.24
  109.3 1.0 slice.28
  110.3 3.3 %collective-permute-start.16 = (bf16[2,64,4096]{2,1,0:T(8,128)(2,1)}, bf16[2,64,4096]{2,1,0:T(8,128)(2,1)}, u32[]{:S(2)}, u32[]{:S(2)}) collective-permute-start(bf16[2,64,4096]{2,1,0:T(8,128)(2,1)} %slice.28), channel_id=1, source_target_pairs={{8,0},{10,2},{12,4},{14,6},{16,24},{18,26},{20,28},{22,30},{9,1},{... | collective-permute-start | bytes 3145736 | tf_op jit(solution)/shard_map/ppermute | solution.py:217
  113.6 2.4 collective-permute-start.12
  116.0 1.3 collective-permute-start.7
  117.3 23.6 %project_half.3 = bf16[1024,2048]{1,0:T(8,128)(2,1)} custom-call(s32[1]{0:T(128)} %bitcast.4.place_ref, bf16[1024,4096]{1,0:T(8,128)(2,1)} %x_ref.7, bf16[4096,4096]{1,0:T(8,128)(2,1)} %w_ref.3), custom_call_target="tpu_custom_call" | custom-call | flops 17179869184 | bytes 29360128 | tf_op jit(solution)/shard_map/project_half/pallas_call | solution.py:65
  141.0 1.3 collective-permute-start.8
  142.3 1.5 broadcast_select_fusion
  143.8 3.5 %collective-permute-done.23.refs_2_ = bf16[160,4096]{1,0:T(8,128)(2,1)} collective-permute-done((bf16[160,4096]{1,0:T(8,128)(2,1)}, bf16[160,4096]{1,0:T(8,128)(2,1)}, u32[]{:S(2)}, u32[]{:S(2)}) %collective-permute-start.23) | collective-permute-done | bytes 1310752 | tf_op jit(solution)/shard_map/ppermute | solution.py:217
  147.4 9.5 %down_rows.3 = f32[10,64,64]{2,1,0:T(8,128)} custom-call(bf16[160,4096]{1,0:T(8,128)(2,1)} %get-tuple-element.54.refs_0_, bf16[160,4096]{1,0:T(8,128)(2,1)} %copy-done.2, bf16[160,4096]{1,0:T(8,128)(2,1)} %collective-permute-done.23.refs_2_, bf16[160,4096]{1,0:T(8,128)(2,1)} %collective-permute-done.24.refs_3_, bf16[4,64,4096]{2,1,0:T(8,128)(2,1)} %bitcast.10, ...), custom_call_target="tpu_custom_call" | custom-call | flops 335544320 | bytes 10485760 | tf_op jit(solution)/shard_map/down_rows/pallas_call | solution.py:110
  156.9 6.1 %collective-permute-start.17 = (bf16[4,64,2048]{2,1,0:T(8,128)(2,1)}, bf16[4,64,2048]{2,1,0:T(8,128)(2,1)}, u32[]{:S(2)}, u32[]{:S(2)}) collective-permute-start(bf16[4,64,2048]{2,1,0:T(8,128)(2,1)} %collective-permute-done.11), channel_id=1, source_target_pairs={{8,0},{10,2},{12,4},{14,6},{16,24},{18,26},{20,28},{22,30},{9,1},{... | collective-permute-start | bytes 3145736 | tf_op jit(solution)/shard_map/ppermute | solution.py:217
  163.0 2.3 collective-permute-start.13
  165.4 1.3 collective-permute-start.9
  166.7 23.7 %project_half.2.own_ref = bf16[1024,2048]{1,0:T(8,128)(2,1)} custom-call(s32[1]{0:T(128)} %bitcast.3.place_ref, bf16[1024,4096]{1,0:T(8,128)(2,1)} %x_ref.7, bf16[4096,4096]{1,0:T(8,128)(2,1)} %w_ref.3), custom_call_target="tpu_custom_call" | custom-call | flops 17179869184 | bytes 29360128 | tf_op jit(solution)/shard_map/project_half/pallas_call | solution.py:65
  190.9 1.7 add_convert_fusion.1.y_ref
  192.6 5.5 %collective-permute-start.18 = (bf16[4,64,2048]{2,1,0:T(8,128)(2,1)}, bf16[4,64,2048]{2,1,0:T(8,128)(2,1)S(1)}, u32[]{:S(2)}, u32[]{:S(2)}) collective-permute-start(bf16[4,64,2048]{2,1,0:T(8,128)(2,1)} %collective-permute-done.12), channel_id=1, source_target_pairs={{8,0},{10,2},{12,4},{14,6},{16,24},{18,26},{20,28},{22,30},{9,1},{... | collective-permute-start | bytes 3145736 | tf_op jit(solution)/shard_map/ppermute | solution.py:217
  198.0 1.3 broadcast_select_fusion.2
  199.4 13.5 %collective-permute-done.13.refs_9_ = bf16[4,64,4096]{2,1,0:T(8,128)(2,1)S(1)} collective-permute-done((bf16[4,64,4096]{2,1,0:T(8,128)(2,1)}, bf16[4,64,4096]{2,1,0:T(8,128)(2,1)S(1)}, u32[]{:S(2)}, u32[]{:S(2)}) %collective-permute-start.13) | collective-permute-done | bytes 2097184 | tf_op jit(solution)/shard_map/ppermute | solution.py:217
  212.8 1.4 copy-done
  214.2 7.3 %down_rows.2 = f32[6,128,64]{2,1,0:T(8,128)} custom-call(bf16[96,4096]{1,0:T(8,128)(2,1)} %get-tuple-element.40.refs_0_, bf16[96,4096]{1,0:T(8,128)(2,1)} %collective-permute-done.1.refs_1_, bf16[96,4096]{1,0:T(8,128)(2,1)} %copy-done.4, bf16[96,4096]{1,0:T(8,128)(2,1)} %collective-permute-done.3.refs_3_, bf16[96,4096]{1,0:T(8,128)(2,1)} %collective-permute-done.6.refs_4_, ...), custom_call_target="tpu_custom_call" | custom-call | flops 402653184 | bytes 9437184 | tf_op jit(solution)/shard_map/down_rows/pallas_call | solution.py:110
  221.6 1.1 fusion.19
  222.7 7.8 %lift_rows.3 = (bf16[160,2048]{1,0:T(8,128)(2,1)}, bf16[160,2048]{1,0:T(8,128)(2,1)}, bf16[160,2048]{1,0:T(8,128)(2,1)}, bf16[160,2048]{1,0:T(8,128)(2,1)}) custom-call(bf16[10,64,64]{2,1,0:T(8,128)(2,1)} %add_convert_fusion.1.y_ref, bf16[4,64,2048]{2,1,0:T(8,128)(2,1)} %refs_0_.1, bf16[4,64,2048]{2,1,0:T(8,128)(2,1)} %collective-permute-done.5.refs_1_, ...), custom_call_target="tpu_custom_call" | custom-call | flops 167772160 | bytes 5242880 | tf_op jit(solution)/shard_map/lift_rows/pallas_call | solution.py:140
  230.5 1.5 collective-permute-start.26
  232.6 1.5 collective-permute-start.28
  234.1 1.5 collective-permute-start.15
  235.6 2.3 broadcast_select_fusion.1.refs_1_
  238.6 5.1 %lift_rows.2 = (bf16[96,2048]{1,0:T(8,128)(2,1)}, bf16[96,2048]{1,0:T(8,128)(2,1)}, bf16[96,2048]{1,0:T(8,128)(2,1)}, bf16[96,2048]{1,0:T(8,128)(2,1)}) custom-call(bf16[6,64,64]{2,1,0:T(8,128)(2,1)} %slice_select_fusion.y_ref, bf16[2,64,2048]{2,1,0:T(8,128)(2,1)} %get-tuple-element.68.refs_0_, bf16[4,64,2048]{2,1,0:T(8,128)(2,1)} %broadcast_select_fusion.1.refs_1_), custom_call_target="tpu_custom_call" | custom-call | flops 100663296 | bytes 3145728 | tf_op jit(solution)/shard_map/lift_rows/pallas_call | solution.py:140
  243.7 1.5 collective-permute-start.19
  245.8 2.6 collective-permute-done.26.rest_5_
  248.3 1.4 collective-permute-start.21
  249.8 2.3 select_add_fusion.target_ref
  252.1 11.8 %collective-permute-done.27.rest_6_ = bf16[160,2048]{1,0:T(8,128)(2,1)S(1)} collective-permute-done((bf16[160,2048]{1,0:T(8,128)(2,1)}, bf16[160,2048]{1,0:T(8,128)(2,1)S(1)}, u32[]{:S(2)}, u32[]{:S(2)}) %collective-permute-start.27) | collective-permute-done | bytes 655392 | tf_op jit(solution)/shard_map/ppermute | solution.py:217
  263.9 6.9 %collective-permute-done.19.rest_1_ = bf16[96,2048]{1,0:T(8,128)(2,1)S(1)} collective-permute-done((bf16[96,2048]{1,0:T(8,128)(2,1)}, bf16[96,2048]{1,0:T(8,128)(2,1)S(1)}, u32[]{:S(2)}, u32[]{:S(2)}) %collective-permute-start.19) | collective-permute-done | bytes 393248 | tf_op jit(solution)/shard_map/ppermute | solution.py:217
  270.8 9.2 %collective-permute-done.20.rest_2_ = bf16[96,2048]{1,0:T(8,128)(2,1)S(1)} collective-permute-done((bf16[96,2048]{1,0:T(8,128)(2,1)}, bf16[96,2048]{1,0:T(8,128)(2,1)S(1)}, u32[]{:S(2)}, u32[]{:S(2)}) %collective-permute-start.20) | collective-permute-done | bytes 393248 | tf_op jit(solution)/shard_map/ppermute | solution.py:217
  280.9 10.1 %finish_rows.1 = bf16[1024,2048]{1,0:T(8,128)(2,1)} custom-call(s32[1024,1]{1,0:T(8,128)} %select_add_fusion.target_ref, bf16[1024,2048]{1,0:T(8,128)(2,1)} %project_half.2.own_ref, bf16[1024,2048]{1,0:T(8,128)(2,1)} %collective-permute-done.other_ref, bf16[96,2048]{1,0:T(8,128)(2,1)} %get-tuple-element.50.rest_0_, bf16[96,2048]{1,0:T(8,128)(2,1)} %copy-done.9, ...), custom_call_target="tpu_custom_call" | custom-call | flops 4294967296 | bytes 16777216 | tf_op jit(solution)/shard_map/finish_rows/pallas_call | solution.py:171
  (59 shorter events, 6.4 us)
Async XLA Ops:
  0.0 47.7 %collective-permute-start.4 = (bf16[4,64,4096]{2,1,0:T(8,128)(2,1)}, bf16[4,64,4096]{2,1,0:T(8,128)(2,1)}, u32[]{:S(2)}, u32[]{:S(2)}) collective-permute-start(bf16[4,64,4096]{2,1,0:T(8,128)(2,1)} %bitcast.8), channel_id=1, source_target_pairs={{0,8},{2,10},{4,12},{6,14},{8,0},{10,2},{12,4},{14,6},{16,24},{18,... | collective-permute-start | bytes 6291464 | tf_op jit(solution)/shard_map/ppermute | solution.py:217
  1.6 60.1 %collective-permute-start.10 = (bf16[4,64,4096]{2,1,0:T(8,128)(2,1)}, bf16[4,64,4096]{2,1,0:T(8,128)(2,1)S(1)}, u32[]{:S(2)}, u32[]{:S(2)}) collective-permute-start(bf16[4,64,4096]{2,1,0:T(8,128)(2,1)} %bitcast.9), channel_id=1, source_target_pairs={{8,16},{10,18},{12,20},{14,22},{16,8},{18,10},{20,12},{22,14},{9,1... | collective-permute-start | bytes 6291464 | tf_op jit(solution)/shard_map/ppermute | solution.py:217
  14.8 45.4 %collective-permute-start.1 = (bf16[96,4096]{1,0:T(8,128)(2,1)}, bf16[96,4096]{1,0:T(8,128)(2,1)}, u32[]{:S(2)}, u32[]{:S(2)}) collective-permute-start(bf16[96,4096]{1,0:T(8,128)(2,1)} %get-tuple-element.36), channel_id=1, source_target_pairs={{0,2},{2,0},{4,6},{6,4},{8,10},{10,8},{12,14},{14,12},{16,18},{18,... | collective-permute-start | bytes 2359304 | tf_op jit(solution)/shard_map/ppermute | solution.py:217
  16.3 43.9 %collective-permute-start.2 = (bf16[96,4096]{1,0:T(8,128)(2,1)}, bf16[96,4096]{1,0:T(8,128)(2,1)S(1)}, u32[]{:S(2)}, u32[]{:S(2)}) collective-permute-start(bf16[96,4096]{1,0:T(8,128)(2,1)} %get-tuple-element.37), channel_id=1, source_target_pairs={{0,4},{2,6},{4,0},{6,2},{8,12},{10,14},{12,8},{14,10},{16,20},{18,... | collective-permute-start | bytes 2359304 | tf_op jit(solution)/shard_map/ppermute | solution.py:217
  47.7 24.3 %collective-permute-start.5 = (bf16[4,64,2048]{2,1,0:T(8,128)(2,1)}, bf16[4,64,2048]{2,1,0:T(8,128)(2,1)}, u32[]{:S(2)}, u32[]{:S(2)}) collective-permute-start(bf16[4,64,2048]{2,1,0:T(8,128)(2,1)} %refs_0_.1), channel_id=1, source_target_pairs={{0,8},{2,10},{4,12},{6,14},{8,0},{10,2},{12,4},{14,6},{16,24},{18,... | collective-permute-start | bytes 3145736 | tf_op jit(solution)/shard_map/ppermute | solution.py:217
  60.1 1.6 copy-start.4
  60.1 46.7 %collective-permute-start.22 = (bf16[160,4096]{1,0:T(8,128)(2,1)}, bf16[160,4096]{1,0:T(8,128)(2,1)S(1)}, u32[]{:S(2)}, u32[]{:S(2)}) collective-permute-start(bf16[160,4096]{1,0:T(8,128)(2,1)} %get-tuple-element.56), channel_id=1, source_target_pairs={{0,2},{2,0},{4,6},{6,4},{8,10},{10,8},{12,14},{14,12},{16,18},{18,... | collective-permute-start | bytes 3932168 | tf_op jit(solution)/shard_map/ppermute | solution.py:217
  61.7 51.9 %collective-permute-start.11 = (bf16[4,64,2048]{2,1,0:T(8,128)(2,1)}, bf16[4,64,2048]{2,1,0:T(8,128)(2,1)}, u32[]{:S(2)}, u32[]{:S(2)}) collective-permute-start(bf16[4,64,2048]{2,1,0:T(8,128)(2,1)} %refs_0_.1), channel_id=1, source_target_pairs={{8,16},{10,18},{12,20},{14,22},{16,8},{18,10},{20,12},{22,14},{9,1... | collective-permute-start | bytes 3145736 | tf_op jit(solution)/shard_map/ppermute | solution.py:217
  63.6 43.2 %collective-permute-start.3 = (bf16[96,4096]{1,0:T(8,128)(2,1)}, bf16[96,4096]{1,0:T(8,128)(2,1)}, u32[]{:S(2)}, u32[]{:S(2)}) collective-permute-start(bf16[96,4096]{1,0:T(8,128)(2,1)} %get-tuple-element.38), channel_id=1, source_target_pairs={{0,6},{2,4},{4,2},{6,0},{8,14},{10,12},{12,10},{14,8},{16,22},{18,... | collective-permute-start | bytes 2359304 | tf_op jit(solution)/shard_map/ppermute | solution.py:217
  72.0 44.0 %collective-permute-start.6 = (bf16[96,4096]{1,0:T(8,128)(2,1)}, bf16[96,4096]{1,0:T(8,128)(2,1)}, u32[]{:S(2)}, u32[]{:S(2)}) collective-permute-start(bf16[96,4096]{1,0:T(8,128)(2,1)} %get-tuple-element.40.refs_0_), channel_id=1, source_target_pairs={{0,8},{2,10},{4,12},{6,14},{24,16},{26,18},{28,20},{30,22},{1,9},{... | collective-permute-start | bytes 2359304 | tf_op jit(solution)/shard_map/ppermute | solution.py:217
  73.3 74.0 %collective-permute-start.23 = (bf16[160,4096]{1,0:T(8,128)(2,1)}, bf16[160,4096]{1,0:T(8,128)(2,1)}, u32[]{:S(2)}, u32[]{:S(2)}) collective-permute-start(bf16[160,4096]{1,0:T(8,128)(2,1)} %get-tuple-element.58), channel_id=1, source_target_pairs={{0,4},{2,6},{4,0},{6,2},{8,12},{10,14},{12,8},{14,10},{16,20},{18,... | collective-permute-start | bytes 3932168 | tf_op jit(solution)/shard_map/ppermute | solution.py:217
  106.8 34.1 %copy-start.2 = (bf16[160,4096]{1,0:T(8,128)(2,1)}, bf16[160,4096]{1,0:T(8,128)(2,1)S(1)}, u32[]{:S(2)}) copy-start(bf16[160,4096]{1,0:T(8,128)(2,1)S(1)} %collective-permute-done.22.refs_1_) | copy-start | bytes 3932164
  106.8 40.6 %collective-permute-start.24 = (bf16[160,4096]{1,0:T(8,128)(2,1)}, bf16[160,4096]{1,0:T(8,128)(2,1)}, u32[]{:S(2)}, u32[]{:S(2)}) collective-permute-start(bf16[160,4096]{1,0:T(8,128)(2,1)} %get-tuple-element.60), channel_id=1, source_target_pairs={{0,6},{2,4},{4,2},{6,0},{8,14},{10,12},{12,10},{14,8},{16,22},{18,... | collective-permute-start | bytes 3932168 | tf_op jit(solution)/shard_map/ppermute | solution.py:217
  110.3 30.7 %collective-permute-start.16 = (bf16[2,64,4096]{2,1,0:T(8,128)(2,1)}, bf16[2,64,4096]{2,1,0:T(8,128)(2,1)}, u32[]{:S(2)}, u32[]{:S(2)}) collective-permute-start(bf16[2,64,4096]{2,1,0:T(8,128)(2,1)} %slice.28), channel_id=1, source_target_pairs={{8,0},{10,2},{12,4},{14,6},{16,24},{18,26},{20,28},{22,30},{9,1},{... | collective-permute-start | bytes 3145736 | tf_op jit(solution)/shard_map/ppermute | solution.py:217
  113.6 49.4 %collective-permute-start.12 = (bf16[4,64,2048]{2,1,0:T(8,128)(2,1)}, bf16[4,64,2048]{2,1,0:T(8,128)(2,1)}, u32[]{:S(2)}, u32[]{:S(2)}) collective-permute-start(bf16[4,64,2048]{2,1,0:T(8,128)(2,1)} %collective-permute-done.5.refs_1_), channel_id=1, source_target_pairs={{8,16},{10,18},{12,20},{14,22},{16,8},{18,10},{20,12},{22,14},{9,1... | collective-permute-start | bytes 3145736 | tf_op jit(solution)/shard_map/ppermute | solution.py:217
  116.0 24.9 %collective-permute-start.7 = (bf16[96,4096]{1,0:T(8,128)(2,1)}, bf16[96,4096]{1,0:T(8,128)(2,1)}, u32[]{:S(2)}, u32[]{:S(2)}) collective-permute-start(bf16[96,4096]{1,0:T(8,128)(2,1)} %collective-permute-done.1.refs_1_), channel_id=1, source_target_pairs={{0,8},{2,10},{4,12},{6,14},{24,16},{26,18},{28,20},{30,22},{1,9},{... | collective-permute-start | bytes 2359304 | tf_op jit(solution)/shard_map/ppermute | solution.py:217
  140.9 104.3 %collective-permute-start = (bf16[1024,2048]{1,0:T(8,128)(2,1)}, bf16[1024,2048]{1,0:T(8,128)(2,1)}, u32[]{:S(2)}, u32[]{:S(2)}) collective-permute-start(bf16[1024,2048]{1,0:T(8,128)(2,1)} %project_half.3), channel_id=1, source_target_pairs={{0,1},{1,0},{2,3},{3,2},{4,5},{5,4},{6,7},{7,6},{8,9},{9,8},{10,11... | collective-permute-start | bytes 12582920 | tf_op jit(solution)/shard_map/ppermute | solution.py:265
  141.0 24.3 %collective-permute-start.8 = (bf16[96,4096]{1,0:T(8,128)(2,1)}, bf16[96,4096]{1,0:T(8,128)(2,1)S(1)}, u32[]{:S(2)}, u32[]{:S(2)}) collective-permute-start(bf16[96,4096]{1,0:T(8,128)(2,1)} %copy-done.4), channel_id=1, source_target_pairs={{0,8},{2,10},{4,12},{6,14},{24,16},{26,18},{28,20},{30,22},{1,9},{... | collective-permute-start | bytes 2359304 | tf_op jit(solution)/shard_map/ppermute | solution.py:217
  156.9 34.0 %collective-permute-start.25 = (f32[10,64,64]{2,1,0:T(8,128)}, f32[10,64,64]{2,1,0:T(8,128)}, u32[]{:S(2)}, u32[]{:S(2)}) collective-permute-start(f32[10,64,64]{2,1,0:T(8,128)} %down_rows.3), channel_id=1, source_target_pairs={{0,1},{1,0},{2,3},{3,2},{4,5},{5,4},{6,7},{7,6},{8,9},{9,8},{10,11... | collective-permute-start | bytes 491528 | tf_op jit(solution)/shard_map/ppermute | solution.py:269
  156.9 35.7 %collective-permute-start.17 = (bf16[4,64,2048]{2,1,0:T(8,128)(2,1)}, bf16[4,64,2048]{2,1,0:T(8,128)(2,1)}, u32[]{:S(2)}, u32[]{:S(2)}) collective-permute-start(bf16[4,64,2048]{2,1,0:T(8,128)(2,1)} %collective-permute-done.11), channel_id=1, source_target_pairs={{8,0},{10,2},{12,4},{14,6},{16,24},{18,26},{20,28},{22,30},{9,1},{... | collective-permute-start | bytes 3145736 | tf_op jit(solution)/shard_map/ppermute | solution.py:217
  163.0 49.8 %collective-permute-start.13 = (bf16[4,64,4096]{2,1,0:T(8,128)(2,1)}, bf16[4,64,4096]{2,1,0:T(8,128)(2,1)S(1)}, u32[]{:S(2)}, u32[]{:S(2)}) collective-permute-start(bf16[4,64,4096]{2,1,0:T(8,128)(2,1)} %collective-permute-done.4.refs_5_), channel_id=1, source_target_pairs={{8,16},{10,18},{12,20},{14,22},{16,8},{18,10},{20,12},{22,14},{9,1... | collective-permute-start | bytes 6291464 | tf_op jit(solution)/shard_map/ppermute | solution.py:217
  165.4 25.0 %copy-start.5 = (bf16[96,4096]{1,0:T(8,128)(2,1)}, bf16[96,4096]{1,0:T(8,128)(2,1)S(1)}, u32[]{:S(2)}) copy-start(bf16[96,4096]{1,0:T(8,128)(2,1)S(1)} %collective-permute-done.8.refs_6_) | copy-start | bytes 2359300
  165.4 34.0 %collective-permute-start.9 = (bf16[96,4096]{1,0:T(8,128)(2,1)}, bf16[96,4096]{1,0:T(8,128)(2,1)}, u32[]{:S(2)}, u32[]{:S(2)}) collective-permute-start(bf16[96,4096]{1,0:T(8,128)(2,1)} %collective-permute-done.3.refs_3_), channel_id=1, source_target_pairs={{0,8},{2,10},{4,12},{6,14},{24,16},{26,18},{28,20},{30,22},{1,9},{... | collective-permute-start | bytes 2359304 | tf_op jit(solution)/shard_map/ppermute | solution.py:217
  166.7 24.2 %copy-start.3 = (f32[10,64,64]{2,1,0:T(8,128)S(1)}, f32[10,64,64]{2,1,0:T(8,128)}, u32[]{:S(2)}) copy-start(f32[10,64,64]{2,1,0:T(8,128)} %down_rows.3) | copy-start | bytes 491524
  192.6 41.6 %collective-permute-start.18 = (bf16[4,64,2048]{2,1,0:T(8,128)(2,1)}, bf16[4,64,2048]{2,1,0:T(8,128)(2,1)S(1)}, u32[]{:S(2)}, u32[]{:S(2)}) collective-permute-start(bf16[4,64,2048]{2,1,0:T(8,128)(2,1)} %collective-permute-done.12), channel_id=1, source_target_pairs={{8,0},{10,2},{12,4},{14,6},{16,24},{18,26},{20,28},{22,30},{9,1},{... | collective-permute-start | bytes 3145736 | tf_op jit(solution)/shard_map/ppermute | solution.py:217
  212.8 1.4 copy-start
  221.5 12.6 %copy-start.1 = (f32[6,128,64]{2,1,0:T(8,128)S(1)}, f32[6,128,64]{2,1,0:T(8,128)}, u32[]{:S(2)}) copy-start(f32[6,128,64]{2,1,0:T(8,128)} %down_rows.2) | copy-start | bytes 589828
  221.5 11.1 %collective-permute-start.14 = (f32[6,128,64]{2,1,0:T(8,128)}, f32[6,128,64]{2,1,0:T(8,128)S(1)}, u32[]{:S(2)}, u32[]{:S(2)}) collective-permute-start(f32[6,128,64]{2,1,0:T(8,128)} %down_rows.2), channel_id=1, source_target_pairs={{0,1},{1,0},{2,3},{3,2},{4,5},{5,4},{6,7},{7,6},{8,9},{9,8},{10,11... | collective-permute-start | bytes 589832 | tf_op jit(solution)/shard_map/ppermute | solution.py:269
  230.5 17.8 %collective-permute-start.26 = (bf16[160,2048]{1,0:T(8,128)(2,1)}, bf16[160,2048]{1,0:T(8,128)(2,1)S(1)}, u32[]{:S(2)}, u32[]{:S(2)}) collective-permute-start(bf16[160,2048]{1,0:T(8,128)(2,1)} %get-tuple-element.62), channel_id=1, source_target_pairs={{0,2},{2,0},{4,6},{6,4},{8,10},{10,8},{12,14},{14,12},{16,18},{18,... | collective-permute-start | bytes 1966088 | tf_op jit(solution)/shard_map/ppermute | solution.py:217
  232.1 31.8 %collective-permute-start.27 = (bf16[160,2048]{1,0:T(8,128)(2,1)}, bf16[160,2048]{1,0:T(8,128)(2,1)S(1)}, u32[]{:S(2)}, u32[]{:S(2)}) collective-permute-start(bf16[160,2048]{1,0:T(8,128)(2,1)} %get-tuple-element.63), channel_id=1, source_target_pairs={{0,4},{2,6},{4,0},{6,2},{8,12},{10,14},{12,8},{14,10},{16,20},{18,... | collective-permute-start | bytes 1966088 | tf_op jit(solution)/shard_map/ppermute | solution.py:217
  232.6 31.3 %collective-permute-start.28 = (bf16[160,2048]{1,0:T(8,128)(2,1)}, bf16[160,2048]{1,0:T(8,128)(2,1)S(1)}, u32[]{:S(2)}, u32[]{:S(2)}) collective-permute-start(bf16[160,2048]{1,0:T(8,128)(2,1)} %get-tuple-element.64), channel_id=1, source_target_pairs={{0,6},{2,4},{4,2},{6,0},{8,14},{10,12},{12,10},{14,8},{16,22},{18,... | collective-permute-start | bytes 1966088 | tf_op jit(solution)/shard_map/ppermute | solution.py:217
  234.1 3.8 %collective-permute-start.15 = (bf16[6,64,64]{2,1,0:T(8,128)(2,1)S(1)}, bf16[6,64,64]{2,1,0:T(8,128)(2,1)S(1)}, u32[]{:S(2)}, u32[]{:S(2)}) collective-permute-start(bf16[6,64,64]{2,1,0:T(8,128)(2,1)S(1)} %slice.27), channel_id=1, source_target_pairs={{8,0},{10,2},{12,4},{14,6},{16,24},{18,26},{20,28},{22,30},{9,1},{... | collective-permute-start | bytes 147464 | tf_op jit(solution)/shard_map/ppermute | solution.py:217
  243.7 27.1 %collective-permute-start.19 = (bf16[96,2048]{1,0:T(8,128)(2,1)}, bf16[96,2048]{1,0:T(8,128)(2,1)S(1)}, u32[]{:S(2)}, u32[]{:S(2)}) collective-permute-start(bf16[96,2048]{1,0:T(8,128)(2,1)} %get-tuple-element.51), channel_id=1, source_target_pairs={{0,2},{2,0},{4,6},{6,4},{8,10},{10,8},{12,14},{14,12},{16,18},{18,... | collective-permute-start | bytes 1179656 | tf_op jit(solution)/shard_map/ppermute | solution.py:217
  245.2 34.8 %collective-permute-start.20 = (bf16[96,2048]{1,0:T(8,128)(2,1)}, bf16[96,2048]{1,0:T(8,128)(2,1)S(1)}, u32[]{:S(2)}, u32[]{:S(2)}) collective-permute-start(bf16[96,2048]{1,0:T(8,128)(2,1)} %get-tuple-element.52), channel_id=1, source_target_pairs={{0,4},{2,6},{4,0},{6,2},{8,12},{10,14},{12,8},{14,10},{16,20},{18,... | collective-permute-start | bytes 1179656 | tf_op jit(solution)/shard_map/ppermute | solution.py:217
  248.3 31.7 %copy-start.6 = (bf16[160,2048]{1,0:T(8,128)(2,1)}, bf16[160,2048]{1,0:T(8,128)(2,1)S(1)}, u32[]{:S(2)}) copy-start(bf16[160,2048]{1,0:T(8,128)(2,1)S(1)} %collective-permute-done.26.rest_5_) | copy-start | bytes 1966084
  248.3 31.7 %collective-permute-start.21 = (bf16[96,2048]{1,0:T(8,128)(2,1)}, bf16[96,2048]{1,0:T(8,128)(2,1)S(1)}, u32[]{:S(2)}, u32[]{:S(2)}) collective-permute-start(bf16[96,2048]{1,0:T(8,128)(2,1)} %get-tuple-element.53), channel_id=1, source_target_pairs={{0,6},{2,4},{4,2},{6,0},{8,14},{10,12},{12,10},{14,8},{16,22},{18,... | collective-permute-start | bytes 1179656 | tf_op jit(solution)/shard_map/ppermute | solution.py:217
  263.9 16.2 %copy-start.7 = (bf16[160,2048]{1,0:T(8,128)(2,1)}, bf16[160,2048]{1,0:T(8,128)(2,1)S(1)}, u32[]{:S(2)}) copy-start(bf16[160,2048]{1,0:T(8,128)(2,1)S(1)} %collective-permute-done.27.rest_6_) | copy-start | bytes 1966084
  263.9 16.2 %copy-start.8 = (bf16[160,2048]{1,0:T(8,128)(2,1)}, bf16[160,2048]{1,0:T(8,128)(2,1)S(1)}, u32[]{:S(2)}) copy-start(bf16[160,2048]{1,0:T(8,128)(2,1)S(1)} %collective-permute-done.28.rest_7_) | copy-start | bytes 1966084
  270.8 9.2 %copy-start.9 = (bf16[96,2048]{1,0:T(8,128)(2,1)}, bf16[96,2048]{1,0:T(8,128)(2,1)S(1)}, u32[]{:S(2)}) copy-start(bf16[96,2048]{1,0:T(8,128)(2,1)S(1)} %collective-permute-done.19.rest_1_) | copy-start | bytes 1179652
  280.0 0.8 copy-start.10
  280.0 0.9 copy-start.11

commit v3 on v2

--- a/solution.py
+++ b/solution.py
@@ -39,7 +39,7 @@
 
 def pack(target, x, first, part, parts):
     rows, width = x.shape
-    tile = 512
+    tile = 1024
     return pl.pallas_call(
         functools.partial(pack_kernel, first),
         grid=(width // tile,),
@@ -80,107 +80,157 @@
     )(half.reshape(1), x, w)
 
 
-def spans(arrays):
-    ends, start = [], 0
-    for array in arrays:
-        ends.append((start, start + array.shape[0]))
-        start += array.shape[0]
-    return ends
-
-
-def picked(start, end):
-    return lambda i: (jnp.clip(i - start, 0, end - start - 1), 0, 0)
-
-
-def down_kernel(ranges, *refs):
-    xs, ws, o_ref = refs[: -1 - len(ranges)], refs[-1 - len(ranges) : -1], refs[-1]
+def factor_specs(groups, rank, tile):
+    specs = []
+    for arrays, first, count in groups:
+        shape = (count, rank, tile)
+        specs += [pl.BlockSpec(shape, lambda k, at=first // count: (at, 0, k))] * len(arrays)
+    return specs
+
+
+def factors(refs, groups):
+    at = start = 0
+    for held, count in groups:
+        total = functools.reduce(jnp.add, [ref[...] for ref in refs[at : at + held]])
+        yield start, count, total.reshape(count * total.shape[1], total.shape[2])
+        at += held
+        start += count
+
+
+def flat(groups):
+    return [array for arrays, _, _ in groups for array in arrays]
+
+
+def shape_of(groups):
+    return [(len(arrays), count) for arrays, _, count in groups]
+
+
+def down_kernel(groups, sources, *refs):
+    xs, ws, o_ref = refs[:sources], refs[sources:-1], refs[-1]
     step = pl.program_id(0)
-    rows = jnp.concatenate([x[...] for x in xs], axis=0)
-    for w_ref, (start, end) in zip(ws, ranges):
-
-        @pl.when((step >= start) & (step < end))
-        def _():
-            o_ref[...] = lax.dot_general(rows, w_ref[...], NT, preferred_element_type=jnp.float32)
-
-
-def down(xs, ws):
-    ranges = spans(ws)
-    adapters, (_, rank, width) = ranges[-1][1], ws[0].shape
-    rows = len(xs) * MOST
-    return pl.pallas_call(
-        functools.partial(down_kernel, ranges),
-        grid=(adapters,),
-        in_specs=[pl.BlockSpec((MOST, width), lambda i: (i, 0))] * len(xs)
-        + [pl.BlockSpec((None, rank, width), picked(*span)) for span in ranges],
-        out_specs=pl.BlockSpec((None, rows, rank), lambda i: (i, 0, 0)),
-        out_shape=jax.ShapeDtypeStruct((adapters, rows, rank), jnp.float32),
-        compiler_params=params(),
-        cost_estimate=cost(2 * adapters * rows * rank * width, 2 * adapters * width * (rank + rows)),
+    sides = sources // COLUMNS
+    side_rows = o_ref.shape[0] // sides
+
+    @pl.when(step == 0)
+    def _():
+        o_ref[...] = jnp.zeros_like(o_ref)
+
+    for start, count, w in factors(ws, groups):
+        rank = w.shape[0] // count
+        rows = jnp.concatenate([x[start * MOST : (start + count) * MOST] for x in xs], axis=0)
+        y = lax.dot_general(rows, w, NT, preferred_element_type=jnp.float32)
+        owner = lax.broadcasted_iota(jnp.int32, y.shape, 0) // MOST % count
+        y = jnp.where(owner == lax.broadcasted_iota(jnp.int32, y.shape, 1) // rank, y, 0.0)
+        part = COLUMNS * count * MOST
+        for side in range(sides):
+            at = side * side_rows + start * COLUMNS * MOST
+            o_ref[at : at + part, : w.shape[0]] += y[side * part : (side + 1) * part]
+
+
+def down(xs, groups):
+    served = sum(count for _, _, count in groups)
+    _, rank, width = groups[0][0][0].shape
+    tile = 1024
+    rows = len(xs) * served * MOST
+    wide = max(count for _, _, count in groups) * rank
+
+    def block(section):
+        return pl.BlockSpec((served * MOST, tile), lambda k: (section, k))
+
+    return pl.pallas_call(
+        functools.partial(down_kernel, shape_of(groups), len(xs)),
+        grid=(width // tile,),
+        in_specs=[block(section) for _, section in xs] + factor_specs(groups, rank, tile),
+        out_specs=pl.BlockSpec((rows, wide), lambda k: (0, 0)),
+        out_shape=jax.ShapeDtypeStruct((rows, wide), jnp.float32),
+        compiler_params=params(),
+        cost_estimate=cost(2 * rows * wide * width, 2 * width * (served * rank + rows)),
         name="down_rows",
-    )(*xs, *ws)
-
-
-def lift_kernel(ranges, y_ref, *refs):
-    us, outs = refs[: len(ranges)], refs[len(ranges) :]
-    step = pl.program_id(0)
-    for u_ref, (start, end) in zip(us, ranges):
-
-        @pl.when((step >= start) & (step < end))
-        def _():
-            rows = jnp.dot(y_ref[...], u_ref[...], preferred_element_type=jnp.float32).astype(jnp.bfloat16)
-            for k, out in enumerate(outs):
-                out[...] = rows[k * MOST : (k + 1) * MOST]
-
-
-def lift(y, us):
-    ranges = spans(us)
-    adapters, rows, rank = y.shape
-    columns = us[0].shape[2]
-    parts = rows // MOST
-    return pl.pallas_call(
-        functools.partial(lift_kernel, ranges),
-        grid=(adapters,),
-        in_specs=[pl.BlockSpec((None, rows, rank), lambda i: (i, 0, 0))]
-        + [pl.BlockSpec((None, rank, columns), picked(*span)) for span in ranges],
-        out_specs=[pl.BlockSpec((MOST, columns), lambda i: (i, 0))] * parts,
-        out_shape=[jax.ShapeDtypeStruct((adapters * MOST, columns), jnp.bfloat16)] * parts,
-        compiler_params=params(),
-        cost_estimate=cost(2 * adapters * rows * rank * columns, 2 * adapters * columns * (rank + rows)),
-        name="lift_rows",
-    )(y, *us)
-
-
-def finish_kernel(target_ref, own_ref, other_ref, *rest):
-    pieces, o_ref, onehot = rest[:-2], rest[-2], rest[-1]
+    )(*[x for x, _ in xs], *flat(groups))
+
+
+def lift_kernel(groups, count_y, *refs):
+    outs, y = refs[-1 - COLUMNS : -1], refs[-1]
+    ys, us = refs[:count_y], refs[count_y : -1 - COLUMNS]
 
     @pl.when(pl.program_id(0) == 0)
     def _():
-        place = lax.broadcasted_iota(jnp.int32, onehot.shape, 1)
-        onehot[...] = (place == target_ref[...]).astype(jnp.bfloat16)
-
+        y[...] = functools.reduce(jnp.add, [ref[...] for ref in ys]).astype(jnp.bfloat16)
+
+    for start, count, u in factors(us, groups):
+        part = count * MOST
+        at = start * COLUMNS * MOST
+        low = y[at : at + COLUMNS * part, : u.shape[0]]
+        rows = jnp.dot(low, u, preferred_element_type=jnp.float32).astype(jnp.bfloat16)
+        for k, out in enumerate(outs):
+            out[start * MOST : start * MOST + part] = rows[k * part : (k + 1) * part]
+
+
+def lift(ys, groups):
+    served = sum(count for _, _, count in groups)
+    _, rank, columns = groups[0][0][0].shape
+    tile = 512
+    rows, wide = served * COLUMNS * MOST, ys[0].shape[1]
+    return pl.pallas_call(
+        functools.partial(lift_kernel, shape_of(groups), len(ys)),
+        grid=(columns // tile,),
+        in_specs=[pl.BlockSpec((rows, wide), lambda k: (0, 0))] * len(ys) + factor_specs(groups, rank, tile),
+        out_specs=[pl.BlockSpec((served * MOST, tile), lambda k: (0, k))] * COLUMNS,
+        out_shape=[jax.ShapeDtypeStruct((served * MOST, columns), jnp.bfloat16)] * COLUMNS,
+        scratch_shapes=[pltpu.VMEM((rows, wide), jnp.bfloat16)],
+        compiler_params=params(),
+        cost_estimate=cost(2 * rows * wide * columns, 2 * columns * (served * rank + rows)),
+        name="lift_rows",
+    )(*ys, *flat(groups))
+
+
+def finish_kernel(count, onehot_ref, *rest):
+    bases, pieces, o_ref = rest[:count], rest[count:-1], rest[-1]
     lifted = jnp.concatenate([piece[...] for piece in pieces], axis=0)
-    total = jnp.dot(onehot[...], lifted, preferred_element_type=jnp.float32)
-    base = own_ref[...].astype(jnp.float32) + other_ref[...].astype(jnp.float32)
-    o_ref[...] = (base + total).astype(o_ref.dtype)
-
-
-def finish(target, own, other, pieces):
-    rows, columns = own.shape
+    total = jnp.dot(onehot_ref[...], lifted, preferred_element_type=jnp.float32)
+    for base in bases:
+        total += base[...].astype(jnp.float32)
+    o_ref[...] = total.astype(o_ref.dtype)
+
+
+def finish(onehot, bases, pieces, dtype):
+    rows, columns = bases[0].shape
     tile = 512
-    places = sum(piece.shape[0] for piece in pieces)
-    return pl.pallas_call(
-        finish_kernel,
+    held = onehot.shape[1]
+    return pl.pallas_call(
+        functools.partial(finish_kernel, len(bases)),
         grid=(columns // tile,),
-        in_specs=[pl.BlockSpec((rows, 1), lambda i: (0, 0))]
-        + [pl.BlockSpec((rows, tile), lambda i: (0, i))] * 2
+        in_specs=[pl.BlockSpec((rows, held), lambda i: (0, 0))]
+        + [pl.BlockSpec((rows, tile), lambda i: (0, i)) for _ in bases]
         + [pl.BlockSpec((piece.shape[0], tile), lambda i: (0, i)) for piece in pieces],
         out_specs=pl.BlockSpec((rows, tile), lambda i: (0, i)),
-        out_shape=jax.ShapeDtypeStruct((rows, columns), jnp.bfloat16),
-        scratch_shapes=[pltpu.VMEM((rows, places), jnp.bfloat16)],
-        compiler_params=params(),
-        cost_estimate=cost(2 * rows * places * columns, 8 * rows * columns),
+        out_shape=jax.ShapeDtypeStruct((rows, columns), dtype),
+        compiler_params=params(),
+        cost_estimate=cost(2 * rows * held * columns, 8 * rows * columns),
         name="finish_rows",
-    )(target, own, other, *pieces)
+    )(onehot, *bases, *pieces)
+
+
+def join_kernel(*refs):
+    pieces, o_ref = refs[:-1], refs[-1]
+    rows = pieces[0].shape[0]
+    for k, piece in enumerate(pieces):
+        o_ref[k * rows : (k + 1) * rows] = piece[...]
+
+
+def join(pieces):
+    rows, width = pieces[0].shape
+    tile = 1024
+    return pl.pallas_call(
+        join_kernel,
+        grid=(width // tile,),
+        in_specs=[pl.BlockSpec((rows, tile), lambda k: (0, k))] * len(pieces),
+        out_specs=pl.BlockSpec((rows * len(pieces), tile), lambda k: (0, k)),
+        out_shape=jax.ShapeDtypeStruct((rows * len(pieces), width), pieces[0].dtype),
+        compiler_params=params(),
+        cost_estimate=cost(0, 4 * rows * len(pieces) * width),
+        name="join_rows",
+    )(*pieces)
 
 
 def places(request_adapter, adapter_slot, total):
@@ -208,7 +258,6 @@
     rest = 4 * owned - served
     me = lax.axis_index("rep")
     plane, column = me // COLUMNS, me % COLUMNS
-    inner = (plane == 1) | (plane == 2)
     every = range(COLUMNS * PLANES)
     inside = [r for r in every if r // COLUMNS in (1, 2)]
     outside = [r for r in every if r // COLUMNS in (0, 3)]
@@ -235,49 +284,58 @@
 
     down_own = jnp.swapaxes(slot_down_weight, 1, 2)
     up_own = slot_up_weight
+    tp = lax.axis_index("tp")
     down_pair = send(down_own, pair)
     down_near = send(down_own, across)
 
+    split = COLUMNS * rest * MOST
     away = pack(target[None, :], hidden_input, 0, rest * MOST, COLUMNS)
-    home = pack(target[None, :], hidden_input, COLUMNS * rest * MOST, served * MOST, COLUMNS)
+    home = pack(target[None, :], after(hidden_input, away[0]), split, served * MOST, COLUMNS)
+    spots = lax.broadcasted_iota(jnp.int32, (target.shape[0], 4 * owned * COLUMNS * MOST), 1)
+    onehot = (target[:, None] == spots).astype(jnp.bfloat16)
+    back_away, back_home = onehot[:, :split], onehot[:, split:]
     away = [away[0]] + [send(away[d], turn[d]) for d in range(1, COLUMNS)]
-
-    up_pair = send(up_own, pair, down_pair)
-    up_near = send(up_own, across, down_near)
-    beside = [home[0]] + [send(home[d], turn[d], away[1], away[2]) for d in (1, 2)]
-    beside.append(send(home[3], turn[3], away[3], beside[1]))
-
-    down_out = send(down_near[:cut], outward, up_pair)
-    up_far = send(up_pair, across, up_near)
-    moved, last = [], up_pair
-    for rows in away:
-        last = send(rows, inward, last)
-        moved.append(last)
-    down_far = send(down_pair, across, up_far)
+    given = project(1 - tp, after(hidden_input, home[0], back_away, back_home), query_weight)
+
+    up_pair = send(up_own, pair, down_pair, given)
+    up_near = send(up_own, across, down_near, given)
+    beside = [home[0]] + [send(home[d], turn[d], away[d], given) for d in (1, 2)]
+    moving = join(away)
+    base_own = project(tp, after(hidden_input, down_pair, down_near, moving), query_weight)
+
+    moved = send(moving, inward, up_pair, beside[1], beside[2], base_own)
+    down_out = send(down_near[:cut], outward, up_pair, base_own)
+    up_far = send(up_pair, across, up_near, base_own)
+    beside.append(send(home[3], turn[3], beside[1], beside[2], base_own))
+    down_far = send(down_pair, across, up_far, down_out)
     up_near_out = send(up_near, outward, down_out)
-    up_far_out = send(up_far, outward, up_near_out)
-    down_part = jnp.where(inner, down_near[:cut], down_out)
-    up_near = jnp.where(inner, up_near, up_near_out)
-    up_far = jnp.where(inner, up_far, up_far_out)
-
-    tp = lax.axis_index("tp")
-    given = project(1 - tp, hidden_input, query_weight)
-    base_other = lax.ppermute(given, "tp", SWAP)
-    base_own = project(tp, hidden_input, query_weight)
-
-    def both(y):
-        return (y + lax.ppermute(y, "tp", SWAP)).astype(jnp.bfloat16)
-
-    low = both(down(beside, [down_own, down_pair, down_part]))
-    rows = lift(low, [up_own, up_pair, up_near[:cut]])
-    lifted = [rows[0]] + [send(rows[d], turn[d]) for d in range(1, COLUMNS)]
-
-    half = COLUMNS * MOST
-    low = both(down(away + moved, [down_near[cut:], down_far]))
-    low = jnp.where(inner, low[:, :half], send(low[:, half:], outward))
-    rows = lift(low, [up_near[cut:], up_far])
-    lifted = [rows[0]] + [send(rows[d], turn[d]) for d in range(1, COLUMNS)] + lifted
-    return finish(target[:, None], base_own, base_other, lifted)
+    base_other = lax.ppermute(after(given, beside[3]), "tp", SWAP)
+
+    def swapped(y):
+        return lax.ppermute(y, "tp", SWAP)
+
+    low = down(
+        [(rows, 0) for rows in beside],
+        [([down_own], 0, owned), ([down_pair], 0, owned), ([down_near, down_out], 0, cut)],
+    )
+    up_far_out = send(up_far, outward, up_near_out, low)
+    rows = lift(
+        [low, swapped(low)], [([up_own], 0, owned), ([up_pair], 0, owned), ([up_near, up_near_out], 0, cut)]
+    )
+    lifted_home = [rows[0]] + [send(rows[d], turn[d]) for d in range(1, COLUMNS)]
+
+    low = down(
+        [(after(away[0], up_far_out, rows[0]), 0)] + [(rows, 0) for rows in away[1:]] + [(moved, d) for d in range(COLUMNS)],
+        [([down_near], cut, owned - cut), ([down_far], 0, owned)],
+    )
+    low = (low + swapped(low)).astype(jnp.bfloat16)
+    rows = lift(
+        [low, send(low[low.shape[0] // 2 :], outward)],
+        [([up_near, up_near_out], cut, owned - cut), ([up_far, up_far_out], 0, owned)],
+    )
+    lifted_away = [rows[0]] + [send(rows[d], turn[d]) for d in range(1, COLUMNS)]
+    part = finish(back_home, [after(base_own, rows[0]), base_other], lifted_home, jnp.float32)
+    return finish(back_away, [part], lifted_away, jnp.bfloat16)
 
 
 def by_gather(hidden_input, query_weight, slot_down_weight, slot_up_weight, request_adapter, adapter_slot):

time: 293 us -> 240 us (0.82)
  the two profiles are of different devices: /device:TPU:20 before, /device:TPU:0 now
where the time goes in v3:
time: 240 us; the launch traced here: 239 us
  Pallas kernels  110 us (46%)
  waiting for transfers between devices  77.1 us (32%)
  starting transfers between devices  38.2 us (16%)
  local copies, waits for them, and re-layouts  9.93 us (4%)
  other arithmetic  3.14 us (1%)
    ppermute x23, waiting for transfers between devices, send(): return lax.ppermute(after(x, *earlier) if earlier else x, 'rep', pairs)  74.8 us
    pallas_call x2, Pallas kernels, project(): pl.pallas_call(project_kernel, grid_spec=pltpu.PrefetchScalarGridSpec(num...  47.4 us
    ppermute x23, starting transfers between devices, send(): return lax.ppermute(after(x, *earlier) if earlier else x, 'rep', pairs)  38.2 us
    pallas_call x2, Pallas kernels, finish(): pl.pallas_call(functools.partial(finish_kernel, len(bases)), grid=(column...  18.5 us
    pallas_call x2, Pallas kernels, pack(): pl.pallas_call(functools.partial(pack_kernel, first), grid=(width // tile...  17 us
    pallas_call x2, Pallas kernels, down(): pl.pallas_call(functools.partial(down_kernel, shape_of(groups), len(xs)),...  13 us
    pallas_call x2, Pallas kernels, lift(): pl.pallas_call(functools.partial(lift_kernel, shape_of(groups), len(ys)),...  9.91 us
    unnamed x36, local copies, waits for them, and re-layouts  7.63 us
  transfers between devices with their start and end apart: 26, of which 7 were waited for; matrix products, arithmetic and copies ran while one was open for 3% of the time, Pallas kernels for 43%

profile of v3, /device:TPU:0, one launch (start us, length us, event | category | flops | bytes accessed | tf_op | source)
XLA Modules:
  0.0 239.4 jit_solution(10417664193618185399)
XLA Ops:
  0.0 0.8 collective-permute-start.1
  0.8 5.8 %collective-permute-start = (bf16[4,64,4096]{2,1,0:T(8,128)(2,1)}, bf16[4,64,4096]{2,1,0:T(8,128)(2,1)}, u32[]{:S(2)}, u32[]{:S(2)}) collective-permute-start(bf16[4,64,4096]{2,1,0:T(8,128)(2,1)} %bitcast.7), channel_id=1, source_target_pairs={{0,8},{2,10},{4,12},{6,14},{8,0},{10,2},{12,4},{14,6},{16,24},{18,... | collective-permute-start | bytes 6291464 | tf_op jit(solution)/shard_map/ppermute | solution.py:266
  6.6 0.8 select_reduce_fusion
  8.0 0.7 fusion.14.target_ref
  8.7 7.5 %pack_rows.2 = (bf16[96,4096]{1,0:T(8,128)(2,1)}, bf16[96,4096]{1,0:T(8,128)(2,1)}, bf16[96,4096]{1,0:T(8,128)(2,1)}, bf16[96,4096]{1,0:T(8,128)(2,1)}) custom-call(s32[1,1024]{1,0:T(1,128)} %fusion.14.target_ref, bf16[1024,4096]{1,0:T(8,128)(2,1)} %x_ref.4), custom_call_target="tpu_custom_call" | custom-call | flops 3221225472 | bytes 11534336 | tf_op jit(solution)/shard_map/pack_rows/pallas_call | solution.py:43
  16.2 1.5 collective-permute-start.2
  17.7 1.5 collective-permute-start.3
  20.1 1.0 slice.16.onehot_ref
  21.1 1.2 slice.17.onehot_ref
  22.3 9.5 %pack_rows.3 = (bf16[160,4096]{1,0:T(8,128)(2,1)}, bf16[160,4096]{1,0:T(8,128)(2,1)}, bf16[160,4096]{1,0:T(8,128)(2,1)}, bf16[160,4096]{1,0:T(8,128)(2,1)}) custom-call(s32[1,1024]{1,0:T(1,128)} %fusion.14.target_ref, bf16[1024,4096]{1,0:T(8,128)(2,1)} %x_ref.4), custom_call_target="tpu_custom_call" | custom-call | flops 5368709120 | bytes 13631488 | tf_op jit(solution)/shard_map/pack_rows/pallas_call | solution.py:43
  31.8 23.7 %project_half.3 = bf16[1024,2048]{1,0:T(8,128)(2,1)} custom-call(s32[1]{0:T(128)} %bitcast.5.place_ref, bf16[1024,4096]{1,0:T(8,128)(2,1)} %x_ref.4, bf16[4096,4096]{1,0:T(8,128)(2,1)} %w_ref.3), custom_call_target="tpu_custom_call" | custom-call | flops 17179869184 | bytes 29360128 | tf_op jit(solution)/shard_map/project_half/pallas_call | solution.py:65
  55.5 1.6 collective-permute-start.10
  57.1 1.5 collective-permute-start.11
  58.6 4.4 %join_rows.1 = bf16[384,4096]{1,0:T(8,128)(2,1)} custom-call(bf16[96,4096]{1,0:T(8,128)(2,1)} %get-tuple-element.59.refs_0_, bf16[96,4096]{1,0:T(8,128)(2,1)} %copy-done.3, bf16[96,4096]{1,0:T(8,128)(2,1)} %collective-permute-done.3.refs_2_, bf16[96,4096]{1,0:T(8,128)(2,1)} %collective-permute-done.4.refs_3_), custom_call_target="tpu_custom_call" | custom-call | bytes 6291456 | tf_op jit(solution)/shard_map/join_rows/pallas_call | solution.py:224
  63.1 1.6 collective-permute-start.6
  64.8 23.7 %project_half.2.rest_0_ = bf16[1024,2048]{1,0:T(8,128)(2,1)} custom-call(s32[1]{0:T(128)} %bitcast.1.place_ref, bf16[1024,4096]{1,0:T(8,128)(2,1)} %x_ref.4, bf16[4096,4096]{1,0:T(8,128)(2,1)} %w_ref.3), custom_call_target="tpu_custom_call" | custom-call | flops 17179869184 | bytes 29360128 | tf_op jit(solution)/shard_map/project_half/pallas_call | solution.py:65
  89.2 1.3 collective-permute-start.8
  90.5 1.7 collective-permute-start.7
  92.1 7.7 %collective-permute-start.15 = (bf16[384,4096]{1,0:T(8,128)(2,1)}, bf16[384,4096]{1,0:T(8,128)(2,1)S(1)}, u32[]{:S(2)}, u32[]{:S(2)}) collective-permute-start(bf16[384,4096]{1,0:T(8,128)(2,1)} %join_rows.1), channel_id=1, source_target_pairs={{0,8},{2,10},{4,12},{6,14},{24,16},{26,18},{28,20},{30,22},{1,9},{... | collective-permute-start | bytes 9437192 | tf_op jit(solution)/shard_map/ppermute | solution.py:266
  99.8 18.3 %collective-permute-done.12.refs_3_ = bf16[160,4096]{1,0:T(8,128)(2,1)} collective-permute-done((bf16[160,4096]{1,0:T(8,128)(2,1)S(1)}, bf16[160,4096]{1,0:T(8,128)(2,1)}, u32[]{:S(2)}, u32[]{:S(2)}) %collective-permute-start.12) | collective-permute-done | bytes 1310752 | tf_op jit(solution)/shard_map/ppermute | solution.py:266
  118.1 1.3 collective-permute-start.9
  119.4 2.0 collective-permute-start.16
  121.5 6.6 %down_rows.2.refs_0_ = f32[640,256]{1,0:T(8,128)} custom-call(bf16[160,4096]{1,0:T(8,128)(2,1)} %get-tuple-element.44.refs_0_, bf16[160,4096]{1,0:T(8,128)(2,1)} %copy-done.5, bf16[160,4096]{1,0:T(8,128)(2,1)} %copy-done.6, bf16[160,4096]{1,0:T(8,128)(2,1)} %collective-permute-done.12.refs_3_, bf16[4,64,4096]{2,1,0:T(8,128)(2,1)} %bitcast.8, ...), custom_call_target="tpu_custom_call" | custom-call | flops 1342177280 | bytes 10485760 | tf_op jit(solution)/shard_map/down_rows/pallas_call | solution.py:140
  128.0 17.9 %collective-permute-done.9.refs_5_.refs_3_ = bf16[4,64,2048]{2,1,0:T(8,128)(2,1)} collective-permute-done((bf16[4,64,2048]{2,1,0:T(8,128)(2,1)}, bf16[4,64,2048]{2,1,0:T(8,128)(2,1)}, u32[]{:S(2)}, u32[]{:S(2)}) %collective-permute-start.9) | collective-permute-done | bytes 1048608 | tf_op jit(solution)/shard_map/ppermute | solution.py:266
  145.9 1.3 collective-permute-start.13
  147.3 2.3 collective-permute-done.14.refs_1_
  149.6 0.8 copy-done.11
  150.4 5.4 %lift_rows.2 = (bf16[160,2048]{1,0:T(8,128)(2,1)}, bf16[160,2048]{1,0:T(8,128)(2,1)}, bf16[160,2048]{1,0:T(8,128)(2,1)}, bf16[160,2048]{1,0:T(8,128)(2,1)}) custom-call(f32[640,256]{1,0:T(8,128)} %down_rows.2.refs_0_, f32[640,256]{1,0:T(8,128)} %copy-done.11, bf16[4,64,2048]{2,1,0:T(8,128)(2,1)} %refs_2_.1, ...), custom_call_target="tpu_custom_call" | custom-call | flops 671088640 | bytes 5242880 | tf_op jit(solution)/shard_map/lift_rows/pallas_call | solution.py:174
  155.8 17.1 %collective-permute-done.13.refs_5_ = bf16[4,64,2048]{2,1,0:T(8,128)(2,1)} collective-permute-done((bf16[4,64,2048]{2,1,0:T(8,128)(2,1)}, bf16[4,64,2048]{2,1,0:T(8,128)(2,1)}, u32[]{:S(2)}, u32[]{:S(2)}) %collective-permute-start.13) | collective-permute-done | bytes 1048608 | tf_op jit(solution)/shard_map/ppermute | solution.py:266
  172.9 1.6 copy-done
  174.5 6.4 %down_rows.3 = f32[768,256]{1,0:T(8,128)} custom-call(bf16[96,4096]{1,0:T(8,128)(2,1)} %get-tuple-element.59.refs_0_, bf16[96,4096]{1,0:T(8,128)(2,1)} %copy-done.3, bf16[96,4096]{1,0:T(8,128)(2,1)} %collective-permute-done.3.refs_2_, bf16[96,4096]{1,0:T(8,128)(2,1)} %collective-permute-done.4.refs_3_, bf16[384,4096]{1,0:T(8,128)(2,1)} %copy-done, ...), custom_call_target="tpu_custom_call" | custom-call | flops 1610612736 | bytes 9437184 | tf_op jit(solution)/shard_map/down_rows/pallas_call | solution.py:140
  181.6 0.8 collective-permute-start.21
  182.4 2.1 collective-permute-start.22
  184.6 1.2 add_convert_fusion.refs_0_
  185.8 1.3 collective-permute-start.18
  187.1 7.0 %collective-permute-done.18.refs_1_ = bf16[384,256]{1,0:T(8,128)(2,1)S(1)} collective-permute-done((bf16[384,256]{1,0:T(8,128)(2,1)S(1)}, bf16[384,256]{1,0:T(8,128)(2,1)S(1)}, u32[]{:S(2)}, u32[]{:S(2)}) %collective-permute-start.18) | collective-permute-done | bytes 196640 | tf_op jit(solution)/shard_map/ppermute | solution.py:266
  194.1 0.7 copy-done.15
  194.8 4.5 %lift_rows.3 = (bf16[96,2048]{1,0:T(8,128)(2,1)}, bf16[96,2048]{1,0:T(8,128)(2,1)}, bf16[96,2048]{1,0:T(8,128)(2,1)}, bf16[96,2048]{1,0:T(8,128)(2,1)}) custom-call(bf16[768,256]{1,0:T(8,128)(2,1)} %copy-done.4, bf16[384,256]{1,0:T(8,128)(2,1)} %copy-done.15, bf16[4,64,2048]{2,1,0:T(8,128)(2,1)} %collective-permute-done.6.refs_4_.refs_2_, ...), custom_call_target="tpu_custom_call" | custom-call | flops 402653184 | bytes 3145728 | tf_op jit(solution)/shard_map/lift_rows/pallas_call | solution.py:174
  199.9 0.8 collective-permute-start.24
  200.7 12.0 %collective-permute-done.21.rest_4_ = bf16[160,2048]{1,0:T(8,128)(2,1)S(1)} collective-permute-done((bf16[160,2048]{1,0:T(8,128)(2,1)}, bf16[160,2048]{1,0:T(8,128)(2,1)S(1)}, u32[]{:S(2)}, u32[]{:S(2)}) %collective-permute-start.21) | collective-permute-done | bytes 655392 | tf_op jit(solution)/shard_map/ppermute | solution.py:266
  212.7 1.3 collective-permute-start.25
  214.0 0.8 copy-done.10
  214.9 2.0 copy-done.2
  216.9 10.2 %finish_rows.2.rest_0_ = f32[1024,2048]{1,0:T(8,128)} custom-call(bf16[1024,640]{1,0:T(8,128)(2,1)} %slice.17.onehot_ref, bf16[1024,2048]{1,0:T(8,128)(2,1)} %project_half.2.rest_0_, bf16[1024,2048]{1,0:T(8,128)(2,1)} %copy-done.2, bf16[160,2048]{1,0:T(8,128)(2,1)} %get-tuple-element.58.rest_2_, bf16[160,2048]{1,0:T(8,128)(2,1)} %copy-done.8, ...), custom_call_target="tpu_custom_call" | custom-call | flops 2684354560 | bytes 16777216 | tf_op jit(solution)/shard_map/finish_rows/pallas_call | solution.py:200
  227.1 2.4 %collective-permute-done.24.rest_3_ = bf16[96,2048]{1,0:T(8,128)(2,1)S(1)} collective-permute-done((bf16[96,2048]{1,0:T(8,128)(2,1)}, bf16[96,2048]{1,0:T(8,128)(2,1)S(1)}, u32[]{:S(2)}, u32[]{:S(2)}) %collective-permute-start.24) | collective-permute-done | bytes 393248 | tf_op jit(solution)/shard_map/ppermute | solution.py:266
  229.5 0.8 copy-done.13
  230.3 0.8 copy-done.14
  231.1 8.3 %finish_rows.3 = bf16[1024,2048]{1,0:T(8,128)(2,1)} custom-call(bf16[1024,384]{1,0:T(8,128)(2,1)} %slice.16.onehot_ref, f32[1024,2048]{1,0:T(8,128)} %finish_rows.2.rest_0_, bf16[96,2048]{1,0:T(8,128)(2,1)} %get-tuple-element.62.rest_1_, bf16[96,2048]{1,0:T(8,128)(2,1)} %copy-done.12, bf16[96,2048]{1,0:T(8,128)(2,1)} %copy-done.13, bf16[96,2048]{1,0:T(8,128)(2,1)} %copy-done.14), custom_call_target="tpu_custom_call" | custom-call | flops 1610612736 | bytes 16777216 | tf_op jit(solution)/shard_map/finish_rows/pallas_call | solution.py:200
  (62 shorter events, 3.6 us)
Async XLA Ops:
  0.0 63.0 %collective-permute-start.1 = (bf16[4,64,4096]{2,1,0:T(8,128)(2,1)}, bf16[4,64,4096]{2,1,0:T(8,128)(2,1)S(1)}, u32[]{:S(2)}, u32[]{:S(2)}) collective-permute-start(bf16[4,64,4096]{2,1,0:T(8,128)(2,1)} %bitcast.6), channel_id=1, source_target_pairs={{8,16},{10,18},{12,20},{14,22},{16,8},{18,10},{20,12},{22,14},{9,1... | collective-permute-start | bytes 6291464 | tf_op jit(solution)/shard_map/ppermute | solution.py:266
  0.8 62.2 %collective-permute-start = (bf16[4,64,4096]{2,1,0:T(8,128)(2,1)}, bf16[4,64,4096]{2,1,0:T(8,128)(2,1)}, u32[]{:S(2)}, u32[]{:S(2)}) collective-permute-start(bf16[4,64,4096]{2,1,0:T(8,128)(2,1)} %bitcast.7), channel_id=1, source_target_pairs={{0,8},{2,10},{4,12},{6,14},{8,0},{10,2},{12,4},{14,6},{16,24},{18,... | collective-permute-start | bytes 6291464 | tf_op jit(solution)/shard_map/ppermute | solution.py:266
  16.2 39.3 %collective-permute-start.2 = (bf16[96,4096]{1,0:T(8,128)(2,1)}, bf16[96,4096]{1,0:T(8,128)(2,1)S(1)}, u32[]{:S(2)}, u32[]{:S(2)}) collective-permute-start(bf16[96,4096]{1,0:T(8,128)(2,1)} %get-tuple-element.39), channel_id=1, source_target_pairs={{0,2},{2,0},{4,6},{6,4},{8,10},{10,8},{12,14},{14,12},{16,18},{18,... | collective-permute-start | bytes 2359304 | tf_op jit(solution)/shard_map/ppermute | solution.py:266
  17.7 37.8 %collective-permute-start.3 = (bf16[96,4096]{1,0:T(8,128)(2,1)}, bf16[96,4096]{1,0:T(8,128)(2,1)}, u32[]{:S(2)}, u32[]{:S(2)}) collective-permute-start(bf16[96,4096]{1,0:T(8,128)(2,1)} %get-tuple-element.40), channel_id=1, source_target_pairs={{0,4},{2,6},{4,0},{6,2},{8,12},{10,14},{12,8},{14,10},{16,20},{18,... | collective-permute-start | bytes 2359304 | tf_op jit(solution)/shard_map/ppermute | solution.py:266
  19.2 39.4 %collective-permute-start.4 = (bf16[96,4096]{1,0:T(8,128)(2,1)}, bf16[96,4096]{1,0:T(8,128)(2,1)}, u32[]{:S(2)}, u32[]{:S(2)}) collective-permute-start(bf16[96,4096]{1,0:T(8,128)(2,1)} %get-tuple-element.41), channel_id=1, source_target_pairs={{0,6},{2,4},{4,2},{6,0},{8,14},{10,12},{12,10},{14,8},{16,22},{18,... | collective-permute-start | bytes 2359304 | tf_op jit(solution)/shard_map/ppermute | solution.py:266
  55.5 3.1 %copy-start.3 = (bf16[96,4096]{1,0:T(8,128)(2,1)}, bf16[96,4096]{1,0:T(8,128)(2,1)S(1)}, u32[]{:S(2)}) copy-start(bf16[96,4096]{1,0:T(8,128)(2,1)S(1)} %collective-permute-done.2.refs_1_) | copy-start | bytes 2359300
  55.5 7.5 %copy-start.7 = (bf16[4,64,2048]{2,1,0:T(8,128)(2,1)S(1)}, bf16[4,64,2048]{2,1,0:T(8,128)(2,1)}, u32[]{:S(2)}) copy-start(bf16[4,64,2048]{2,1,0:T(8,128)(2,1)} %refs_2_.1) | copy-start | bytes 3145732
  55.5 32.9 %collective-permute-start.10 = (bf16[160,4096]{1,0:T(8,128)(2,1)}, bf16[160,4096]{1,0:T(8,128)(2,1)S(1)}, u32[]{:S(2)}, u32[]{:S(2)}) collective-permute-start(bf16[160,4096]{1,0:T(8,128)(2,1)} %get-tuple-element.52), channel_id=1, source_target_pairs={{0,2},{2,0},{4,6},{6,4},{8,10},{10,8},{12,14},{14,12},{16,18},{18,... | collective-permute-start | bytes 3932168 | tf_op jit(solution)/shard_map/ppermute | solution.py:266
  57.1 31.4 %collective-permute-start.11 = (bf16[160,4096]{1,0:T(8,128)(2,1)}, bf16[160,4096]{1,0:T(8,128)(2,1)S(1)}, u32[]{:S(2)}, u32[]{:S(2)}) collective-permute-start(bf16[160,4096]{1,0:T(8,128)(2,1)} %get-tuple-element.54), channel_id=1, source_target_pairs={{0,4},{2,6},{4,0},{6,2},{8,12},{10,14},{12,8},{14,10},{16,20},{18,... | collective-permute-start | bytes 3932168 | tf_op jit(solution)/shard_map/ppermute | solution.py:266
  63.0 26.1 %copy-start.1 = (bf16[4,64,4096]{2,1,0:T(8,128)(2,1)}, bf16[4,64,4096]{2,1,0:T(8,128)(2,1)S(1)}, u32[]{:S(2)}) copy-start(bf16[4,64,4096]{2,1,0:T(8,128)(2,1)S(1)} %collective-permute-done.1.refs_6_.refs_8_) | copy-start | bytes 6291460
  63.0 26.1 %collective-permute-start.5 = (bf16[4,64,2048]{2,1,0:T(8,128)(2,1)S(1)}, bf16[4,64,2048]{2,1,0:T(8,128)(2,1)}, u32[]{:S(2)}, u32[]{:S(2)}) collective-permute-start(bf16[4,64,2048]{2,1,0:T(8,128)(2,1)S(1)} %copy-done.7), channel_id=1, source_target_pairs={{0,8},{2,10},{4,12},{6,14},{8,0},{10,2},{12,4},{14,6},{16,24},{18,... | collective-permute-start | bytes 3145736 | tf_op jit(solution)/shard_map/ppermute | solution.py:266
  63.1 27.3 %collective-permute-start.6 = (bf16[4,64,2048]{2,1,0:T(8,128)(2,1)S(1)}, bf16[4,64,2048]{2,1,0:T(8,128)(2,1)}, u32[]{:S(2)}, u32[]{:S(2)}) collective-permute-start(bf16[4,64,2048]{2,1,0:T(8,128)(2,1)S(1)} %copy-done.7), channel_id=1, source_target_pairs={{8,16},{10,18},{12,20},{14,22},{16,8},{18,10},{20,12},{22,14},{9,1... | collective-permute-start | bytes 3145736 | tf_op jit(solution)/shard_map/ppermute | solution.py:266
  64.8 23.7 %copy-start.16 = (bf16[160,4096]{1,0:T(8,128)(2,1)S(1)}, bf16[160,4096]{1,0:T(8,128)(2,1)}, u32[]{:S(2)}) copy-start(bf16[160,4096]{1,0:T(8,128)(2,1)} %get-tuple-element.56) | copy-start | bytes 3932164
  88.5 2.0 copy-start.5
  88.5 2.0 copy-start.6
  88.5 29.6 %collective-permute-start.12 = (bf16[160,4096]{1,0:T(8,128)(2,1)S(1)}, bf16[160,4096]{1,0:T(8,128)(2,1)}, u32[]{:S(2)}, u32[]{:S(2)}) collective-permute-start(bf16[160,4096]{1,0:T(8,128)(2,1)S(1)} %copy-done.16), channel_id=1, source_target_pairs={{0,6},{2,4},{4,2},{6,0},{8,14},{10,12},{12,10},{14,8},{16,22},{18,... | collective-permute-start | bytes 3932168 | tf_op jit(solution)/shard_map/ppermute | solution.py:266
  89.2 29.0 %collective-permute-start.8 = (bf16[2,64,4096]{2,1,0:T(8,128)(2,1)S(1)}, bf16[2,64,4096]{2,1,0:T(8,128)(2,1)}, u32[]{:S(2)}, u32[]{:S(2)}) collective-permute-start(bf16[2,64,4096]{2,1,0:T(8,128)(2,1)S(1)} %slice.18), channel_id=1, source_target_pairs={{8,0},{10,2},{12,4},{14,6},{16,24},{18,26},{20,28},{22,30},{9,1},{... | collective-permute-start | bytes 3145736 | tf_op jit(solution)/shard_map/ppermute | solution.py:266
  90.5 28.9 %collective-permute-start.7 = (bf16[4,64,2048]{2,1,0:T(8,128)(2,1)}, bf16[4,64,2048]{2,1,0:T(8,128)(2,1)}, u32[]{:S(2)}, u32[]{:S(2)}) collective-permute-start(bf16[4,64,2048]{2,1,0:T(8,128)(2,1)} %collective-permute-done.5.refs_3_), channel_id=1, source_target_pairs={{8,16},{10,18},{12,20},{14,22},{16,8},{18,10},{20,12},{22,14},{9,1... | collective-permute-start | bytes 3145736 | tf_op jit(solution)/shard_map/ppermute | solution.py:266
  92.1 80.8 %collective-permute-start.15 = (bf16[384,4096]{1,0:T(8,128)(2,1)}, bf16[384,4096]{1,0:T(8,128)(2,1)S(1)}, u32[]{:S(2)}, u32[]{:S(2)}) collective-permute-start(bf16[384,4096]{1,0:T(8,128)(2,1)} %join_rows.1), channel_id=1, source_target_pairs={{0,8},{2,10},{4,12},{6,14},{24,16},{26,18},{28,20},{30,22},{1,9},{... | collective-permute-start | bytes 9437192 | tf_op jit(solution)/shard_map/ppermute | solution.py:266
  118.1 95.9 %collective-permute-start.19 = (bf16[1024,2048]{1,0:T(8,128)(2,1)}, bf16[1024,2048]{1,0:T(8,128)(2,1)S(1)}, u32[]{:S(2)}, u32[]{:S(2)}) collective-permute-start(bf16[1024,2048]{1,0:T(8,128)(2,1)} %project_half.3), channel_id=1, source_target_pairs={{0,1},{1,0},{2,3},{3,2},{4,5},{5,4},{6,7},{7,6},{8,9},{9,8},{10,11... | collective-permute-start | bytes 12582920 | tf_op jit(solution)/shard_map/ppermute | solution.py:312
  118.1 27.8 %collective-permute-start.9 = (bf16[4,64,2048]{2,1,0:T(8,128)(2,1)}, bf16[4,64,2048]{2,1,0:T(8,128)(2,1)}, u32[]{:S(2)}, u32[]{:S(2)}) collective-permute-start(bf16[4,64,2048]{2,1,0:T(8,128)(2,1)} %collective-permute-done.6.refs_4_.refs_2_), channel_id=1, source_target_pairs={{8,0},{10,2},{12,4},{14,6},{16,24},{18,26},{20,28},{22,30},{9,1},{... | collective-permute-start | bytes 3145736 | tf_op jit(solution)/shard_map/ppermute | solution.py:266
  119.4 53.5 %collective-permute-start.16 = (bf16[4,64,4096]{2,1,0:T(8,128)(2,1)}, bf16[4,64,4096]{2,1,0:T(8,128)(2,1)}, u32[]{:S(2)}, u32[]{:S(2)}) collective-permute-start(bf16[4,64,4096]{2,1,0:T(8,128)(2,1)} %collective-permute-done.refs_5_), channel_id=1, source_target_pairs={{8,16},{10,18},{12,20},{14,22},{16,8},{18,10},{20,12},{22,14},{9,1... | collective-permute-start | bytes 6291464 | tf_op jit(solution)/shard_map/ppermute | solution.py:266
  145.9 27.0 %collective-permute-start.13 = (bf16[4,64,2048]{2,1,0:T(8,128)(2,1)}, bf16[4,64,2048]{2,1,0:T(8,128)(2,1)}, u32[]{:S(2)}, u32[]{:S(2)}) collective-permute-start(bf16[4,64,2048]{2,1,0:T(8,128)(2,1)} %collective-permute-done.7.refs_4_), channel_id=1, source_target_pairs={{8,0},{10,2},{12,4},{14,6},{16,24},{18,26},{20,28},{22,30},{9,1},{... | collective-permute-start | bytes 3145736 | tf_op jit(solution)/shard_map/ppermute | solution.py:266
  147.2 2.4 collective-permute-start.14
  149.6 0.8 copy-start.11
  172.9 9.6 %copy-start.17 = (bf16[160,2048]{1,0:T(8,128)(2,1)S(1)}, bf16[160,2048]{1,0:T(8,128)(2,1)}, u32[]{:S(2)}) copy-start(bf16[160,2048]{1,0:T(8,128)(2,1)} %get-tuple-element.67) | copy-start | bytes 1966084
  172.9 1.7 copy-start
  181.0 3.6 %collective-permute-start.17 = (f32[768,256]{1,0:T(8,128)}, f32[768,256]{1,0:T(8,128)S(1)}, u32[]{:S(2)}, u32[]{:S(2)}) collective-permute-start(f32[768,256]{1,0:T(8,128)} %down_rows.3), channel_id=1, source_target_pairs={{0,1},{1,0},{2,3},{3,2},{4,5},{5,4},{6,7},{7,6},{8,9},{9,8},{10,11... | collective-permute-start | bytes 2359304 | tf_op jit(solution)/shard_map/ppermute | solution.py:315
  181.0 18.9 %collective-permute-start.20 = (bf16[160,2048]{1,0:T(8,128)(2,1)}, bf16[160,2048]{1,0:T(8,128)(2,1)S(1)}, u32[]{:S(2)}, u32[]{:S(2)}) collective-permute-start(bf16[160,2048]{1,0:T(8,128)(2,1)} %get-tuple-element.65), channel_id=1, source_target_pairs={{0,2},{2,0},{4,6},{6,4},{8,10},{10,8},{12,14},{14,12},{16,18},{18,... | collective-permute-start | bytes 1966088 | tf_op jit(solution)/shard_map/ppermute | solution.py:266
  181.6 31.1 %collective-permute-start.21 = (bf16[160,2048]{1,0:T(8,128)(2,1)}, bf16[160,2048]{1,0:T(8,128)(2,1)S(1)}, u32[]{:S(2)}, u32[]{:S(2)}) collective-permute-start(bf16[160,2048]{1,0:T(8,128)(2,1)} %get-tuple-element.66), channel_id=1, source_target_pairs={{0,4},{2,6},{4,0},{6,2},{8,12},{10,14},{12,8},{14,10},{16,20},{18,... | collective-permute-start | bytes 1966088 | tf_op jit(solution)/shard_map/ppermute | solution.py:266
  182.4 31.6 %collective-permute-start.22 = (bf16[160,2048]{1,0:T(8,128)(2,1)S(1)}, bf16[160,2048]{1,0:T(8,128)(2,1)S(1)}, u32[]{:S(2)}, u32[]{:S(2)}) collective-permute-start(bf16[160,2048]{1,0:T(8,128)(2,1)S(1)} %copy-done.17), channel_id=1, source_target_pairs={{0,6},{2,4},{4,2},{6,0},{8,14},{10,12},{12,10},{14,8},{16,22},{18,... | collective-permute-start | bytes 1966088 | tf_op jit(solution)/shard_map/ppermute | solution.py:266
  185.8 8.3 %copy-start.4 = (bf16[768,256]{1,0:T(8,128)(2,1)}, bf16[768,256]{1,0:T(8,128)(2,1)S(1)}, u32[]{:S(2)}) copy-start(bf16[768,256]{1,0:T(8,128)(2,1)S(1)} %add_convert_fusion.refs_0_) | copy-start | bytes 1179652
  185.8 8.3 %collective-permute-start.18 = (bf16[384,256]{1,0:T(8,128)(2,1)S(1)}, bf16[384,256]{1,0:T(8,128)(2,1)S(1)}, u32[]{:S(2)}, u32[]{:S(2)}) collective-permute-start(bf16[384,256]{1,0:T(8,128)(2,1)S(1)} %slice.19), channel_id=1, source_target_pairs={{8,0},{10,2},{12,4},{14,6},{16,24},{18,26},{20,28},{22,30},{9,1},{... | collective-permute-start | bytes 589832 | tf_op jit(solution)/shard_map/ppermute | solution.py:266
  194.1 0.7 copy-start.15
  199.3 27.8 %collective-permute-start.23 = (bf16[96,2048]{1,0:T(8,128)(2,1)}, bf16[96,2048]{1,0:T(8,128)(2,1)S(1)}, u32[]{:S(2)}, u32[]{:S(2)}) collective-permute-start(bf16[96,2048]{1,0:T(8,128)(2,1)} %get-tuple-element.68), channel_id=1, source_target_pairs={{0,2},{2,0},{4,6},{6,4},{8,10},{10,8},{12,14},{14,12},{16,18},{18,... | collective-permute-start | bytes 1179656 | tf_op jit(solution)/shard_map/ppermute | solution.py:266
  199.9 14.1 %copy-start.8 = (bf16[160,2048]{1,0:T(8,128)(2,1)}, bf16[160,2048]{1,0:T(8,128)(2,1)S(1)}, u32[]{:S(2)}) copy-start(bf16[160,2048]{1,0:T(8,128)(2,1)S(1)} %collective-permute-done.20.rest_3_) | copy-start | bytes 1966084
  199.9 29.6 %collective-permute-start.24 = (bf16[96,2048]{1,0:T(8,128)(2,1)}, bf16[96,2048]{1,0:T(8,128)(2,1)S(1)}, u32[]{:S(2)}, u32[]{:S(2)}) collective-permute-start(bf16[96,2048]{1,0:T(8,128)(2,1)} %get-tuple-element.69), channel_id=1, source_target_pairs={{0,4},{2,6},{4,0},{6,2},{8,12},{10,14},{12,8},{14,10},{16,20},{18,... | collective-permute-start | bytes 1179656 | tf_op jit(solution)/shard_map/ppermute | solution.py:266
  212.7 1.3 copy-start.9
  212.7 16.8 %collective-permute-start.25 = (bf16[96,2048]{1,0:T(8,128)(2,1)}, bf16[96,2048]{1,0:T(8,128)(2,1)S(1)}, u32[]{:S(2)}, u32[]{:S(2)}) collective-permute-start(bf16[96,2048]{1,0:T(8,128)(2,1)} %get-tuple-element.70), channel_id=1, source_target_pairs={{0,6},{2,4},{4,2},{6,0},{8,14},{10,12},{12,10},{14,8},{16,22},{18,... | collective-permute-start | bytes 1179656 | tf_op jit(solution)/shard_map/ppermute | solution.py:266
  214.0 0.8 copy-start.10
  214.9 2.0 copy-start.2
  227.1 2.4 %copy-start.12 = (bf16[96,2048]{1,0:T(8,128)(2,1)}, bf16[96,2048]{1,0:T(8,128)(2,1)S(1)}, u32[]{:S(2)}) copy-start(bf16[96,2048]{1,0:T(8,128)(2,1)S(1)} %collective-permute-done.23.rest_2_) | copy-start | bytes 1179652
  229.5 0.8 copy-start.13
  230.3 0.8 copy-start.14

commit v4 on v3

--- a/solution.py
+++ b/solution.py
@@ -247,6 +247,9 @@
     return slots, position
 
 
+EARLIER = {"home": ["away"], "given": ["home", "onehots"], "up_pair": ["down_pair", "given"], "up_near": ["down_near", "given"], "home1": ["away1", "given"], "home2": ["away2", "given"], "base_own": ["down_pair", "down_near", "joined"], "moved": ["up_pair", "home1", "home2", "base_own"], "down_out": ["up_pair", "base_own"], "up_far": ["up_near", "base_own"], "home3": ["home1", "home2", "base_own"], "down_far": ["up_far", "down_out"], "up_near_out": ["down_out"], "base_other": ["low_away"], "up_far_out": ["up_near_out", "low_home"], "low_away": ["up_far_out", "lift_home1", "lift_home2"], "part": ["rows_away"], "lift_home3": ["lift_home1"]}
+
+
 def after(x, *earlier):
     return lax.optimization_barrier((x, *earlier))[0]
 
@@ -261,10 +264,6 @@
     every = range(COLUMNS * PLANES)
     inside = [r for r in every if r // COLUMNS in (1, 2)]
     outside = [r for r in every if r // COLUMNS in (0, 3)]
-
-    def send(x, pairs, *earlier):
-        return lax.ppermute(after(x, *earlier) if earlier else x, "rep", pairs)
-
     pair = [(r, r ^ 4) for r in every]
     across = [(r, r ^ 12) for r in inside]
     outward = [(r, r ^ 4) for r in inside]
@@ -281,61 +280,106 @@
     there = (turned * rest + number - served) * MOST
     here = (COLUMNS * rest + turned * served + number) * MOST
     target = jnp.where(number < served, here, there) + position
+    split = COLUMNS * rest * MOST
+    spots = lax.broadcasted_iota(jnp.int32, (target.shape[0], 4 * owned * COLUMNS * MOST), 1)
+    onehot = (target[:, None] == spots).astype(jnp.bfloat16)
+    back_away, back_home = onehot[:, :split], onehot[:, split:]
 
     down_own = jnp.swapaxes(slot_down_weight, 1, 2)
     up_own = slot_up_weight
     tp = lax.axis_index("tp")
-    down_pair = send(down_own, pair)
-    down_near = send(down_own, across)
-
-    split = COLUMNS * rest * MOST
-    away = pack(target[None, :], hidden_input, 0, rest * MOST, COLUMNS)
-    home = pack(target[None, :], after(hidden_input, away[0]), split, served * MOST, COLUMNS)
-    spots = lax.broadcasted_iota(jnp.int32, (target.shape[0], 4 * owned * COLUMNS * MOST), 1)
-    onehot = (target[:, None] == spots).astype(jnp.bfloat16)
-    back_away, back_home = onehot[:, :split], onehot[:, split:]
-    away = [away[0]] + [send(away[d], turn[d]) for d in range(1, COLUMNS)]
-    given = project(1 - tp, after(hidden_input, home[0], back_away, back_home), query_weight)
-
-    up_pair = send(up_own, pair, down_pair, given)
-    up_near = send(up_own, across, down_near, given)
-    beside = [home[0]] + [send(home[d], turn[d], away[d], given) for d in (1, 2)]
-    moving = join(away)
-    base_own = project(tp, after(hidden_input, down_pair, down_near, moving), query_weight)
-
-    moved = send(moving, inward, up_pair, beside[1], beside[2], base_own)
-    down_out = send(down_near[:cut], outward, up_pair, base_own)
-    up_far = send(up_pair, across, up_near, base_own)
-    beside.append(send(home[3], turn[3], beside[1], beside[2], base_own))
-    down_far = send(down_pair, across, up_far, down_out)
-    up_near_out = send(up_near, outward, down_out)
-    base_other = lax.ppermute(after(given, beside[3]), "tp", SWAP)
-
-    def swapped(y):
-        return lax.ppermute(y, "tp", SWAP)
-
-    low = down(
-        [(rows, 0) for rows in beside],
-        [([down_own], 0, owned), ([down_pair], 0, owned), ([down_near, down_out], 0, cut)],
-    )
-    up_far_out = send(up_far, outward, up_near_out, low)
-    rows = lift(
-        [low, swapped(low)], [([up_own], 0, owned), ([up_pair], 0, owned), ([up_near, up_near_out], 0, cut)]
-    )
-    lifted_home = [rows[0]] + [send(rows[d], turn[d]) for d in range(1, COLUMNS)]
-
-    low = down(
-        [(after(away[0], up_far_out, rows[0]), 0)] + [(rows, 0) for rows in away[1:]] + [(moved, d) for d in range(COLUMNS)],
-        [([down_near], cut, owned - cut), ([down_far], 0, owned)],
-    )
-    low = (low + swapped(low)).astype(jnp.bfloat16)
-    rows = lift(
-        [low, send(low[low.shape[0] // 2 :], outward)],
-        [([up_near, up_near_out], cut, owned - cut), ([up_far, up_far_out], 0, owned)],
-    )
-    lifted_away = [rows[0]] + [send(rows[d], turn[d]) for d in range(1, COLUMNS)]
-    part = finish(back_home, [after(base_own, rows[0]), base_other], lifted_home, jnp.float32)
-    return finish(back_away, [part], lifted_away, jnp.bfloat16)
+    made = {}
+
+    def need(name):
+        if name not in made:
+            made[name] = steps[name](name)
+        return made[name]
+
+    def gate(name, x):
+        earlier = [need(one) for one in EARLIER.get(name, ())]
+        return after(x, *earlier) if earlier else x
+
+    def send(pairs, what):
+        return lambda name: lax.ppermute(gate(name, what()), "rep", pairs)
+
+    def swap(what):
+        return lambda name: lax.ppermute(gate(name, what()), "tp", SWAP)
+
+    def packed(first, count):
+        return lambda name: pack(target[None, :], gate(name, hidden_input), first, count * MOST, COLUMNS)
+
+    def rows_away():
+        return [need("away")[0]] + [need(f"away{d}") for d in (1, 2, 3)]
+
+    def rows_home():
+        return [need("home")[0]] + [need(f"home{d}") for d in (1, 2, 3)]
+
+    def lower_home(name):
+        factors = [([down_own], 0, owned), ([need("down_pair")], 0, owned)]
+        factors.append(([need("down_near"), need("down_out")], 0, cut))
+        first, *others = rows_home()
+        return down([(rows, 0) for rows in (gate(name, first), *others)], factors)
+
+    def lift_home(name):
+        factors = [([up_own], 0, owned), ([need("up_pair")], 0, owned)]
+        factors.append(([need("up_near"), need("up_near_out")], 0, cut))
+        return lift([gate(name, need("low_home")), need("low_home_swap")], factors)
+
+    def lower_away(name):
+        first, *others = rows_away()
+        xs = [(rows, 0) for rows in (gate(name, first), *others)] + [(need("moved"), d) for d in range(COLUMNS)]
+        return down(xs, [([need("down_near")], cut, owned - cut), ([need("down_far")], 0, owned)])
+
+    def lift_away(name):
+        factors = [([need("up_near"), need("up_near_out")], cut, owned - cut)]
+        factors.append(([need("up_far"), need("up_far_out")], 0, owned))
+        return lift([gate(name, need("low_sum")), need("low_out")], factors)
+
+    def sum_away(name):
+        return (need("low_away") + need("low_away_swap")).astype(jnp.bfloat16)
+
+    def finish_home(name):
+        pieces = [need("rows_home")[0]] + [need(f"lift_home{d}") for d in (1, 2, 3)]
+        return finish(back_home, [gate(name, need("base_own")), need("base_other")], pieces, jnp.float32)
+
+    def finish_away(name):
+        pieces = [need("rows_away")[0]] + [need(f"lift_away{d}") for d in (1, 2, 3)]
+        return finish(back_away, [need("part")], pieces, jnp.bfloat16)
+
+    steps = {
+        "away": packed(0, rest),
+        "home": packed(split, served),
+        "given": lambda name: project(1 - tp, gate(name, hidden_input), query_weight),
+        "base_own": lambda name: project(tp, gate(name, hidden_input), query_weight),
+        "base_other": swap(lambda: need("given")),
+        "down_pair": send(pair, lambda: down_own),
+        "down_near": send(across, lambda: down_own),
+        "down_far": send(across, lambda: need("down_pair")),
+        "down_out": send(outward, lambda: need("down_near")[:cut]),
+        "up_pair": send(pair, lambda: up_own),
+        "up_near": send(across, lambda: up_own),
+        "up_far": send(across, lambda: need("up_pair")),
+        "up_near_out": send(outward, lambda: need("up_near")),
+        "up_far_out": send(outward, lambda: need("up_far")),
+        "joined": lambda name: join([gate(name, need("away")[0]), *rows_away()[1:]]),
+        "moved": send(inward, lambda: need("joined")),
+        "low_home": lower_home,
+        "low_home_swap": swap(lambda: need("low_home")),
+        "rows_home": lift_home,
+        "low_away": lower_away,
+        "low_away_swap": swap(lambda: need("low_away")),
+        "low_sum": sum_away,
+        "low_out": send(outward, lambda: need("low_sum")[need("low_sum").shape[0] // 2 :]),
+        "rows_away": lift_away,
+        "part": finish_home,
+        "queries": finish_away,
+        "onehots": lambda name: (back_away, back_home),
+    }
+    for d in (1, 2, 3):
+        for side in ("away", "home"):
+            steps[f"{side}{d}"] = send(turn[d], lambda d=d, side=side: need(side)[d])
+            steps[f"lift_{side}{d}"] = send(turn[d], lambda d=d, side=side: need(f"rows_{side}")[d])
+    return need("queries")
 
 
 def by_gather(hidden_input, query_weight, slot_down_weight, slot_up_weight, request_adapter, adapter_slot):

time: 240 us -> 227 us (0.946)
  waiting for transfers between devices: 77.1 us -> 60.9 us
  local copies, waits for them, and re-layouts: 9.93 us -> 13.4 us
    ppermute x26, waiting for transfers between devices: 77.1 us -> 60.9 us  [the longest x23 53.7 us: send(): return lambda name: lax.ppermute(gate(name, what()), 'rep', pairs)]
    unnamed x36 -> x44, local copies, waits for them, and re-layouts: 7.63 us -> 10.1 us
  transfers between devices with their start and end apart: 26 -> 26, of which waited for: 7 -> 10; matrix products, arithmetic and copies ran while one was open for 3% -> 3% of each run, Pallas kernels for 43% -> 42%
where the time goes in v4:
time: 227 us; the launch traced here: 226 us
  Pallas kernels  110 us (48%)
  waiting for transfers between devices  60.9 us (27%)
  starting transfers between devices  37.6 us (17%)
  local copies, waits for them, and re-layouts  13.4 us (6%)
  other arithmetic  3.15 us (1%)
    ppermute x23, waiting for transfers between devices, send(): return lambda name: lax.ppermute(gate(name, what()), 'rep', pairs)  53.7 us
    pallas_call x2, Pallas kernels, project(): pl.pallas_call(project_kernel, grid_spec=pltpu.PrefetchScalarGridSpec(num...  47.3 us
    ppermute x23, starting transfers between devices, send(): return lambda name: lax.ppermute(gate(name, what()), 'rep', pairs)  36.9 us
    pallas_call x2, Pallas kernels, finish(): pl.pallas_call(functools.partial(finish_kernel, len(bases)), grid=(column...  18.5 us
    pallas_call x2, Pallas kernels, pack(): pl.pallas_call(functools.partial(pack_kernel, first), grid=(width // tile...  17 us
    pallas_call x2, Pallas kernels, down(): pl.pallas_call(functools.partial(down_kernel, shape_of(groups), len(xs)),...  13 us
    unnamed x44, local copies, waits for them, and re-layouts  10.1 us
    pallas_call x2, Pallas kernels, lift(): pl.pallas_call(functools.partial(lift_kernel, shape_of(groups), len(ys)),...  10 us
  transfers between devices with their start and end apart: 26, of which 10 were waited for; matrix products, arithmetic and copies ran while one was open for 3% of the time, Pallas kernels for 42%

profile of v4, /device:TPU:0, one launch (start us, length us, event | category | flops | bytes accessed | tf_op | source)
XLA Modules:
  0.0 226.0 jit_solution(11212270600173118884)
XLA Ops:
  0.0 0.8 collective-permute-start.1
  0.8 5.8 %collective-permute-start = (bf16[4,64,4096]{2,1,0:T(8,128)(2,1)}, bf16[4,64,4096]{2,1,0:T(8,128)(2,1)}, u32[]{:S(2)}, u32[]{:S(2)}) collective-permute-start(bf16[4,64,4096]{2,1,0:T(8,128)(2,1)} %bitcast.7), channel_id=1, source_target_pairs={{0,8},{2,10},{4,12},{6,14},{8,0},{10,2},{12,4},{14,6},{16,24},{18,... | collective-permute-start | bytes 6291464 | tf_op jit(solution)/shard_map/ppermute | solution.py:303
  6.6 0.8 select_reduce_fusion
  8.7 7.5 %pack_rows.2 = (bf16[96,4096]{1,0:T(8,128)(2,1)}, bf16[96,4096]{1,0:T(8,128)(2,1)}, bf16[96,4096]{1,0:T(8,128)(2,1)}, bf16[96,4096]{1,0:T(8,128)(2,1)}) custom-call(s32[1,1024]{1,0:T(1,128)} %fusion.14.target_ref, bf16[1024,4096]{1,0:T(8,128)(2,1)} %x_ref.4), custom_call_target="tpu_custom_call" | custom-call | flops 3221225472 | bytes 11534336 | tf_op jit(solution)/shard_map/pack_rows/pallas_call | solution.py:43
  16.2 1.5 collective-permute-start.2
  17.7 1.5 collective-permute-start.3
  20.1 1.0 slice.16.onehot_ref
  21.2 1.2 slice.17.onehot_ref
  22.4 9.5 %pack_rows.3 = (bf16[160,4096]{1,0:T(8,128)(2,1)}, bf16[160,4096]{1,0:T(8,128)(2,1)}, bf16[160,4096]{1,0:T(8,128)(2,1)}, bf16[160,4096]{1,0:T(8,128)(2,1)}) custom-call(s32[1,1024]{1,0:T(1,128)} %fusion.14.target_ref, bf16[1024,4096]{1,0:T(8,128)(2,1)} %x_ref.4), custom_call_target="tpu_custom_call" | custom-call | flops 5368709120 | bytes 13631488 | tf_op jit(solution)/shard_map/pack_rows/pallas_call | solution.py:43
  31.9 23.7 %project_half.3 = bf16[1024,2048]{1,0:T(8,128)(2,1)} custom-call(s32[1]{0:T(128)} %bitcast.5.place_ref, bf16[1024,4096]{1,0:T(8,128)(2,1)} %x_ref.4, bf16[4096,4096]{1,0:T(8,128)(2,1)} %w_ref.3), custom_call_target="tpu_custom_call" | custom-call | flops 17179869184 | bytes 29360128 | tf_op jit(solution)/shard_map/project_half/pallas_call | solution.py:65
  55.5 1.6 collective-permute-start.10
  57.1 1.5 collective-permute-start.11
  58.6 4.4 %join_rows.1 = bf16[384,4096]{1,0:T(8,128)(2,1)} custom-call(bf16[96,4096]{1,0:T(8,128)(2,1)} %get-tuple-element.61.refs_0_, bf16[96,4096]{1,0:T(8,128)(2,1)} %copy-done.5, bf16[96,4096]{1,0:T(8,128)(2,1)} %collective-permute-done.3.refs_2_, bf16[96,4096]{1,0:T(8,128)(2,1)} %collective-permute-done.4.refs_3_), custom_call_target="tpu_custom_call" | custom-call | bytes 6291456 | tf_op jit(solution)/shard_map/join_rows/pallas_call | solution.py:224
  63.9 1.1 slice.18
  65.0 23.6 %project_half.2.rest_0_ = bf16[1024,2048]{1,0:T(8,128)(2,1)} custom-call(s32[1]{0:T(128)} %bitcast.1.place_ref, bf16[1024,4096]{1,0:T(8,128)(2,1)} %x_ref.4, bf16[4096,4096]{1,0:T(8,128)(2,1)} %w_ref.3), custom_call_target="tpu_custom_call" | custom-call | flops 17179869184 | bytes 29360128 | tf_op jit(solution)/shard_map/project_half/pallas_call | solution.py:65
  88.6 1.3 collective-permute-start.8
  90.7 1.0 copy-done.7
  91.7 8.5 %collective-permute-start.17 = (bf16[384,4096]{1,0:T(8,128)(2,1)}, bf16[384,4096]{1,0:T(8,128)(2,1)S(1)}, u32[]{:S(2)}, u32[]{:S(2)}) collective-permute-start(bf16[384,4096]{1,0:T(8,128)(2,1)} %join_rows.1), channel_id=1, source_target_pairs={{0,8},{2,10},{4,12},{6,14},{24,16},{26,18},{28,20},{30,22},{1,9},{... | collective-permute-start | bytes 9437192 | tf_op jit(solution)/shard_map/ppermute | solution.py:303
  100.8 13.5 %collective-permute-done.8.refs_7_ = bf16[2,64,4096]{2,1,0:T(8,128)(2,1)S(1)} collective-permute-done((bf16[2,64,4096]{2,1,0:T(8,128)(2,1)}, bf16[2,64,4096]{2,1,0:T(8,128)(2,1)S(1)}, u32[]{:S(2)}, u32[]{:S(2)}) %collective-permute-start.8) | collective-permute-done | bytes 1048608 | tf_op jit(solution)/shard_map/ppermute | solution.py:303
  114.3 1.3 collective-permute-start.9
  115.6 1.0 copy-done.11
  116.6 2.0 collective-permute-start.18
  118.6 10.2 %collective-permute-done.12.refs_3_ = bf16[160,4096]{1,0:T(8,128)(2,1)S(1)} collective-permute-done((bf16[160,4096]{1,0:T(8,128)(2,1)}, bf16[160,4096]{1,0:T(8,128)(2,1)S(1)}, u32[]{:S(2)}, u32[]{:S(2)}) %collective-permute-start.12) | collective-permute-done | bytes 1310752 | tf_op jit(solution)/shard_map/ppermute | solution.py:303
  128.9 1.1 copy-done.8
  129.9 6.6 %down_rows.2.refs_0_ = f32[640,256]{1,0:T(8,128)} custom-call(bf16[160,4096]{1,0:T(8,128)(2,1)} %get-tuple-element.45.refs_0_, bf16[160,4096]{1,0:T(8,128)(2,1)} %copy-done.7, bf16[160,4096]{1,0:T(8,128)(2,1)} %collective-permute-done.11.refs_2_, bf16[160,4096]{1,0:T(8,128)(2,1)} %copy-done.8, bf16[4,64,4096]{2,1,0:T(8,128)(2,1)} %bitcast.8, ...), custom_call_target="tpu_custom_call" | custom-call | flops 1342177280 | bytes 10485760 | tf_op jit(solution)/shard_map/down_rows/pallas_call | solution.py:140
  136.6 1.3 collective-permute-done.9.refs_5_.refs_3_
  137.9 1.3 collective-permute-start.13
  139.3 0.9 copy-done.16
  140.1 5.4 %lift_rows.2 = (bf16[160,2048]{1,0:T(8,128)(2,1)}, bf16[160,2048]{1,0:T(8,128)(2,1)}, bf16[160,2048]{1,0:T(8,128)(2,1)}, bf16[160,2048]{1,0:T(8,128)(2,1)}) custom-call(f32[640,256]{1,0:T(8,128)} %down_rows.2.refs_0_, f32[640,256]{1,0:T(8,128)} %copy-done.16, bf16[4,64,2048]{2,1,0:T(8,128)(2,1)} %refs_2_.1, ...), custom_call_target="tpu_custom_call" | custom-call | flops 671088640 | bytes 5242880 | tf_op jit(solution)/shard_map/lift_rows/pallas_call | solution.py:174
  146.1 1.1 collective-permute-start.16
  147.2 14.9 %collective-permute-done.15.rest_3_ = bf16[160,2048]{1,0:T(8,128)(2,1)S(1)} collective-permute-done((bf16[160,2048]{1,0:T(8,128)(2,1)}, bf16[160,2048]{1,0:T(8,128)(2,1)S(1)}, u32[]{:S(2)}, u32[]{:S(2)}) %collective-permute-start.15) | collective-permute-done | bytes 655392 | tf_op jit(solution)/shard_map/ppermute | solution.py:303
  162.4 1.8 collective-permute-done.13.refs_5_
  164.9 1.6 copy-done
  166.5 6.4 %down_rows.3 = f32[768,256]{1,0:T(8,128)} custom-call(bf16[96,4096]{1,0:T(8,128)(2,1)} %get-tuple-element.61.refs_0_, bf16[96,4096]{1,0:T(8,128)(2,1)} %copy-done.5, bf16[96,4096]{1,0:T(8,128)(2,1)} %collective-permute-done.3.refs_2_, bf16[96,4096]{1,0:T(8,128)(2,1)} %collective-permute-done.4.refs_3_, bf16[384,4096]{1,0:T(8,128)(2,1)} %copy-done, ...), custom_call_target="tpu_custom_call" | custom-call | flops 1610612736 | bytes 9437184 | tf_op jit(solution)/shard_map/down_rows/pallas_call | solution.py:140
  173.6 0.8 collective-permute-start.22
  174.3 7.2 %collective-permute-done.19 = f32[768,256]{1,0:T(8,128)S(1)} collective-permute-done((f32[768,256]{1,0:T(8,128)}, f32[768,256]{1,0:T(8,128)S(1)}, u32[]{:S(2)}, u32[]{:S(2)}) %collective-permute-start.19) | collective-permute-done | bytes 786464 | tf_op jit(solution)/shard_map/ppermute | solution.py:306
  181.5 1.2 add_convert_fusion.refs_0_
  182.8 1.3 collective-permute-start.20
  184.1 7.6 %collective-permute-done.20.refs_1_ = bf16[384,256]{1,0:T(8,128)(2,1)S(1)} collective-permute-done((bf16[384,256]{1,0:T(8,128)(2,1)S(1)}, bf16[384,256]{1,0:T(8,128)(2,1)S(1)}, u32[]{:S(2)}, u32[]{:S(2)}) %collective-permute-start.20) | collective-permute-done | bytes 196640 | tf_op jit(solution)/shard_map/ppermute | solution.py:303
  192.3 4.6 %lift_rows.3 = (bf16[96,2048]{1,0:T(8,128)(2,1)}, bf16[96,2048]{1,0:T(8,128)(2,1)}, bf16[96,2048]{1,0:T(8,128)(2,1)}, bf16[96,2048]{1,0:T(8,128)(2,1)}) custom-call(bf16[768,256]{1,0:T(8,128)(2,1)} %copy-done.6, bf16[384,256]{1,0:T(8,128)(2,1)} %copy-done.20, bf16[4,64,2048]{2,1,0:T(8,128)(2,1)} %copy-done.3, bf16[4,64,2048]{2,1,0:T(8,128)(2,1)} %copy-done.4, ...), custom_call_target="tpu_custom_call" | custom-call | flops 402653184 | bytes 3145728 | tf_op jit(solution)/shard_map/lift_rows/pallas_call | solution.py:174
  197.5 0.8 collective-permute-start.24
  198.3 2.1 collective-permute-start.25
  200.5 0.8 copy-done.15
  201.3 1.4 copy-done.2
  202.7 10.2 %finish_rows.2.rest_0_ = f32[1024,2048]{1,0:T(8,128)} custom-call(bf16[1024,640]{1,0:T(8,128)(2,1)} %slice.17.onehot_ref, bf16[1024,2048]{1,0:T(8,128)(2,1)} %project_half.2.rest_0_, bf16[1024,2048]{1,0:T(8,128)(2,1)} %copy-done.2, bf16[160,2048]{1,0:T(8,128)(2,1)} %get-tuple-element.70.rest_2_, bf16[160,2048]{1,0:T(8,128)(2,1)} %copy-done.13, ...), custom_call_target="tpu_custom_call" | custom-call | flops 2684354560 | bytes 16777216 | tf_op jit(solution)/shard_map/finish_rows/pallas_call | solution.py:200
  212.9 3.3 %collective-permute-done.24.rest_3_ = bf16[96,2048]{1,0:T(8,128)(2,1)S(1)} collective-permute-done((bf16[96,2048]{1,0:T(8,128)(2,1)}, bf16[96,2048]{1,0:T(8,128)(2,1)S(1)}, u32[]{:S(2)}, u32[]{:S(2)}) %collective-permute-start.24) | collective-permute-done | bytes 393248 | tf_op jit(solution)/shard_map/ppermute | solution.py:303
  216.9 0.8 copy-done.19
  217.7 8.3 %finish_rows.3 = bf16[1024,2048]{1,0:T(8,128)(2,1)} custom-call(bf16[1024,384]{1,0:T(8,128)(2,1)} %slice.16.onehot_ref, f32[1024,2048]{1,0:T(8,128)} %finish_rows.2.rest_0_, bf16[96,2048]{1,0:T(8,128)(2,1)} %get-tuple-element.64.rest_1_, bf16[96,2048]{1,0:T(8,128)(2,1)} %copy-done.17, bf16[96,2048]{1,0:T(8,128)(2,1)} %copy-done.18, bf16[96,2048]{1,0:T(8,128)(2,1)} %copy-done.19), custom_call_target="tpu_custom_call" | custom-call | flops 1610612736 | bytes 16777216 | tf_op jit(solution)/shard_map/finish_rows/pallas_call | solution.py:200
  (70 shorter events, 8.5 us)
Async XLA Ops:
  0.0 63.0 %collective-permute-start.1 = (bf16[4,64,4096]{2,1,0:T(8,128)(2,1)}, bf16[4,64,4096]{2,1,0:T(8,128)(2,1)S(1)}, u32[]{:S(2)}, u32[]{:S(2)}) collective-permute-start(bf16[4,64,4096]{2,1,0:T(8,128)(2,1)} %bitcast.6), channel_id=1, source_target_pairs={{8,16},{10,18},{12,20},{14,22},{16,8},{18,10},{20,12},{22,14},{9,1... | collective-permute-start | bytes 6291464 | tf_op jit(solution)/shard_map/ppermute | solution.py:303
  0.8 62.2 %collective-permute-start = (bf16[4,64,4096]{2,1,0:T(8,128)(2,1)}, bf16[4,64,4096]{2,1,0:T(8,128)(2,1)}, u32[]{:S(2)}, u32[]{:S(2)}) collective-permute-start(bf16[4,64,4096]{2,1,0:T(8,128)(2,1)} %bitcast.7), channel_id=1, source_target_pairs={{0,8},{2,10},{4,12},{6,14},{8,0},{10,2},{12,4},{14,6},{16,24},{18,... | collective-permute-start | bytes 6291464 | tf_op jit(solution)/shard_map/ppermute | solution.py:303
  16.2 39.3 %collective-permute-start.2 = (bf16[96,4096]{1,0:T(8,128)(2,1)}, bf16[96,4096]{1,0:T(8,128)(2,1)S(1)}, u32[]{:S(2)}, u32[]{:S(2)}) collective-permute-start(bf16[96,4096]{1,0:T(8,128)(2,1)} %get-tuple-element.40), channel_id=1, source_target_pairs={{0,2},{2,0},{4,6},{6,4},{8,10},{10,8},{12,14},{14,12},{16,18},{18,... | collective-permute-start | bytes 2359304 | tf_op jit(solution)/shard_map/ppermute | solution.py:303
  17.7 37.8 %collective-permute-start.3 = (bf16[96,4096]{1,0:T(8,128)(2,1)}, bf16[96,4096]{1,0:T(8,128)(2,1)}, u32[]{:S(2)}, u32[]{:S(2)}) collective-permute-start(bf16[96,4096]{1,0:T(8,128)(2,1)} %get-tuple-element.41), channel_id=1, source_target_pairs={{0,4},{2,6},{4,0},{6,2},{8,12},{10,14},{12,8},{14,10},{16,20},{18,... | collective-permute-start | bytes 2359304 | tf_op jit(solution)/shard_map/ppermute | solution.py:303
  19.2 39.4 %collective-permute-start.4 = (bf16[96,4096]{1,0:T(8,128)(2,1)}, bf16[96,4096]{1,0:T(8,128)(2,1)}, u32[]{:S(2)}, u32[]{:S(2)}) collective-permute-start(bf16[96,4096]{1,0:T(8,128)(2,1)} %get-tuple-element.42), channel_id=1, source_target_pairs={{0,6},{2,4},{4,2},{6,0},{8,14},{10,12},{12,10},{14,8},{16,22},{18,... | collective-permute-start | bytes 2359304 | tf_op jit(solution)/shard_map/ppermute | solution.py:303
  55.5 7.5 %copy-start.10 = (bf16[4,64,2048]{2,1,0:T(8,128)(2,1)S(1)}, bf16[4,64,2048]{2,1,0:T(8,128)(2,1)}, u32[]{:S(2)}) copy-start(bf16[4,64,2048]{2,1,0:T(8,128)(2,1)} %refs_2_.1) | copy-start | bytes 3145732
  55.5 3.1 %copy-start.5 = (bf16[96,4096]{1,0:T(8,128)(2,1)}, bf16[96,4096]{1,0:T(8,128)(2,1)S(1)}, u32[]{:S(2)}) copy-start(bf16[96,4096]{1,0:T(8,128)(2,1)S(1)} %collective-permute-done.2.refs_1_) | copy-start | bytes 2359300
  55.5 35.1 %collective-permute-start.10 = (bf16[160,4096]{1,0:T(8,128)(2,1)}, bf16[160,4096]{1,0:T(8,128)(2,1)S(1)}, u32[]{:S(2)}, u32[]{:S(2)}) collective-permute-start(bf16[160,4096]{1,0:T(8,128)(2,1)} %get-tuple-element.55), channel_id=1, source_target_pairs={{0,2},{2,0},{4,6},{6,4},{8,10},{10,8},{12,14},{14,12},{16,18},{18,... | collective-permute-start | bytes 3932168 | tf_op jit(solution)/shard_map/ppermute | solution.py:303
  57.1 34.6 %collective-permute-start.11 = (bf16[160,4096]{1,0:T(8,128)(2,1)}, bf16[160,4096]{1,0:T(8,128)(2,1)}, u32[]{:S(2)}, u32[]{:S(2)}) collective-permute-start(bf16[160,4096]{1,0:T(8,128)(2,1)} %get-tuple-element.56), channel_id=1, source_target_pairs={{0,4},{2,6},{4,0},{6,2},{8,12},{10,14},{12,8},{14,10},{16,20},{18,... | collective-permute-start | bytes 3932168 | tf_op jit(solution)/shard_map/ppermute | solution.py:303
  63.0 25.6 %copy-start.1 = (bf16[4,64,4096]{2,1,0:T(8,128)(2,1)}, bf16[4,64,4096]{2,1,0:T(8,128)(2,1)S(1)}, u32[]{:S(2)}) copy-start(bf16[4,64,4096]{2,1,0:T(8,128)(2,1)S(1)} %collective-permute-done.1.refs_6_.refs_8_) | copy-start | bytes 6291460
  63.1 25.6 %collective-permute-start.5 = (bf16[4,64,2048]{2,1,0:T(8,128)(2,1)S(1)}, bf16[4,64,2048]{2,1,0:T(8,128)(2,1)}, u32[]{:S(2)}, u32[]{:S(2)}) collective-permute-start(bf16[4,64,2048]{2,1,0:T(8,128)(2,1)S(1)} %copy-done.10), channel_id=1, source_target_pairs={{0,8},{2,10},{4,12},{6,14},{8,0},{10,2},{12,4},{14,6},{16,24},{18,... | collective-permute-start | bytes 3145736 | tf_op jit(solution)/shard_map/ppermute | solution.py:303
  63.2 26.7 %collective-permute-start.6 = (bf16[4,64,2048]{2,1,0:T(8,128)(2,1)S(1)}, bf16[4,64,2048]{2,1,0:T(8,128)(2,1)S(1)}, u32[]{:S(2)}, u32[]{:S(2)}) collective-permute-start(bf16[4,64,2048]{2,1,0:T(8,128)(2,1)S(1)} %copy-done.10), channel_id=1, source_target_pairs={{8,16},{10,18},{12,20},{14,22},{16,8},{18,10},{20,12},{22,14},{9,1... | collective-permute-start | bytes 3145736 | tf_op jit(solution)/shard_map/ppermute | solution.py:303
  88.6 25.7 %collective-permute-start.8 = (bf16[2,64,4096]{2,1,0:T(8,128)(2,1)}, bf16[2,64,4096]{2,1,0:T(8,128)(2,1)S(1)}, u32[]{:S(2)}, u32[]{:S(2)}) collective-permute-start(bf16[2,64,4096]{2,1,0:T(8,128)(2,1)} %slice.18), channel_id=1, source_target_pairs={{8,0},{10,2},{12,4},{14,6},{16,24},{18,26},{20,28},{22,30},{9,1},{... | collective-permute-start | bytes 3145736 | tf_op jit(solution)/shard_map/ppermute | solution.py:303
  89.9 46.6 %copy-start.3 = (bf16[4,64,2048]{2,1,0:T(8,128)(2,1)}, bf16[4,64,2048]{2,1,0:T(8,128)(2,1)S(1)}, u32[]{:S(2)}) copy-start(bf16[4,64,2048]{2,1,0:T(8,128)(2,1)S(1)} %collective-permute-done.6.refs_4_.refs_2_) | copy-start | bytes 3145732
  89.9 25.7 %collective-permute-start.7 = (bf16[4,64,2048]{2,1,0:T(8,128)(2,1)}, bf16[4,64,2048]{2,1,0:T(8,128)(2,1)S(1)}, u32[]{:S(2)}, u32[]{:S(2)}) collective-permute-start(bf16[4,64,2048]{2,1,0:T(8,128)(2,1)} %collective-permute-done.5.refs_3_), channel_id=1, source_target_pairs={{8,16},{10,18},{12,20},{14,22},{16,8},{18,10},{20,12},{22,14},{9,1... | collective-permute-start | bytes 3145736 | tf_op jit(solution)/shard_map/ppermute | solution.py:303
  90.7 1.1 copy-start.7
  91.7 73.2 %collective-permute-start.17 = (bf16[384,4096]{1,0:T(8,128)(2,1)}, bf16[384,4096]{1,0:T(8,128)(2,1)S(1)}, u32[]{:S(2)}, u32[]{:S(2)}) collective-permute-start(bf16[384,4096]{1,0:T(8,128)(2,1)} %join_rows.1), channel_id=1, source_target_pairs={{0,8},{2,10},{4,12},{6,14},{24,16},{26,18},{28,20},{30,22},{1,9},{... | collective-permute-start | bytes 9437192 | tf_op jit(solution)/shard_map/ppermute | solution.py:303
  100.3 28.6 %collective-permute-start.12 = (bf16[160,4096]{1,0:T(8,128)(2,1)}, bf16[160,4096]{1,0:T(8,128)(2,1)S(1)}, u32[]{:S(2)}, u32[]{:S(2)}) collective-permute-start(bf16[160,4096]{1,0:T(8,128)(2,1)} %get-tuple-element.57), channel_id=1, source_target_pairs={{0,6},{2,4},{4,2},{6,0},{8,14},{10,12},{12,10},{14,8},{16,22},{18,... | collective-permute-start | bytes 3932168 | tf_op jit(solution)/shard_map/ppermute | solution.py:303
  114.3 14.5 %copy-start.9 = (bf16[2,64,4096]{2,1,0:T(8,128)(2,1)}, bf16[2,64,4096]{2,1,0:T(8,128)(2,1)S(1)}, u32[]{:S(2)}) copy-start(bf16[2,64,4096]{2,1,0:T(8,128)(2,1)S(1)} %collective-permute-done.8.refs_7_) | copy-start | bytes 3145732
  114.3 23.6 %collective-permute-start.9 = (bf16[4,64,2048]{2,1,0:T(8,128)(2,1)S(1)}, bf16[4,64,2048]{2,1,0:T(8,128)(2,1)S(1)}, u32[]{:S(2)}, u32[]{:S(2)}) collective-permute-start(bf16[4,64,2048]{2,1,0:T(8,128)(2,1)S(1)} %collective-permute-done.6.refs_4_.refs_2_), channel_id=1, source_target_pairs={{8,0},{10,2},{12,4},{14,6},{16,24},{18,26},{20,28},{22,30},{9,1},{... | collective-permute-start | bytes 3145736 | tf_op jit(solution)/shard_map/ppermute | solution.py:303
  115.6 1.0 copy-start.11
  116.6 47.6 %collective-permute-start.18 = (bf16[4,64,4096]{2,1,0:T(8,128)(2,1)}, bf16[4,64,4096]{2,1,0:T(8,128)(2,1)}, u32[]{:S(2)}, u32[]{:S(2)}) collective-permute-start(bf16[4,64,4096]{2,1,0:T(8,128)(2,1)} %collective-permute-done.refs_5_), channel_id=1, source_target_pairs={{8,16},{10,18},{12,20},{14,22},{16,8},{18,10},{20,12},{22,14},{9,1... | collective-permute-start | bytes 6291464 | tf_op jit(solution)/shard_map/ppermute | solution.py:303
  128.9 1.1 copy-start.8
  136.5 2.7 %collective-permute-start.14 = (f32[640,256]{1,0:T(8,128)}, f32[640,256]{1,0:T(8,128)S(1)}, u32[]{:S(2)}, u32[]{:S(2)}) collective-permute-start(f32[640,256]{1,0:T(8,128)} %down_rows.2.refs_0_), channel_id=1, source_target_pairs={{0,1},{1,0},{2,3},{3,2},{4,5},{5,4},{6,7},{7,6},{8,9},{9,8},{10,11... | collective-permute-start | bytes 1966088 | tf_op jit(solution)/shard_map/ppermute | solution.py:306
  137.9 1.3 copy-start.4
  137.9 26.3 %collective-permute-start.13 = (bf16[4,64,2048]{2,1,0:T(8,128)(2,1)}, bf16[4,64,2048]{2,1,0:T(8,128)(2,1)S(1)}, u32[]{:S(2)}, u32[]{:S(2)}) collective-permute-start(bf16[4,64,2048]{2,1,0:T(8,128)(2,1)} %copy-done.11), channel_id=1, source_target_pairs={{8,0},{10,2},{12,4},{14,6},{16,24},{18,26},{20,28},{22,30},{9,1},{... | collective-permute-start | bytes 3145736 | tf_op jit(solution)/shard_map/ppermute | solution.py:303
  139.2 0.9 copy-start.16
  145.5 16.7 %collective-permute-start.15 = (bf16[160,2048]{1,0:T(8,128)(2,1)}, bf16[160,2048]{1,0:T(8,128)(2,1)S(1)}, u32[]{:S(2)}, u32[]{:S(2)}) collective-permute-start(bf16[160,2048]{1,0:T(8,128)(2,1)} %get-tuple-element.59), channel_id=1, source_target_pairs={{0,2},{2,0},{4,6},{6,4},{8,10},{10,8},{12,14},{14,12},{16,18},{18,... | collective-permute-start | bytes 1966088 | tf_op jit(solution)/shard_map/ppermute | solution.py:303
  146.1 27.5 %copy-start.21 = (bf16[160,2048]{1,0:T(8,128)(2,1)S(1)}, bf16[160,2048]{1,0:T(8,128)(2,1)}, u32[]{:S(2)}) copy-start(bf16[160,2048]{1,0:T(8,128)(2,1)} %get-tuple-element.72) | copy-start | bytes 1966084
  146.1 16.3 %collective-permute-start.16 = (bf16[160,2048]{1,0:T(8,128)(2,1)}, bf16[160,2048]{1,0:T(8,128)(2,1)S(1)}, u32[]{:S(2)}, u32[]{:S(2)}) collective-permute-start(bf16[160,2048]{1,0:T(8,128)(2,1)} %get-tuple-element.60), channel_id=1, source_target_pairs={{0,4},{2,6},{4,0},{6,2},{8,12},{10,14},{12,8},{14,10},{16,20},{18,... | collective-permute-start | bytes 1966088 | tf_op jit(solution)/shard_map/ppermute | solution.py:303
  162.2 10.8 %copy-start.13 = (bf16[160,2048]{1,0:T(8,128)(2,1)}, bf16[160,2048]{1,0:T(8,128)(2,1)S(1)}, u32[]{:S(2)}) copy-start(bf16[160,2048]{1,0:T(8,128)(2,1)S(1)} %collective-permute-done.15.rest_3_) | copy-start | bytes 1966084
  162.4 10.5 %copy-start.14 = (bf16[160,2048]{1,0:T(8,128)(2,1)}, bf16[160,2048]{1,0:T(8,128)(2,1)S(1)}, u32[]{:S(2)}) copy-start(bf16[160,2048]{1,0:T(8,128)(2,1)S(1)} %collective-permute-done.16.rest_4_) | copy-start | bytes 1966084
  164.2 8.7 %copy-start.12 = (bf16[4,64,2048]{2,1,0:T(8,128)(2,1)}, bf16[4,64,2048]{2,1,0:T(8,128)(2,1)S(1)}, u32[]{:S(2)}) copy-start(bf16[4,64,2048]{2,1,0:T(8,128)(2,1)S(1)} %collective-permute-done.13.refs_5_) | copy-start | bytes 3145732
  164.9 1.6 copy-start
  173.0 27.5 %collective-permute-start.21 = (bf16[1024,2048]{1,0:T(8,128)(2,1)}, bf16[1024,2048]{1,0:T(8,128)(2,1)S(1)}, u32[]{:S(2)}, u32[]{:S(2)}) collective-permute-start(bf16[1024,2048]{1,0:T(8,128)(2,1)} %project_half.3), channel_id=1, source_target_pairs={{0,1},{1,0},{2,3},{3,2},{4,5},{5,4},{6,7},{7,6},{8,9},{9,8},{10,11... | collective-permute-start | bytes 12582920 | tf_op jit(solution)/shard_map/ppermute | solution.py:306
  173.0 8.5 %collective-permute-start.19 = (f32[768,256]{1,0:T(8,128)}, f32[768,256]{1,0:T(8,128)S(1)}, u32[]{:S(2)}, u32[]{:S(2)}) collective-permute-start(f32[768,256]{1,0:T(8,128)} %down_rows.3), channel_id=1, source_target_pairs={{0,1},{1,0},{2,3},{3,2},{4,5},{5,4},{6,7},{7,6},{8,9},{9,8},{10,11... | collective-permute-start | bytes 2359304 | tf_op jit(solution)/shard_map/ppermute | solution.py:306
  173.6 26.9 %collective-permute-start.22 = (bf16[160,2048]{1,0:T(8,128)(2,1)S(1)}, bf16[160,2048]{1,0:T(8,128)(2,1)S(1)}, u32[]{:S(2)}, u32[]{:S(2)}) collective-permute-start(bf16[160,2048]{1,0:T(8,128)(2,1)S(1)} %copy-done.21), channel_id=1, source_target_pairs={{0,6},{2,4},{4,2},{6,0},{8,14},{10,12},{12,10},{14,8},{16,22},{18,... | collective-permute-start | bytes 1966088 | tf_op jit(solution)/shard_map/ppermute | solution.py:303
  182.7 8.9 %copy-start.6 = (bf16[768,256]{1,0:T(8,128)(2,1)}, bf16[768,256]{1,0:T(8,128)(2,1)S(1)}, u32[]{:S(2)}) copy-start(bf16[768,256]{1,0:T(8,128)(2,1)S(1)} %add_convert_fusion.refs_0_) | copy-start | bytes 1179652
  182.8 8.9 %collective-permute-start.20 = (bf16[384,256]{1,0:T(8,128)(2,1)S(1)}, bf16[384,256]{1,0:T(8,128)(2,1)S(1)}, u32[]{:S(2)}, u32[]{:S(2)}) collective-permute-start(bf16[384,256]{1,0:T(8,128)(2,1)S(1)} %slice.19), channel_id=1, source_target_pairs={{8,0},{10,2},{12,4},{14,6},{16,24},{18,26},{20,28},{22,30},{9,1},{... | collective-permute-start | bytes 589832 | tf_op jit(solution)/shard_map/ppermute | solution.py:303
  191.6 0.7 copy-start.20
  196.9 16.0 %collective-permute-start.23 = (bf16[96,2048]{1,0:T(8,128)(2,1)}, bf16[96,2048]{1,0:T(8,128)(2,1)S(1)}, u32[]{:S(2)}, u32[]{:S(2)}) collective-permute-start(bf16[96,2048]{1,0:T(8,128)(2,1)} %get-tuple-element.65), channel_id=1, source_target_pairs={{0,2},{2,0},{4,6},{6,4},{8,10},{10,8},{12,14},{14,12},{16,18},{18,... | collective-permute-start | bytes 1179656 | tf_op jit(solution)/shard_map/ppermute | solution.py:303
  197.5 18.7 %collective-permute-start.24 = (bf16[96,2048]{1,0:T(8,128)(2,1)}, bf16[96,2048]{1,0:T(8,128)(2,1)S(1)}, u32[]{:S(2)}, u32[]{:S(2)}) collective-permute-start(bf16[96,2048]{1,0:T(8,128)(2,1)} %get-tuple-element.66), channel_id=1, source_target_pairs={{0,4},{2,6},{4,0},{6,2},{8,12},{10,14},{12,8},{14,10},{16,20},{18,... | collective-permute-start | bytes 1179656 | tf_op jit(solution)/shard_map/ppermute | solution.py:303
  198.3 17.9 %collective-permute-start.25 = (bf16[96,2048]{1,0:T(8,128)(2,1)}, bf16[96,2048]{1,0:T(8,128)(2,1)S(1)}, u32[]{:S(2)}, u32[]{:S(2)}) collective-permute-start(bf16[96,2048]{1,0:T(8,128)(2,1)} %get-tuple-element.67), channel_id=1, source_target_pairs={{0,6},{2,4},{4,2},{6,0},{8,14},{10,12},{12,10},{14,8},{16,22},{18,... | collective-permute-start | bytes 1179656 | tf_op jit(solution)/shard_map/ppermute | solution.py:303
  200.4 0.8 copy-start.15
  200.4 2.2 copy-start.2
  212.9 3.3 %copy-start.17 = (bf16[96,2048]{1,0:T(8,128)(2,1)}, bf16[96,2048]{1,0:T(8,128)(2,1)S(1)}, u32[]{:S(2)}) copy-start(bf16[96,2048]{1,0:T(8,128)(2,1)S(1)} %collective-permute-done.23.rest_2_) | copy-start | bytes 1179652
  216.2 0.7 copy-start.18
  216.9 0.8 copy-start.19

commit v5 on v3

--- a/solution.py
+++ b/solution.py
@@ -13,6 +13,7 @@
 SWAP = [(0, 1), (1, 0)]
 LIMIT = 56 * 1024 * 1024
 NT = (((1,), (1,)), ((), ()))
+TILE = 256
 
 
 def params(steps=1):
@@ -23,32 +24,33 @@
     return pl.CostEstimate(flops=flops, bytes_accessed=size, transcendentals=0)
 
 
-def pack_kernel(first, target_ref, x_ref, *rest):
+def pack_kernel(target_ref, x_ref, *rest):
     outs, onehot = rest[:-1], rest[-1]
 
     @pl.when(pl.program_id(0) == 0)
     def _():
-        place = lax.broadcasted_iota(jnp.int32, onehot.shape, 0) + first
+        place = lax.broadcasted_iota(jnp.int32, onehot.shape, 0)
         onehot[...] = (place == target_ref[...]).astype(jnp.bfloat16)
 
     packed = jnp.dot(onehot[...], x_ref[...], preferred_element_type=jnp.float32).astype(jnp.bfloat16)
-    part = onehot.shape[0] // len(outs)
-    for k, out in enumerate(outs):
-        out[...] = packed[k * part : (k + 1) * part]
-
-
-def pack(target, x, first, part, parts):
+    at = 0
+    for out in outs:
+        out[...] = packed[at : at + out.shape[0]]
+        at += out.shape[0]
+
+
+def pack(target, x, parts):
     rows, width = x.shape
     tile = 1024
     return pl.pallas_call(
-        functools.partial(pack_kernel, first),
+        pack_kernel,
         grid=(width // tile,),
         in_specs=[pl.BlockSpec((1, rows), lambda i: (0, 0)), pl.BlockSpec((rows, tile), lambda i: (0, i))],
-        out_specs=[pl.BlockSpec((part, tile), lambda i: (0, i))] * parts,
-        out_shape=[jax.ShapeDtypeStruct((part, width), x.dtype)] * parts,
-        scratch_shapes=[pltpu.VMEM((part * parts, rows), jnp.bfloat16)],
-        compiler_params=params(),
-        cost_estimate=cost(2 * part * parts * rows * width, 2 * (rows + part * parts) * width),
+        out_specs=[pl.BlockSpec((part, tile), lambda i: (0, i)) for part in parts],
+        out_shape=[jax.ShapeDtypeStruct((part, width), x.dtype) for part in parts],
+        scratch_shapes=[pltpu.VMEM((sum(parts), rows), jnp.bfloat16)],
+        compiler_params=params(),
+        cost_estimate=cost(2 * sum(parts) * rows * width, 2 * (rows + sum(parts)) * width),
         name="pack_rows",
     )(target, x)
 
@@ -57,19 +59,19 @@
     o_ref[...] = jnp.dot(x_ref[...], w_ref[...], preferred_element_type=jnp.float32).astype(o_ref.dtype)
 
 
-def project(half, x, w):
+def project(half, x, w, first, count):
     rows, width = x.shape
-    columns = w.shape[1] // 2
-    tile = 256
-    steps = columns // tile
+    tile = TILE
+    steps = w.shape[1] // 2 // tile
+    columns = count * tile
     return pl.pallas_call(
         project_kernel,
         grid_spec=pltpu.PrefetchScalarGridSpec(
             num_scalar_prefetch=1,
-            grid=(steps,),
+            grid=(count,),
             in_specs=[
                 pl.BlockSpec((rows, width), lambda i, place: (0, 0)),
-                pl.BlockSpec((width, tile), lambda i, place: (0, place[0] * steps + i)),
+                pl.BlockSpec((width, tile), lambda i, place: (0, place[0] * steps + first + i)),
             ],
             out_specs=pl.BlockSpec((rows, tile), lambda i, place: (0, i)),
         ),
@@ -184,31 +186,45 @@
     )(*ys, *flat(groups))
 
 
-def finish_kernel(count, onehot_ref, *rest):
+def finish_kernel(starts, onehot_ref, *rest):
+    count = sum(len(own) for own in starts)
     bases, pieces, o_ref = rest[:count], rest[count:-1], rest[-1]
+    step = pl.program_id(0)
     lifted = jnp.concatenate([piece[...] for piece in pieces], axis=0)
     total = jnp.dot(onehot_ref[...], lifted, preferred_element_type=jnp.float32)
-    for base in bases:
-        total += base[...].astype(jnp.float32)
+    at = 0
+    for own in starts:
+        base = bases[at][...]
+        for k in range(1, len(own)):
+            base = jnp.where(step >= own[k], bases[at + k][...], base)
+        total += base.astype(jnp.float32)
+        at += len(own)
     o_ref[...] = total.astype(o_ref.dtype)
 
 
-def finish(onehot, bases, pieces, dtype):
-    rows, columns = bases[0].shape
-    tile = 512
+def finish(onehot, bases, pieces, tile, dtype):
+    rows, columns = onehot.shape[0], pieces[0].shape[1]
     held = onehot.shape[1]
-    return pl.pallas_call(
-        functools.partial(finish_kernel, len(bases)),
+    starts, specs = [], []
+    for arrays in bases:
+        at, own = 0, []
+        for array in arrays:
+            steps = array.shape[1] // tile
+            own.append(at)
+            specs.append(pl.BlockSpec((rows, tile), lambda i, at=at, steps=steps: (0, jnp.clip(i - at, 0, steps - 1))))
+            at += steps
+        starts.append(own)
+    return pl.pallas_call(
+        functools.partial(finish_kernel, starts),
         grid=(columns // tile,),
-        in_specs=[pl.BlockSpec((rows, held), lambda i: (0, 0))]
-        + [pl.BlockSpec((rows, tile), lambda i: (0, i)) for _ in bases]
+        in_specs=[pl.BlockSpec((rows, held), lambda i: (0, 0)), *specs]
         + [pl.BlockSpec((piece.shape[0], tile), lambda i: (0, i)) for piece in pieces],
         out_specs=pl.BlockSpec((rows, tile), lambda i: (0, i)),
         out_shape=jax.ShapeDtypeStruct((rows, columns), dtype),
         compiler_params=params(),
         cost_estimate=cost(2 * rows * held * columns, 8 * rows * columns),
         name="finish_rows",
-    )(onehot, *bases, *pieces)
+    )(onehot, *[array for arrays in bases for array in arrays], *pieces)
 
 
 def join_kernel(*refs):
@@ -285,57 +301,66 @@
     down_own = jnp.swapaxes(slot_down_weight, 1, 2)
     up_own = slot_up_weight
     tp = lax.axis_index("tp")
+    tiles = query_weight.shape[1] // 2 // TILE
+    early = tiles * 5 // 8
     down_pair = send(down_own, pair)
     down_near = send(down_own, across)
 
-    split = COLUMNS * rest * MOST
-    away = pack(target[None, :], hidden_input, 0, rest * MOST, COLUMNS)
-    home = pack(target[None, :], after(hidden_input, away[0]), split, served * MOST, COLUMNS)
-    spots = lax.broadcasted_iota(jnp.int32, (target.shape[0], 4 * owned * COLUMNS * MOST), 1)
-    onehot = (target[:, None] == spots).astype(jnp.bfloat16)
-    back_away, back_home = onehot[:, :split], onehot[:, split:]
+    packed = pack(target[None, :], hidden_input, [rest * MOST] * COLUMNS + [served * MOST] * COLUMNS)
+    away, home = packed[:COLUMNS], packed[COLUMNS:]
     away = [away[0]] + [send(away[d], turn[d]) for d in range(1, COLUMNS)]
-    given = project(1 - tp, after(hidden_input, home[0], back_away, back_home), query_weight)
+    given = project(1 - tp, after(hidden_input, home[0]), query_weight, 0, tiles)
 
     up_pair = send(up_own, pair, down_pair, given)
     up_near = send(up_own, across, down_near, given)
     beside = [home[0]] + [send(home[d], turn[d], away[d], given) for d in (1, 2)]
     moving = join(away)
-    base_own = project(tp, after(hidden_input, down_pair, down_near, moving), query_weight)
-
-    moved = send(moving, inward, up_pair, beside[1], beside[2], base_own)
-    down_out = send(down_near[:cut], outward, up_pair, base_own)
-    up_far = send(up_pair, across, up_near, base_own)
-    beside.append(send(home[3], turn[3], beside[1], beside[2], base_own))
+    base_own = [project(tp, after(hidden_input, down_pair, down_near, moving), query_weight, 0, early)]
+
+    moved = send(moving, inward, up_pair, base_own[0])
+    down_out = send(down_near[:cut], outward, up_pair, base_own[0])
+    up_far = send(up_pair, across, up_near, base_own[0])
+    beside.append(send(home[3], turn[3], beside[1], beside[2], base_own[0]))
+    base_own.append(project(tp, after(hidden_input, beside[1], beside[2], up_near), query_weight, early, tiles - early))
     down_far = send(down_pair, across, up_far, down_out)
-    up_near_out = send(up_near, outward, down_out)
-    base_other = lax.ppermute(after(given, beside[3]), "tp", SWAP)
-
-    def swapped(y):
-        return lax.ppermute(y, "tp", SWAP)
+    up_near_out = send(up_near, outward, down_out, base_own[1])
+
+    split = COLUMNS * rest * MOST
+    spots = lax.broadcasted_iota(jnp.int32, (target.shape[0], 4 * owned * COLUMNS * MOST), 1)
+    onehot = (after(target, given)[:, None] == spots).astype(jnp.bfloat16)
+    back_away, back_home = onehot[:, :split], onehot[:, split:]
+
+    def swapped(y, *earlier):
+        return lax.ppermute(after(y, *earlier) if earlier else y, "tp", SWAP)
 
     low = down(
-        [(rows, 0) for rows in beside],
+        [(after(beside[0], base_own[1]), 0)] + [(rows, 0) for rows in beside[1:]],
         [([down_own], 0, owned), ([down_pair], 0, owned), ([down_near, down_out], 0, cut)],
     )
     up_far_out = send(up_far, outward, up_near_out, low)
     rows = lift(
         [low, swapped(low)], [([up_own], 0, owned), ([up_pair], 0, owned), ([up_near, up_near_out], 0, cut)]
     )
-    lifted_home = [rows[0]] + [send(rows[d], turn[d]) for d in range(1, COLUMNS)]
+    lifted_home = [rows[0]] + [send(rows[d], turn[d]) for d in (1, 2)]
+    lifted_home.append(send(rows[3], turn[3], lifted_home[1]))
 
     low = down(
-        [(after(away[0], up_far_out, rows[0]), 0)] + [(rows, 0) for rows in away[1:]] + [(moved, d) for d in range(COLUMNS)],
+        [(after(away[0], up_far_out, lifted_home[1], lifted_home[2]), 0)]
+        + [(rows, 0) for rows in away[1:]]
+        + [(moved, d) for d in range(COLUMNS)],
         [([down_near], cut, owned - cut), ([down_far], 0, owned)],
     )
-    low = (low + swapped(low)).astype(jnp.bfloat16)
+    low_other = swapped(low)
+    base_other = swapped(given, low_other)
+    low = (low + low_other).astype(jnp.bfloat16)
     rows = lift(
         [low, send(low[low.shape[0] // 2 :], outward)],
         [([up_near, up_near_out], cut, owned - cut), ([up_far, up_far_out], 0, owned)],
     )
     lifted_away = [rows[0]] + [send(rows[d], turn[d]) for d in range(1, COLUMNS)]
-    part = finish(back_home, [after(base_own, rows[0]), base_other], lifted_home, jnp.float32)
-    return finish(back_away, [part], lifted_away, jnp.bfloat16)
+    base_own[0] = after(base_own[0], rows[0])
+    part = finish(back_home, [base_own, [base_other]], lifted_home, TILE, jnp.float32)
+    return finish(back_away, [[part]], lifted_away, 2 * TILE, jnp.bfloat16)
 
 
 def by_gather(hidden_input, query_weight, slot_down_weight, slot_up_weight, request_adapter, adapter_slot):

time: 240 us -> 214 us (0.89)
  waiting for transfers between devices: 77.1 us -> 45.7 us
  starting transfers between devices: 38.2 us -> 41.4 us
    ppermute x23, waiting for transfers between devices: 74.8 us -> 43.2 us  [send(): return lax.ppermute(after(x, *earlier) if earlier else x, 'rep', pairs)]
    pallas_call x2 -> x3, Pallas kernels: 47.4 us -> 52.2 us  [project(): pl.pallas_call(project_kernel, grid_spec=pltpu.PrefetchScalarGridSpec(num...]
    pallas_call x4 -> x3, Pallas kernels: 35.5 us -> 32.4 us  [the longest x2 19.9 us: finish(): pl.pallas_call(functools.partial(finish_kernel, starts), grid=(columns //...]
    ppermute x23, starting transfers between devices: 38.2 us -> 41.1 us  [send(): return lax.ppermute(after(x, *earlier) if earlier else x, 'rep', pairs)]
    unnamed x36 -> x38, local copies, waits for them, and re-layouts: 7.63 us -> 7.06 us
  transfers between devices with their start and end apart: 26 -> 26, of which waited for: 7 -> 11; matrix products, arithmetic and copies ran while one was open for 3% -> 3% of each run, Pallas kernels for 43% -> 46%
where the time goes in v5:
time: 214 us; the launch traced here: 213 us
  Pallas kernels  112 us (52%)
  waiting for transfers between devices  45.7 us (21%)
  starting transfers between devices  41.4 us (19%)
  local copies, waits for them, and re-layouts  10.3 us (5%)
  other arithmetic  3.21 us (2%)
    pallas_call x3, Pallas kernels, project(): pl.pallas_call(project_kernel, grid_spec=pltpu.PrefetchScalarGridSpec(num...  52.2 us
    ppermute x23, waiting for transfers between devices, send(): return lax.ppermute(after(x, *earlier) if earlier else x, 'rep', pairs)  43.2 us
    ppermute x23, starting transfers between devices, send(): return lax.ppermute(after(x, *earlier) if earlier else x, 'rep', pairs)  41.1 us
    pallas_call x2, Pallas kernels, finish(): pl.pallas_call(functools.partial(finish_kernel, starts), grid=(columns //...  19.9 us
    pallas_call x2, Pallas kernels, down(): pl.pallas_call(functools.partial(down_kernel, shape_of(groups), len(xs)),...  12.9 us
    pallas_call x1, Pallas kernels, pack(): pl.pallas_call(pack_kernel, grid=(width // tile,), in_specs=[pl.BlockSpec...  12.5 us
    pallas_call x2, Pallas kernels, lift(): pl.pallas_call(functools.partial(lift_kernel, shape_of(groups), len(ys)),...  9.89 us
    unnamed x38, local copies, waits for them, and re-layouts  7.06 us
  transfers between devices with their start and end apart: 26, of which 11 were waited for; matrix products, arithmetic and copies ran while one was open for 3% of the time, Pallas kernels for 46%

profile of v5, /device:TPU:0, one launch (start us, length us, event | category | flops | bytes accessed | tf_op | source)
XLA Modules:
  0.0 213.2 jit_solution(16502444464671863490)
XLA Ops:
  0.8 5.8 %collective-permute-start = (bf16[4,64,4096]{2,1,0:T(8,128)(2,1)}, bf16[4,64,4096]{2,1,0:T(8,128)(2,1)}, u32[]{:S(2)}, u32[]{:S(2)}) collective-permute-start(bf16[4,64,4096]{2,1,0:T(8,128)(2,1)} %bitcast.7), channel_id=1, source_target_pairs={{0,8},{2,10},{4,12},{6,14},{8,0},{10,2},{12,4},{14,6},{16,24},{18,... | collective-permute-start | bytes 6291464 | tf_op jit(solution)/shard_map/ppermute | solution.py:282
  6.6 0.8 select_reduce_fusion
  8.7 12.5 %pack_rows.1 = (bf16[96,4096]{1,0:T(8,128)(2,1)}, bf16[96,4096]{1,0:T(8,128)(2,1)}, bf16[96,4096]{1,0:T(8,128)(2,1)}, bf16[96,4096]{1,0:T(8,128)(2,1)}, bf16[160...) custom-call(s32[1,1024]{1,0:T(1,128)} %fusion.14.target_ref, ...), custom_call_target="tpu_custom_call" | custom-call | flops 8589934592 | bytes 16777216 | tf_op jit(solution)/shard_map/pack_rows/pallas_call | solution.py:45
  21.2 1.5 collective-permute-start.3
  22.7 1.5 collective-permute-start.2
  24.7 23.7 %project_half.3 = bf16[1024,2048]{1,0:T(8,128)(2,1)} custom-call(s32[1]{0:T(128)} %bitcast.1.place_ref, bf16[1024,4096]{1,0:T(8,128)(2,1)} %x_ref.4, bf16[4096,4096]{1,0:T(8,128)(2,1)} %w_ref.5), custom_call_target="tpu_custom_call" | custom-call | flops 17179869184 | bytes 29360128 | tf_op jit(solution)/shard_map/project_half/pallas_call | solution.py:67
  48.4 3.9 %collective-permute-done.refs_5_ = bf16[4,64,4096]{2,1,0:T(8,128)(2,1)} collective-permute-done((bf16[4,64,4096]{2,1,0:T(8,128)(2,1)}, bf16[4,64,4096]{2,1,0:T(8,128)(2,1)}, u32[]{:S(2)}, u32[]{:S(2)}) %collective-permute-start) | collective-permute-done | bytes 2097184 | tf_op jit(solution)/shard_map/ppermute | solution.py:282
  52.2 1.7 collective-permute-start.5
  54.7 1.6 collective-permute-start.10
  56.3 1.5 collective-permute-start.9
  57.8 1.4 collective-permute-done.4.refs_3_
  59.2 4.3 %join_rows.1 = bf16[384,4096]{1,0:T(8,128)(2,1)} custom-call(bf16[96,4096]{1,0:T(8,128)(2,1)} %get-tuple-element.65.refs_0_, bf16[96,4096]{1,0:T(8,128)(2,1)} %collective-permute-done.2.refs_1_, bf16[96,4096]{1,0:T(8,128)(2,1)} %collective-permute-done.3.refs_2_, bf16[96,4096]{1,0:T(8,128)(2,1)} %collective-permute-done.4.refs_3_), custom_call_target="tpu_custom_call" | custom-call | bytes 6291456 | tf_op jit(solution)/shard_map/join_rows/pallas_call | solution.py:240
  63.5 1.1 slice.18
  64.6 16.6 %project_half.4.rest_0_ = bf16[1024,1280]{1,0:T(8,128)(2,1)} custom-call(s32[1]{0:T(128)} %bitcast.4.place_ref, bf16[1024,4096]{1,0:T(8,128)(2,1)} %x_ref.4, bf16[4096,4096]{1,0:T(8,128)(2,1)} %w_ref.5), custom_call_target="tpu_custom_call" | custom-call | flops 10737418240 | bytes 21495808 | tf_op jit(solution)/shard_map/project_half/pallas_call | solution.py:67
  81.2 1.3 collective-permute-start.8
  82.5 1.6 collective-permute-start.7
  84.2 6.4 %collective-permute-start.17 = (bf16[384,4096]{1,0:T(8,128)(2,1)}, bf16[384,4096]{1,0:T(8,128)(2,1)S(1)}, u32[]{:S(2)}, u32[]{:S(2)}) collective-permute-start(bf16[384,4096]{1,0:T(8,128)(2,1)} %join_rows.1), channel_id=1, source_target_pairs={{0,8},{2,10},{4,12},{6,14},{24,16},{26,18},{28,20},{30,22},{1,9},{... | collective-permute-start | bytes 9437192 | tf_op jit(solution)/shard_map/ppermute | solution.py:282
  90.6 2.5 %collective-permute-start.12 = (bf16[160,4096]{1,0:T(8,128)(2,1)}, bf16[160,4096]{1,0:T(8,128)(2,1)}, u32[]{:S(2)}, u32[]{:S(2)}) collective-permute-start(bf16[160,4096]{1,0:T(8,128)(2,1)} %get-tuple-element.61), channel_id=1, source_target_pairs={{0,6},{2,4},{4,2},{6,0},{8,14},{10,12},{12,10},{14,8},{16,22},{18,... | collective-permute-start | bytes 3932168 | tf_op jit(solution)/shard_map/ppermute | solution.py:282
  93.2 12.0 %project_half.5.rest_1_ = bf16[1024,768]{1,0:T(8,128)(2,1)} custom-call(s32[1]{0:T(128)} %bitcast.4.place_ref, bf16[1024,4096]{1,0:T(8,128)(2,1)} %x_ref.4, bf16[4096,4096]{1,0:T(8,128)(2,1)} %w_ref.5), custom_call_target="tpu_custom_call" | custom-call | flops 6442450944 | bytes 16252928 | tf_op jit(solution)/shard_map/project_half/pallas_call | solution.py:67
  105.6 1.3 collective-permute-start.11
  106.9 0.8 collective-permute-start.18
  107.7 11.2 %collective-permute-done.12.refs_3_ = bf16[160,4096]{1,0:T(8,128)(2,1)} collective-permute-done((bf16[160,4096]{1,0:T(8,128)(2,1)}, bf16[160,4096]{1,0:T(8,128)(2,1)}, u32[]{:S(2)}, u32[]{:S(2)}) %collective-permute-start.12) | collective-permute-done | bytes 1310752 | tf_op jit(solution)/shard_map/ppermute | solution.py:282
  118.9 6.6 %down_rows.2.refs_0_ = f32[640,256]{1,0:T(8,128)} custom-call(bf16[160,4096]{1,0:T(8,128)(2,1)} %get-tuple-element.59.refs_0_, bf16[160,4096]{1,0:T(8,128)(2,1)} %collective-permute-done.9.refs_1_, bf16[160,4096]{1,0:T(8,128)(2,1)} %copy-done.7, bf16[160,4096]{1,0:T(8,128)(2,1)} %collective-permute-done.12.refs_3_, bf16[4,64,4096]{2,1,0:T(8,128)(2,1)} %bitcast.8, ...), custom_call_target="tpu_custom_call" | custom-call | flops 1342177280 | bytes 10485760 | tf_op jit(solution)/shard_map/down_rows/pallas_call | solution.py:142
  125.4 3.3 %collective-permute-done.11.refs_5_.refs_3_ = bf16[4,64,2048]{2,1,0:T(8,128)(2,1)S(1)} collective-permute-done((bf16[4,64,2048]{2,1,0:T(8,128)(2,1)S(1)}, bf16[4,64,2048]{2,1,0:T(8,128)(2,1)S(1)}, u32[]{:S(2)}, u32[]{:S(2)}) %collective-permute-start.11) | collective-permute-done | bytes 1048608 | tf_op jit(solution)/shard_map/ppermute | solution.py:282
  128.7 1.3 collective-permute-start.13
  130.0 0.8 copy-done.13
  130.9 5.4 %lift_rows.2 = (bf16[160,2048]{1,0:T(8,128)(2,1)}, bf16[160,2048]{1,0:T(8,128)(2,1)}, bf16[160,2048]{1,0:T(8,128)(2,1)}, bf16[160,2048]{1,0:T(8,128)(2,1)}) custom-call(f32[640,256]{1,0:T(8,128)} %down_rows.2.refs_0_, f32[640,256]{1,0:T(8,128)} %copy-done.13, bf16[4,64,2048]{2,1,0:T(8,128)(2,1)} %refs_2_.1, ...), custom_call_target="tpu_custom_call" | custom-call | flops 671088640 | bytes 5242880 | tf_op jit(solution)/shard_map/lift_rows/pallas_call | solution.py:176
  136.2 1.5 collective-permute-start.15
  137.7 1.5 collective-permute-start.16
  139.3 11.7 %collective-permute-done.15.rest_4_ = bf16[160,2048]{1,0:T(8,128)(2,1)S(1)} collective-permute-done((bf16[160,2048]{1,0:T(8,128)(2,1)}, bf16[160,2048]{1,0:T(8,128)(2,1)S(1)}, u32[]{:S(2)}, u32[]{:S(2)}) %collective-permute-start.15) | collective-permute-done | bytes 655392 | tf_op jit(solution)/shard_map/ppermute | solution.py:282
  151.0 1.2 collective-permute-done.16.rest_5_
  152.2 0.9 collective-permute-done.13.refs_5_
  153.1 1.7 collective-permute-done.17.refs_4_.refs_5_.refs_6_.refs_7_
  154.8 1.6 copy-done
  156.4 6.3 %down_rows.3 = f32[768,256]{1,0:T(8,128)} custom-call(bf16[96,4096]{1,0:T(8,128)(2,1)} %get-tuple-element.65.refs_0_, bf16[96,4096]{1,0:T(8,128)(2,1)} %collective-permute-done.2.refs_1_, bf16[96,4096]{1,0:T(8,128)(2,1)} %collective-permute-done.3.refs_2_, bf16[96,4096]{1,0:T(8,128)(2,1)} %collective-permute-done.4.refs_3_, bf16[384,4096]{1,0:T(8,128)(2,1)} %copy-done, ...), custom_call_target="tpu_custom_call" | custom-call | flops 1610612736 | bytes 9437184 | tf_op jit(solution)/shard_map/down_rows/pallas_call | solution.py:142
  162.9 2.5 %collective-permute-done.19 = f32[768,256]{1,0:T(8,128)S(1)} collective-permute-done((f32[768,256]{1,0:T(8,128)}, f32[768,256]{1,0:T(8,128)S(1)}, u32[]{:S(2)}, u32[]{:S(2)}) %collective-permute-start.19) | collective-permute-done | bytes 786464 | tf_op jit(solution)/shard_map/ppermute | solution.py:334
  165.5 2.5 %collective-permute-start.22 = (bf16[160,2048]{1,0:T(8,128)(2,1)S(1)}, bf16[160,2048]{1,0:T(8,128)(2,1)S(1)}, u32[]{:S(2)}, u32[]{:S(2)}) collective-permute-start(bf16[160,2048]{1,0:T(8,128)(2,1)S(1)} %copy-done.18), channel_id=1, source_target_pairs={{0,6},{2,4},{4,2},{6,0},{8,14},{10,12},{12,10},{14,8},{16,22},{18,... | collective-permute-start | bytes 1966088 | tf_op jit(solution)/shard_map/ppermute | solution.py:282
  168.0 1.3 add_convert_fusion.refs_0_
  169.3 1.3 collective-permute-start.20
  170.6 7.5 %collective-permute-done.20.refs_1_ = bf16[384,256]{1,0:T(8,128)(2,1)S(1)} collective-permute-done((bf16[384,256]{1,0:T(8,128)(2,1)S(1)}, bf16[384,256]{1,0:T(8,128)(2,1)S(1)}, u32[]{:S(2)}, u32[]{:S(2)}) %collective-permute-start.20) | collective-permute-done | bytes 196640 | tf_op jit(solution)/shard_map/ppermute | solution.py:282
  178.7 4.5 %lift_rows.3 = (bf16[96,2048]{1,0:T(8,128)(2,1)}, bf16[96,2048]{1,0:T(8,128)(2,1)}, bf16[96,2048]{1,0:T(8,128)(2,1)}, bf16[96,2048]{1,0:T(8,128)(2,1)}) custom-call(bf16[768,256]{1,0:T(8,128)(2,1)} %copy-done.5, bf16[384,256]{1,0:T(8,128)(2,1)} %copy-done.17, bf16[4,64,2048]{2,1,0:T(8,128)(2,1)} %copy-done.3, bf16[4,64,2048]{2,1,0:T(8,128)(2,1)} %copy-done.4, ...), custom_call_target="tpu_custom_call" | custom-call | flops 402653184 | bytes 3145728 | tf_op jit(solution)/shard_map/lift_rows/pallas_call | solution.py:176
  184.3 2.5 %collective-permute-start.25 = (bf16[96,2048]{1,0:T(8,128)(2,1)}, bf16[96,2048]{1,0:T(8,128)(2,1)S(1)}, u32[]{:S(2)}, u32[]{:S(2)}) collective-permute-start(bf16[96,2048]{1,0:T(8,128)(2,1)} %get-tuple-element.76), channel_id=1, source_target_pairs={{0,6},{2,4},{4,2},{6,0},{8,14},{10,12},{12,10},{14,8},{16,22},{18,... | collective-permute-start | bytes 1179656 | tf_op jit(solution)/shard_map/ppermute | solution.py:282
  187.2 1.2 slice.17.onehot_ref
  188.4 1.0 slice.16.onehot_ref
  189.4 0.8 copy-done.12
  190.3 1.4 copy-done.2
  191.6 12.3 %finish_rows.2.rest_0_ = f32[1024,2048]{1,0:T(8,128)} custom-call(bf16[1024,640]{1,0:T(8,128)(2,1)} %slice.17.onehot_ref, bf16[1024,1280]{1,0:T(8,128)(2,1)} %project_half.4.rest_0_, bf16[1024,768]{1,0:T(8,128)(2,1)} %project_half.5.rest_1_, bf16[1024,2048]{1,0:T(8,128)(2,1)} %copy-done.2, bf16[160,2048]{1,0:T(8,128)(2,1)} %get-tuple-element.71.rest_3_, ...), custom_call_target="tpu_custom_call" | custom-call | flops 2684354560 | bytes 16777216 | tf_op jit(solution)/shard_map/finish_rows/pallas_call | solution.py:217
  205.6 7.7 %finish_rows.3 = bf16[1024,2048]{1,0:T(8,128)(2,1)} custom-call(bf16[1024,384]{1,0:T(8,128)(2,1)} %slice.16.onehot_ref, f32[1024,2048]{1,0:T(8,128)} %finish_rows.2.rest_0_, bf16[96,2048]{1,0:T(8,128)(2,1)} %get-tuple-element.68.rest_1_, bf16[96,2048]{1,0:T(8,128)(2,1)} %copy-done.14, bf16[96,2048]{1,0:T(8,128)(2,1)} %copy-done.15, bf16[96,2048]{1,0:T(8,128)(2,1)} %copy-done.16), custom_call_target="tpu_custom_call" | custom-call | flops 1610612736 | bytes 16777216 | tf_op jit(solution)/shard_map/finish_rows/pallas_call | solution.py:217
  (64 shorter events, 7.9 us)
Async XLA Ops:
  0.0 54.0 %collective-permute-start.1 = (bf16[4,64,4096]{2,1,0:T(8,128)(2,1)}, bf16[4,64,4096]{2,1,0:T(8,128)(2,1)S(1)}, u32[]{:S(2)}, u32[]{:S(2)}) collective-permute-start(bf16[4,64,4096]{2,1,0:T(8,128)(2,1)} %bitcast.6), channel_id=1, source_target_pairs={{8,16},{10,18},{12,20},{14,22},{16,8},{18,10},{20,12},{22,14},{9,1... | collective-permute-start | bytes 6291464 | tf_op jit(solution)/shard_map/ppermute | solution.py:282
  0.8 51.4 %collective-permute-start = (bf16[4,64,4096]{2,1,0:T(8,128)(2,1)}, bf16[4,64,4096]{2,1,0:T(8,128)(2,1)}, u32[]{:S(2)}, u32[]{:S(2)}) collective-permute-start(bf16[4,64,4096]{2,1,0:T(8,128)(2,1)} %bitcast.7), channel_id=1, source_target_pairs={{0,8},{2,10},{4,12},{6,14},{8,0},{10,2},{12,4},{14,6},{16,24},{18,... | collective-permute-start | bytes 6291464 | tf_op jit(solution)/shard_map/ppermute | solution.py:282
  21.2 33.5 %collective-permute-start.3 = (bf16[96,4096]{1,0:T(8,128)(2,1)}, bf16[96,4096]{1,0:T(8,128)(2,1)}, u32[]{:S(2)}, u32[]{:S(2)}) collective-permute-start(bf16[96,4096]{1,0:T(8,128)(2,1)} %get-tuple-element.46), channel_id=1, source_target_pairs={{0,4},{2,6},{4,0},{6,2},{8,12},{10,14},{12,8},{14,10},{16,20},{18,... | collective-permute-start | bytes 2359304 | tf_op jit(solution)/shard_map/ppermute | solution.py:282
  22.7 33.6 %collective-permute-start.2 = (bf16[96,4096]{1,0:T(8,128)(2,1)}, bf16[96,4096]{1,0:T(8,128)(2,1)}, u32[]{:S(2)}, u32[]{:S(2)}) collective-permute-start(bf16[96,4096]{1,0:T(8,128)(2,1)} %get-tuple-element.45), channel_id=1, source_target_pairs={{0,2},{2,0},{4,6},{6,4},{8,10},{10,8},{12,14},{14,12},{16,18},{18,... | collective-permute-start | bytes 2359304 | tf_op jit(solution)/shard_map/ppermute | solution.py:282
  24.2 35.0 %collective-permute-start.4 = (bf16[96,4096]{1,0:T(8,128)(2,1)}, bf16[96,4096]{1,0:T(8,128)(2,1)}, u32[]{:S(2)}, u32[]{:S(2)}) collective-permute-start(bf16[96,4096]{1,0:T(8,128)(2,1)} %get-tuple-element.47), channel_id=1, source_target_pairs={{0,6},{2,4},{4,2},{6,0},{8,14},{10,12},{12,10},{14,8},{16,22},{18,... | collective-permute-start | bytes 2359304 | tf_op jit(solution)/shard_map/ppermute | solution.py:282
  24.7 27.5 %copy-start.8 = (bf16[4,64,2048]{2,1,0:T(8,128)(2,1)S(1)}, bf16[4,64,2048]{2,1,0:T(8,128)(2,1)}, u32[]{:S(2)}) copy-start(bf16[4,64,2048]{2,1,0:T(8,128)(2,1)} %refs_2_.1) | copy-start | bytes 3145732
  52.2 29.0 %collective-permute-start.5 = (bf16[4,64,2048]{2,1,0:T(8,128)(2,1)S(1)}, bf16[4,64,2048]{2,1,0:T(8,128)(2,1)}, u32[]{:S(2)}, u32[]{:S(2)}) collective-permute-start(bf16[4,64,2048]{2,1,0:T(8,128)(2,1)S(1)} %copy-done.8), channel_id=1, source_target_pairs={{0,8},{2,10},{4,12},{6,14},{8,0},{10,2},{12,4},{14,6},{16,24},{18,... | collective-permute-start | bytes 3145736 | tf_op jit(solution)/shard_map/ppermute | solution.py:282
  54.0 9.6 %copy-start.1 = (bf16[4,64,4096]{2,1,0:T(8,128)(2,1)}, bf16[4,64,4096]{2,1,0:T(8,128)(2,1)S(1)}, u32[]{:S(2)}) copy-start(bf16[4,64,4096]{2,1,0:T(8,128)(2,1)S(1)} %collective-permute-done.1.refs_6_.refs_8_) | copy-start | bytes 6291460
  54.0 28.5 %collective-permute-start.6 = (bf16[4,64,2048]{2,1,0:T(8,128)(2,1)S(1)}, bf16[4,64,2048]{2,1,0:T(8,128)(2,1)S(1)}, u32[]{:S(2)}, u32[]{:S(2)}) collective-permute-start(bf16[4,64,2048]{2,1,0:T(8,128)(2,1)S(1)} %copy-done.8), channel_id=1, source_target_pairs={{8,16},{10,18},{12,20},{14,22},{16,8},{18,10},{20,12},{22,14},{9,1... | collective-permute-start | bytes 3145736 | tf_op jit(solution)/shard_map/ppermute | solution.py:282
  54.7 35.9 %collective-permute-start.10 = (bf16[160,4096]{1,0:T(8,128)(2,1)}, bf16[160,4096]{1,0:T(8,128)(2,1)S(1)}, u32[]{:S(2)}, u32[]{:S(2)}) collective-permute-start(bf16[160,4096]{1,0:T(8,128)(2,1)} %get-tuple-element.56), channel_id=1, source_target_pairs={{0,4},{2,6},{4,0},{6,2},{8,12},{10,14},{12,8},{14,10},{16,20},{18,... | collective-permute-start | bytes 3932168 | tf_op jit(solution)/shard_map/ppermute | solution.py:282
  56.3 34.3 %collective-permute-start.9 = (bf16[160,4096]{1,0:T(8,128)(2,1)}, bf16[160,4096]{1,0:T(8,128)(2,1)}, u32[]{:S(2)}, u32[]{:S(2)}) collective-permute-start(bf16[160,4096]{1,0:T(8,128)(2,1)} %get-tuple-element.54), channel_id=1, source_target_pairs={{0,2},{2,0},{4,6},{6,4},{8,10},{10,8},{12,14},{14,12},{16,18},{18,... | collective-permute-start | bytes 3932168 | tf_op jit(solution)/shard_map/ppermute | solution.py:282
  81.2 24.4 %collective-permute-start.8 = (bf16[2,64,4096]{2,1,0:T(8,128)(2,1)}, bf16[2,64,4096]{2,1,0:T(8,128)(2,1)}, u32[]{:S(2)}, u32[]{:S(2)}) collective-permute-start(bf16[2,64,4096]{2,1,0:T(8,128)(2,1)} %slice.18), channel_id=1, source_target_pairs={{8,0},{10,2},{12,4},{14,6},{16,24},{18,26},{20,28},{22,30},{9,1},{... | collective-permute-start | bytes 3145736 | tf_op jit(solution)/shard_map/ppermute | solution.py:282
  82.5 23.1 %copy-start.3 = (bf16[4,64,2048]{2,1,0:T(8,128)(2,1)}, bf16[4,64,2048]{2,1,0:T(8,128)(2,1)S(1)}, u32[]{:S(2)}) copy-start(bf16[4,64,2048]{2,1,0:T(8,128)(2,1)S(1)} %collective-permute-done.6.refs_4_.refs_2_) | copy-start | bytes 3145732
  82.5 24.4 %collective-permute-start.7 = (bf16[4,64,2048]{2,1,0:T(8,128)(2,1)}, bf16[4,64,2048]{2,1,0:T(8,128)(2,1)}, u32[]{:S(2)}, u32[]{:S(2)}) collective-permute-start(bf16[4,64,2048]{2,1,0:T(8,128)(2,1)} %collective-permute-done.5.refs_3_), channel_id=1, source_target_pairs={{8,16},{10,18},{12,20},{14,22},{16,8},{18,10},{20,12},{22,14},{9,1... | collective-permute-start | bytes 3145736 | tf_op jit(solution)/shard_map/ppermute | solution.py:282
  84.2 70.6 %collective-permute-start.17 = (bf16[384,4096]{1,0:T(8,128)(2,1)}, bf16[384,4096]{1,0:T(8,128)(2,1)S(1)}, u32[]{:S(2)}, u32[]{:S(2)}) collective-permute-start(bf16[384,4096]{1,0:T(8,128)(2,1)} %join_rows.1), channel_id=1, source_target_pairs={{0,8},{2,10},{4,12},{6,14},{24,16},{26,18},{28,20},{30,22},{1,9},{... | collective-permute-start | bytes 9437192 | tf_op jit(solution)/shard_map/ppermute | solution.py:282
  90.6 14.5 %copy-start.7 = (bf16[160,4096]{1,0:T(8,128)(2,1)}, bf16[160,4096]{1,0:T(8,128)(2,1)S(1)}, u32[]{:S(2)}) copy-start(bf16[160,4096]{1,0:T(8,128)(2,1)S(1)} %collective-permute-done.10.refs_2_) | copy-start | bytes 3932164
  90.6 28.2 %collective-permute-start.12 = (bf16[160,4096]{1,0:T(8,128)(2,1)}, bf16[160,4096]{1,0:T(8,128)(2,1)}, u32[]{:S(2)}, u32[]{:S(2)}) collective-permute-start(bf16[160,4096]{1,0:T(8,128)(2,1)} %get-tuple-element.61), channel_id=1, source_target_pairs={{0,6},{2,4},{4,2},{6,0},{8,14},{10,12},{12,10},{14,8},{16,22},{18,... | collective-permute-start | bytes 3932168 | tf_op jit(solution)/shard_map/ppermute | solution.py:282
  105.6 23.1 %collective-permute-start.11 = (bf16[4,64,2048]{2,1,0:T(8,128)(2,1)S(1)}, bf16[4,64,2048]{2,1,0:T(8,128)(2,1)S(1)}, u32[]{:S(2)}, u32[]{:S(2)}) collective-permute-start(bf16[4,64,2048]{2,1,0:T(8,128)(2,1)S(1)} %collective-permute-done.6.refs_4_.refs_2_), channel_id=1, source_target_pairs={{8,0},{10,2},{12,4},{14,6},{16,24},{18,26},{20,28},{22,30},{9,1},{... | collective-permute-start | bytes 3145736 | tf_op jit(solution)/shard_map/ppermute | solution.py:282
  106.9 46.2 %collective-permute-start.18 = (bf16[4,64,4096]{2,1,0:T(8,128)(2,1)}, bf16[4,64,4096]{2,1,0:T(8,128)(2,1)S(1)}, u32[]{:S(2)}, u32[]{:S(2)}) collective-permute-start(bf16[4,64,4096]{2,1,0:T(8,128)(2,1)} %collective-permute-done.refs_5_), channel_id=1, source_target_pairs={{8,16},{10,18},{12,20},{14,22},{16,8},{18,10},{20,12},{22,14},{9,1... | collective-permute-start | bytes 6291464 | tf_op jit(solution)/shard_map/ppermute | solution.py:282
  125.4 4.6 %collective-permute-start.14 = (f32[640,256]{1,0:T(8,128)}, f32[640,256]{1,0:T(8,128)S(1)}, u32[]{:S(2)}, u32[]{:S(2)}) collective-permute-start(f32[640,256]{1,0:T(8,128)} %down_rows.2.refs_0_), channel_id=1, source_target_pairs={{0,1},{1,0},{2,3},{3,2},{4,5},{5,4},{6,7},{7,6},{8,9},{9,8},{10,11... | collective-permute-start | bytes 1966088 | tf_op jit(solution)/shard_map/ppermute | solution.py:334
  128.7 1.3 copy-start.4
  128.7 24.4 %collective-permute-start.13 = (bf16[4,64,2048]{2,1,0:T(8,128)(2,1)}, bf16[4,64,2048]{2,1,0:T(8,128)(2,1)S(1)}, u32[]{:S(2)}, u32[]{:S(2)}) collective-permute-start(bf16[4,64,2048]{2,1,0:T(8,128)(2,1)} %collective-permute-done.7.refs_4_), channel_id=1, source_target_pairs={{8,0},{10,2},{12,4},{14,6},{16,24},{18,26},{20,28},{22,30},{9,1},{... | collective-permute-start | bytes 3145736 | tf_op jit(solution)/shard_map/ppermute | solution.py:282
  130.0 0.8 copy-start.13
  136.2 14.7 %collective-permute-start.15 = (bf16[160,2048]{1,0:T(8,128)(2,1)}, bf16[160,2048]{1,0:T(8,128)(2,1)S(1)}, u32[]{:S(2)}, u32[]{:S(2)}) collective-permute-start(bf16[160,2048]{1,0:T(8,128)(2,1)} %get-tuple-element.63), channel_id=1, source_target_pairs={{0,2},{2,0},{4,6},{6,4},{8,10},{10,8},{12,14},{14,12},{16,18},{18,... | collective-permute-start | bytes 1966088 | tf_op jit(solution)/shard_map/ppermute | solution.py:282
  137.7 27.7 %copy-start.18 = (bf16[160,2048]{1,0:T(8,128)(2,1)S(1)}, bf16[160,2048]{1,0:T(8,128)(2,1)}, u32[]{:S(2)}) copy-start(bf16[160,2048]{1,0:T(8,128)(2,1)} %get-tuple-element.73) | copy-start | bytes 1966084
  137.7 14.4 %collective-permute-start.16 = (bf16[160,2048]{1,0:T(8,128)(2,1)}, bf16[160,2048]{1,0:T(8,128)(2,1)S(1)}, u32[]{:S(2)}, u32[]{:S(2)}) collective-permute-start(bf16[160,2048]{1,0:T(8,128)(2,1)} %get-tuple-element.64), channel_id=1, source_target_pairs={{0,4},{2,6},{4,0},{6,2},{8,12},{10,14},{12,8},{14,10},{16,20},{18,... | collective-permute-start | bytes 1966088 | tf_op jit(solution)/shard_map/ppermute | solution.py:282
  151.0 11.8 %copy-start.10 = (bf16[160,2048]{1,0:T(8,128)(2,1)}, bf16[160,2048]{1,0:T(8,128)(2,1)S(1)}, u32[]{:S(2)}) copy-start(bf16[160,2048]{1,0:T(8,128)(2,1)S(1)} %collective-permute-done.15.rest_4_) | copy-start | bytes 1966084
  152.2 10.6 %copy-start.11 = (bf16[160,2048]{1,0:T(8,128)(2,1)}, bf16[160,2048]{1,0:T(8,128)(2,1)S(1)}, u32[]{:S(2)}) copy-start(bf16[160,2048]{1,0:T(8,128)(2,1)S(1)} %collective-permute-done.16.rest_5_) | copy-start | bytes 1966084
  153.1 9.7 %copy-start.9 = (bf16[4,64,2048]{2,1,0:T(8,128)(2,1)}, bf16[4,64,2048]{2,1,0:T(8,128)(2,1)S(1)}, u32[]{:S(2)}) copy-start(bf16[4,64,2048]{2,1,0:T(8,128)(2,1)S(1)} %collective-permute-done.13.refs_5_) | copy-start | bytes 3145732
  153.1 1.7 copy-start.6
  154.8 1.6 copy-start
  162.8 2.6 %collective-permute-start.19 = (f32[768,256]{1,0:T(8,128)}, f32[768,256]{1,0:T(8,128)S(1)}, u32[]{:S(2)}, u32[]{:S(2)}) collective-permute-start(f32[768,256]{1,0:T(8,128)} %down_rows.3), channel_id=1, source_target_pairs={{0,1},{1,0},{2,3},{3,2},{4,5},{5,4},{6,7},{7,6},{8,9},{9,8},{10,11... | collective-permute-start | bytes 2359304 | tf_op jit(solution)/shard_map/ppermute | solution.py:334
  165.3 24.1 %collective-permute-start.21 = (bf16[1024,2048]{1,0:T(8,128)(2,1)}, bf16[1024,2048]{1,0:T(8,128)(2,1)S(1)}, u32[]{:S(2)}, u32[]{:S(2)}) collective-permute-start(bf16[1024,2048]{1,0:T(8,128)(2,1)} %project_half.3), channel_id=1, source_target_pairs={{0,1},{1,0},{2,3},{3,2},{4,5},{5,4},{6,7},{7,6},{8,9},{9,8},{10,11... | collective-permute-start | bytes 12582920 | tf_op jit(solution)/shard_map/ppermute | solution.py:334
  165.5 23.9 %collective-permute-start.22 = (bf16[160,2048]{1,0:T(8,128)(2,1)S(1)}, bf16[160,2048]{1,0:T(8,128)(2,1)S(1)}, u32[]{:S(2)}, u32[]{:S(2)}) collective-permute-start(bf16[160,2048]{1,0:T(8,128)(2,1)S(1)} %copy-done.18), channel_id=1, source_target_pairs={{0,6},{2,4},{4,2},{6,0},{8,14},{10,12},{12,10},{14,8},{16,22},{18,... | collective-permute-start | bytes 1966088 | tf_op jit(solution)/shard_map/ppermute | solution.py:282
  169.2 8.8 %copy-start.5 = (bf16[768,256]{1,0:T(8,128)(2,1)}, bf16[768,256]{1,0:T(8,128)(2,1)S(1)}, u32[]{:S(2)}) copy-start(bf16[768,256]{1,0:T(8,128)(2,1)S(1)} %add_convert_fusion.refs_0_) | copy-start | bytes 1179652
  169.3 8.8 %collective-permute-start.20 = (bf16[384,256]{1,0:T(8,128)(2,1)S(1)}, bf16[384,256]{1,0:T(8,128)(2,1)S(1)}, u32[]{:S(2)}, u32[]{:S(2)}) collective-permute-start(bf16[384,256]{1,0:T(8,128)(2,1)S(1)} %slice.19), channel_id=1, source_target_pairs={{8,0},{10,2},{12,4},{14,6},{16,24},{18,26},{20,28},{22,30},{9,1},{... | collective-permute-start | bytes 589832 | tf_op jit(solution)/shard_map/ppermute | solution.py:282
  178.1 0.7 copy-start.17
  183.3 20.6 %collective-permute-start.23 = (bf16[96,2048]{1,0:T(8,128)(2,1)}, bf16[96,2048]{1,0:T(8,128)(2,1)S(1)}, u32[]{:S(2)}, u32[]{:S(2)}) collective-permute-start(bf16[96,2048]{1,0:T(8,128)(2,1)} %get-tuple-element.74), channel_id=1, source_target_pairs={{0,2},{2,0},{4,6},{6,4},{8,10},{10,8},{12,14},{14,12},{16,18},{18,... | collective-permute-start | bytes 1179656 | tf_op jit(solution)/shard_map/ppermute | solution.py:282
  183.8 20.1 %collective-permute-start.24 = (bf16[96,2048]{1,0:T(8,128)(2,1)}, bf16[96,2048]{1,0:T(8,128)(2,1)S(1)}, u32[]{:S(2)}, u32[]{:S(2)}) collective-permute-start(bf16[96,2048]{1,0:T(8,128)(2,1)} %get-tuple-element.75), channel_id=1, source_target_pairs={{0,4},{2,6},{4,0},{6,2},{8,12},{10,14},{12,8},{14,10},{16,20},{18,... | collective-permute-start | bytes 1179656 | tf_op jit(solution)/shard_map/ppermute | solution.py:282
  184.3 19.6 %collective-permute-start.25 = (bf16[96,2048]{1,0:T(8,128)(2,1)}, bf16[96,2048]{1,0:T(8,128)(2,1)S(1)}, u32[]{:S(2)}, u32[]{:S(2)}) collective-permute-start(bf16[96,2048]{1,0:T(8,128)(2,1)} %get-tuple-element.76), channel_id=1, source_target_pairs={{0,6},{2,4},{4,2},{6,0},{8,14},{10,12},{12,10},{14,8},{16,22},{18,... | collective-permute-start | bytes 1179656 | tf_op jit(solution)/shard_map/ppermute | solution.py:282
  189.4 0.9 copy-start.12
  189.4 2.2 %copy-start.2 = (bf16[1024,2048]{1,0:T(8,128)(2,1)}, bf16[1024,2048]{1,0:T(8,128)(2,1)S(1)}, u32[]{:S(2)}) copy-start(bf16[1024,2048]{1,0:T(8,128)(2,1)S(1)} %collective-permute-done.21.rest_2_) | copy-start | bytes 12582916
  203.9 0.8 copy-start.14
  203.9 0.9 copy-start.15
  204.8 0.8 copy-start.16

commit v6 on v5

--- a/solution.py
+++ b/solution.py
@@ -11,7 +11,7 @@
 COLUMNS = 4
 PLANES = 4
 SWAP = [(0, 1), (1, 0)]
-LIMIT = 56 * 1024 * 1024
+LIMIT = 63 * 1024 * 1024
 NT = (((1,), (1,)), ((), ()))
 TILE = 256
 
@@ -55,31 +55,52 @@
     )(target, x)
 
 
-def project_kernel(place_ref, x_ref, w_ref, o_ref):
-    o_ref[...] = jnp.dot(x_ref[...], w_ref[...], preferred_element_type=jnp.float32).astype(o_ref.dtype)
-
-
-def project(half, x, w, first, count):
+def project_kernel(counts, place_ref, x_ref, w_ref, *outs):
+    step, at = pl.program_id(0), 0
+    product = jnp.dot(x_ref[...], w_ref[...], preferred_element_type=jnp.float32).astype(jnp.bfloat16)
+    for out, count in zip(outs, counts):
+
+        @pl.when((step >= at) & (step < at + count))
+        def _():
+            out[...] = product
+
+        at += count
+
+
+def project(tp, x, w, parts):
     rows, width = x.shape
     tile = TILE
     steps = w.shape[1] // 2 // tile
-    columns = count * tile
-    return pl.pallas_call(
-        project_kernel,
+    counts = [count for _, _, count in parts]
+    firsts = jnp.stack([(1 - tp if given else tp) * steps + first for given, first, _ in parts])
+    columns = sum(counts) * tile
+
+    def w_tile(i, place):
+        at, found = 0, place[0] + i
+        for k, count in enumerate(counts):
+            found = jnp.where(i >= at, place[k] + i - at, found)
+            at += count
+        return 0, found
+
+    def out_spec(at, count):
+        return pl.BlockSpec((rows, tile), lambda i, place: (0, jnp.clip(i - at, 0, count - 1)))
+
+    return pl.pallas_call(
+        functools.partial(project_kernel, counts),
         grid_spec=pltpu.PrefetchScalarGridSpec(
             num_scalar_prefetch=1,
-            grid=(count,),
+            grid=(sum(counts),),
             in_specs=[
                 pl.BlockSpec((rows, width), lambda i, place: (0, 0)),
-                pl.BlockSpec((width, tile), lambda i, place: (0, place[0] * steps + first + i)),
+                pl.BlockSpec((width, tile), w_tile),
             ],
-            out_specs=pl.BlockSpec((rows, tile), lambda i, place: (0, i)),
+            out_specs=[out_spec(sum(counts[:k]), count) for k, count in enumerate(counts)],
         ),
-        out_shape=jax.ShapeDtypeStruct((rows, columns), jnp.bfloat16),
+        out_shape=[jax.ShapeDtypeStruct((rows, count * tile), jnp.bfloat16) for count in counts],
         compiler_params=params(),
         cost_estimate=cost(2 * rows * width * columns, 2 * (rows * width + columns * width + rows * columns)),
         name="project_half",
-    )(half.reshape(1), x, w)
+    )(firsts, x, w)
 
 
 def factor_specs(groups, rank, tile):
@@ -302,28 +323,30 @@
     up_own = slot_up_weight
     tp = lax.axis_index("tp")
     tiles = query_weight.shape[1] // 2 // TILE
-    early = tiles * 5 // 8
+    first, second = tiles // 4, tiles * 5 // 8
     down_pair = send(down_own, pair)
     down_near = send(down_own, across)
 
     packed = pack(target[None, :], hidden_input, [rest * MOST] * COLUMNS + [served * MOST] * COLUMNS)
     away, home = packed[:COLUMNS], packed[COLUMNS:]
     away = [away[0]] + [send(away[d], turn[d]) for d in range(1, COLUMNS)]
-    given = project(1 - tp, after(hidden_input, home[0]), query_weight, 0, tiles)
+    given, own = project(tp, after(hidden_input, home[0]), query_weight, [(True, 0, tiles), (False, 0, first)])
+    base_own = [own]
 
     up_pair = send(up_own, pair, down_pair, given)
     up_near = send(up_own, across, down_near, given)
     beside = [home[0]] + [send(home[d], turn[d], away[d], given) for d in (1, 2)]
     moving = join(away)
-    base_own = [project(tp, after(hidden_input, down_pair, down_near, moving), query_weight, 0, early)]
-
-    moved = send(moving, inward, up_pair, base_own[0])
-    down_out = send(down_near[:cut], outward, up_pair, base_own[0])
-    up_far = send(up_pair, across, up_near, base_own[0])
-    beside.append(send(home[3], turn[3], beside[1], beside[2], base_own[0]))
-    base_own.append(project(tp, after(hidden_input, beside[1], beside[2], up_near), query_weight, early, tiles - early))
+    base_own += project(tp, after(hidden_input, down_pair, down_near, moving), query_weight, [(False, first, second - first)])
+
+    moved = send(moving, inward, up_pair, base_own[1])
+    down_out = send(down_near[:cut], outward, up_pair, base_own[1])
+    up_far = send(up_pair, across, up_near, base_own[1])
+    beside.append(send(home[3], turn[3], beside[1], beside[2], base_own[1]))
+    late = after(hidden_input, beside[1], beside[2], up_near)
+    base_own += project(tp, late, query_weight, [(False, second, tiles - second)])
     down_far = send(down_pair, across, up_far, down_out)
-    up_near_out = send(up_near, outward, down_out, base_own[1])
+    up_near_out = send(up_near, outward, down_out, base_own[2])
 
     split = COLUMNS * rest * MOST
     spots = lax.broadcasted_iota(jnp.int32, (target.shape[0], 4 * owned * COLUMNS * MOST), 1)
@@ -334,7 +357,7 @@
         return lax.ppermute(after(y, *earlier) if earlier else y, "tp", SWAP)
 
     low = down(
-        [(after(beside[0], base_own[1]), 0)] + [(rows, 0) for rows in beside[1:]],
+        [(after(beside[0], base_own[2]), 0)] + [(rows, 0) for rows in beside[1:]],
         [([down_own], 0, owned), ([down_pair], 0, owned), ([down_near, down_out], 0, cut)],
     )
     up_far_out = send(up_far, outward, up_near_out, low)

time: 214 us -> 209 us (0.977)
  waiting for transfers between devices: 45.7 us -> 42 us
  local copies, waits for them, and re-layouts: 10.3 us -> 6.78 us
    unnamed x38 -> x12, local copies, waits for them, and re-layouts: 7.06 us -> 2.29 us
    ppermute x23, waiting for transfers between devices: 43.2 us -> 39.5 us  [send(): return lax.ppermute(after(x, *earlier) if earlier else x, 'rep', pairs)]
  transfers between devices with their start and end apart: 26 -> 26, of which waited for: 11 -> 10; matrix products, arithmetic and copies ran while one was open for 3% -> 4% of each run, Pallas kernels for 46% -> 48%
where the time goes in v6:
time: 209 us; the launch traced here: 208 us
  Pallas kernels  113 us (54%)
  waiting for transfers between devices  42 us (20%)
  starting transfers between devices  41.6 us (20%)
  local copies, waits for them, and re-layouts  6.78 us (3%)
  other arithmetic  3.74 us (2%)
    pallas_call x3, Pallas kernels, project(): pl.pallas_call(functools.partial(project_kernel, counts), grid_spec=pltpu...  54.1 us
    ppermute x23, starting transfers between devices, send(): return lax.ppermute(after(x, *earlier) if earlier else x, 'rep', pairs)  41.5 us
    ppermute x23, waiting for transfers between devices, send(): return lax.ppermute(after(x, *earlier) if earlier else x, 'rep', pairs)  39.5 us
    pallas_call x2, Pallas kernels, finish(): pl.pallas_call(functools.partial(finish_kernel, starts), grid=(columns //...  19.2 us
    pallas_call x2, Pallas kernels, down(): pl.pallas_call(functools.partial(down_kernel, shape_of(groups), len(xs)),...  12.9 us
    pallas_call x1, Pallas kernels, pack(): pl.pallas_call(pack_kernel, grid=(width // tile,), in_specs=[pl.BlockSpec...  12.5 us
    pallas_call x2, Pallas kernels, lift(): pl.pallas_call(functools.partial(lift_kernel, shape_of(groups), len(ys)),...  9.82 us
    pallas_call x1, Pallas kernels, join(): pl.pallas_call(join_kernel, grid=(width // tile,), in_specs=[pl.BlockSpec...  4.39 us
  transfers between devices with their start and end apart: 26, of which 10 were waited for; matrix products, arithmetic and copies ran while one was open for 4% of the time, Pallas kernels for 48%

profile of v6, /device:TPU:0, one launch (start us, length us, event | category | flops | bytes accessed | tf_op | source)
XLA Modules:
  0.0 207.9 jit_solution(13545768981904311347)
XLA Ops:
  0.0 2.1 collective-permute-start.2
  2.1 4.5 %collective-permute-start = (bf16[4,64,4096]{2,1,0:T(8,128)(2,1)}, bf16[4,64,4096]{2,1,0:T(8,128)(2,1)}, u32[]{:S(2)}, u32[]{:S(2)}) collective-permute-start(bf16[4,64,4096]{2,1,0:T(8,128)(2,1)} %bitcast.9), channel_id=1, source_target_pairs={{0,8},{2,10},{4,12},{6,14},{8,0},{10,2},{12,4},{14,6},{16,24},{18,... | collective-permute-start | bytes 6291464 | tf_op jit(solution)/shard_map/ppermute | solution.py:303
  6.6 0.8 select_reduce_fusion
  8.0 0.7 fusion.14.target_ref
  8.7 12.5 %pack_rows.1 = (bf16[96,4096]{1,0:T(8,128)(2,1)}, bf16[96,4096]{1,0:T(8,128)(2,1)}, bf16[96,4096]{1,0:T(8,128)(2,1)}, bf16[96,4096]{1,0:T(8,128)(2,1)}, bf16[160...) custom-call(s32[1,1024]{1,0:T(1,128)} %fusion.14.target_ref, ...), custom_call_target="tpu_custom_call" | custom-call | flops 8589934592 | bytes 16777216 | tf_op jit(solution)/shard_map/pack_rows/pallas_call | solution.py:45
  21.2 1.5 collective-permute-start.5
  22.8 1.5 collective-permute-start.4
  25.3 30.0 %project_half.3 = (bf16[1024,2048]{1,0:T(8,128)(2,1)}, bf16[1024,512]{1,0:T(8,128)(2,1)}) custom-call(s32[2]{0:T(128)} %pad_add_fusion.place_ref, bf16[1024,4096]{1,0:T(8,128)(2,1)} %x_ref.4, bf16[4096,4096]{1,0:T(8,128)(2,1)} %w_ref.5), custom_call_target="tpu_custom_call" | custom-call | flops 21474836480 | bytes 34603008 | tf_op jit(solution)/shard_map/project_half/pallas_call | solution.py:88
  55.4 1.6 collective-permute-start.3
  57.0 1.5 collective-permute-start.10
  58.5 1.5 collective-permute-start.9
  60.0 4.4 %join_rows.1 = bf16[384,4096]{1,0:T(8,128)(2,1)} custom-call(bf16[96,4096]{1,0:T(8,128)(2,1)} %get-tuple-element.69.refs_0_, bf16[96,4096]{1,0:T(8,128)(2,1)} %collective-permute-done.4.refs_1_, bf16[96,4096]{1,0:T(8,128)(2,1)} %copy-done, bf16[96,4096]{1,0:T(8,128)(2,1)} %collective-permute-done.6.refs_3_), custom_call_target="tpu_custom_call" | custom-call | bytes 6291456 | tf_op jit(solution)/shard_map/join_rows/pallas_call | solution.py:261
  64.4 2.3 %slice.18 = bf16[2,64,4096]{2,1,0:T(8,128)(2,1)} slice(bf16[4,64,4096]{2,1,0:T(8,128)(2,1)} %collective-permute-done.2.refs_6_.refs_8_), slice={[0:2], [0:64], [0:4096]} | slice | bytes 2097152 | tf_op jit(solution)/shard_map/slice | solution.py:343
  66.7 12.0 %project_half.4.rest_1_ = bf16[1024,768]{1,0:T(8,128)(2,1)} custom-call(s32[1]{0:T(128)} %bitcast.6.place_ref, bf16[1024,4096]{1,0:T(8,128)(2,1)} %x_ref.4, bf16[4096,4096]{1,0:T(8,128)(2,1)} %w_ref.5), custom_call_target="tpu_custom_call" | custom-call | flops 6442450944 | bytes 16252928 | tf_op jit(solution)/shard_map/project_half/pallas_call | solution.py:88
  79.1 1.3 collective-permute-start.8
  80.4 1.7 collective-permute-start.7
  82.1 8.7 %collective-permute-start.17 = (bf16[384,4096]{1,0:T(8,128)(2,1)}, bf16[384,4096]{1,0:T(8,128)(2,1)}, u32[]{:S(2)}, u32[]{:S(2)}) collective-permute-start(bf16[384,4096]{1,0:T(8,128)(2,1)} %join_rows.1), channel_id=1, source_target_pairs={{0,8},{2,10},{4,12},{6,14},{24,16},{26,18},{28,20},{30,22},{1,9},{... | collective-permute-start | bytes 9437192 | tf_op jit(solution)/shard_map/ppermute | solution.py:303
  90.8 1.6 collective-permute-start.12
  92.4 12.0 %project_half.5.rest_2_ = bf16[1024,768]{1,0:T(8,128)(2,1)} custom-call(s32[1]{0:T(128)} %bitcast.7.place_ref, bf16[1024,4096]{1,0:T(8,128)(2,1)} %x_ref.4, bf16[4096,4096]{1,0:T(8,128)(2,1)} %w_ref.5), custom_call_target="tpu_custom_call" | custom-call | flops 6442450944 | bytes 16252928 | tf_op jit(solution)/shard_map/project_half/pallas_call | solution.py:88
  104.4 1.3 collective-permute-start.11
  105.7 2.0 collective-permute-start.18
  107.8 11.9 %collective-permute-done.12.refs_3_ = bf16[160,4096]{1,0:T(8,128)(2,1)} collective-permute-done((bf16[160,4096]{1,0:T(8,128)(2,1)}, bf16[160,4096]{1,0:T(8,128)(2,1)}, u32[]{:S(2)}, u32[]{:S(2)}) %collective-permute-start.12) | collective-permute-done | bytes 1310752 | tf_op jit(solution)/shard_map/ppermute | solution.py:303
  119.7 6.6 %down_rows.2.refs_0_ = f32[640,256]{1,0:T(8,128)} custom-call(bf16[160,4096]{1,0:T(8,128)(2,1)} %get-tuple-element.63.refs_0_, bf16[160,4096]{1,0:T(8,128)(2,1)} %collective-permute-done.9.refs_1_, bf16[160,4096]{1,0:T(8,128)(2,1)} %collective-permute-done.10.refs_2_, bf16[160,4096]{1,0:T(8,128)(2,1)} %collective-permute-done.12.refs_3_, ...), custom_call_target="tpu_custom_call" | custom-call | flops 1342177280 | bytes 10485760 | tf_op jit(solution)/shard_map/down_rows/pallas_call | solution.py:163
  126.2 1.9 collective-permute-done.11.refs_5_.refs_3_
  128.1 1.3 collective-permute-start.13
  129.4 0.8 copy-done.2
  130.2 5.3 %lift_rows.2 = (bf16[160,2048]{1,0:T(8,128)(2,1)}, bf16[160,2048]{1,0:T(8,128)(2,1)}, bf16[160,2048]{1,0:T(8,128)(2,1)}, bf16[160,2048]{1,0:T(8,128)(2,1)}) custom-call(f32[640,256]{1,0:T(8,128)} %down_rows.2.refs_0_, f32[640,256]{1,0:T(8,128)} %copy-done.2, bf16[4,64,2048]{2,1,0:T(8,128)(2,1)} %refs_2_.1, ...), custom_call_target="tpu_custom_call" | custom-call | flops 671088640 | bytes 5242880 | tf_op jit(solution)/shard_map/lift_rows/pallas_call | solution.py:197
  135.6 1.2 collective-permute-start.15
  136.8 1.5 collective-permute-start.16
  138.3 13.5 %collective-permute-done.15.rest_5_ = bf16[160,2048]{1,0:T(8,128)(2,1)} collective-permute-done((bf16[160,2048]{1,0:T(8,128)(2,1)}, bf16[160,2048]{1,0:T(8,128)(2,1)}, u32[]{:S(2)}, u32[]{:S(2)}) %collective-permute-start.15) | collective-permute-done | bytes 655392 | tf_op jit(solution)/shard_map/ppermute | solution.py:303
  152.1 1.9 collective-permute-done.13.refs_5_
  154.2 6.4 %down_rows.3 = f32[768,256]{1,0:T(8,128)} custom-call(bf16[96,4096]{1,0:T(8,128)(2,1)} %get-tuple-element.69.refs_0_, bf16[96,4096]{1,0:T(8,128)(2,1)} %collective-permute-done.4.refs_1_, bf16[96,4096]{1,0:T(8,128)(2,1)} %copy-done, bf16[96,4096]{1,0:T(8,128)(2,1)} %collective-permute-done.6.refs_3_, ...), custom_call_target="tpu_custom_call" | custom-call | flops 1610612736 | bytes 9437184 | tf_op jit(solution)/shard_map/down_rows/pallas_call | solution.py:163
  160.6 2.5 %collective-permute-done.19 = f32[768,256]{1,0:T(8,128)S(1)} collective-permute-done((f32[768,256]{1,0:T(8,128)}, f32[768,256]{1,0:T(8,128)S(1)}, u32[]{:S(2)}, u32[]{:S(2)}) %collective-permute-start.19) | collective-permute-done | bytes 786464 | tf_op jit(solution)/shard_map/ppermute | solution.py:357
  163.2 1.3 collective-permute-start.22
  164.5 1.2 add_convert_fusion.refs_0_
  165.8 1.3 collective-permute-start.20
  167.1 7.6 %collective-permute-done.20.refs_1_ = bf16[384,256]{1,0:T(8,128)(2,1)S(1)} collective-permute-done((bf16[384,256]{1,0:T(8,128)(2,1)S(1)}, bf16[384,256]{1,0:T(8,128)(2,1)S(1)}, u32[]{:S(2)}, u32[]{:S(2)}) %collective-permute-start.20) | collective-permute-done | bytes 196640 | tf_op jit(solution)/shard_map/ppermute | solution.py:303
  174.7 0.7 copy-done.5
  175.4 4.5 %lift_rows.3 = (bf16[96,2048]{1,0:T(8,128)(2,1)}, bf16[96,2048]{1,0:T(8,128)(2,1)}, bf16[96,2048]{1,0:T(8,128)(2,1)}, bf16[96,2048]{1,0:T(8,128)(2,1)}) custom-call(bf16[768,256]{1,0:T(8,128)(2,1)} %copy-done.1, bf16[384,256]{1,0:T(8,128)(2,1)} %copy-done.5, bf16[4,64,2048]{2,1,0:T(8,128)(2,1)} %collective-permute-done.3.refs_4_.refs_2_, ...), custom_call_target="tpu_custom_call" | custom-call | flops 402653184 | bytes 3145728 | tf_op jit(solution)/shard_map/lift_rows/pallas_call | solution.py:197
  179.9 0.7 collective-permute-start.23
  180.6 1.5 collective-permute-start.24
  182.1 1.3 collective-permute-start.25
  183.8 1.2 slice.17.onehot_ref
  185.0 1.0 slice.16.onehot_ref
  186.0 11.5 %finish_rows.2.rest_0_ = f32[1024,2048]{1,0:T(8,128)} custom-call(bf16[1024,640]{1,0:T(8,128)(2,1)} %slice.17.onehot_ref, bf16[1024,512]{1,0:T(8,128)(2,1)} %get-tuple-element.73.rest_0_, bf16[1024,768]{1,0:T(8,128)(2,1)} %project_half.4.rest_1_, bf16[1024,768]{1,0:T(8,128)(2,1)} %project_half.5.rest_2_, bf16[1024,2048]{1,0:T(8,128)(2,1)} %collective-permute-done.21.rest_3_, ...), custom_call_target="tpu_custom_call" | custom-call | flops 2684354560 | bytes 16777216 | tf_op jit(solution)/shard_map/finish_rows/pallas_call | solution.py:238
  197.6 1.9 collective-permute-done.24.rest_3_
  199.5 0.7 copy-done.4
  200.2 7.7 %finish_rows.3 = bf16[1024,2048]{1,0:T(8,128)(2,1)} custom-call(bf16[1024,384]{1,0:T(8,128)(2,1)} %slice.16.onehot_ref, f32[1024,2048]{1,0:T(8,128)} %finish_rows.2.rest_0_, bf16[96,2048]{1,0:T(8,128)(2,1)} %get-tuple-element.72.rest_1_, bf16[96,2048]{1,0:T(8,128)(2,1)} %copy-done.3, bf16[96,2048]{1,0:T(8,128)(2,1)} %copy-done.4, ...), custom_call_target="tpu_custom_call" | custom-call | flops 1610612736 | bytes 16777216 | tf_op jit(solution)/shard_map/finish_rows/pallas_call | solution.py:238
  (39 shorter events, 3.2 us)
Async XLA Ops:
  0.0 55.4 %collective-permute-start.2 = (bf16[4,64,4096]{2,1,0:T(8,128)(2,1)}, bf16[4,64,4096]{2,1,0:T(8,128)(2,1)}, u32[]{:S(2)}, u32[]{:S(2)}) collective-permute-start(bf16[4,64,4096]{2,1,0:T(8,128)(2,1)} %bitcast.8), channel_id=1, source_target_pairs={{8,16},{10,18},{12,20},{14,22},{16,8},{18,10},{20,12},{22,14},{9,1... | collective-permute-start | bytes 6291464 | tf_op jit(solution)/shard_map/ppermute | solution.py:303
  2.1 53.3 %collective-permute-start = (bf16[4,64,4096]{2,1,0:T(8,128)(2,1)}, bf16[4,64,4096]{2,1,0:T(8,128)(2,1)}, u32[]{:S(2)}, u32[]{:S(2)}) collective-permute-start(bf16[4,64,4096]{2,1,0:T(8,128)(2,1)} %bitcast.9), channel_id=1, source_target_pairs={{0,8},{2,10},{4,12},{6,14},{8,0},{10,2},{12,4},{14,6},{16,24},{18,... | collective-permute-start | bytes 6291464 | tf_op jit(solution)/shard_map/ppermute | solution.py:303
  21.2 35.8 %collective-permute-start.5 = (bf16[96,4096]{1,0:T(8,128)(2,1)}, bf16[96,4096]{1,0:T(8,128)(2,1)S(1)}, u32[]{:S(2)}, u32[]{:S(2)}) collective-permute-start(bf16[96,4096]{1,0:T(8,128)(2,1)} %get-tuple-element.52), channel_id=1, source_target_pairs={{0,4},{2,6},{4,0},{6,2},{8,12},{10,14},{12,8},{14,10},{16,20},{18,... | collective-permute-start | bytes 2359304 | tf_op jit(solution)/shard_map/ppermute | solution.py:303
  22.8 35.8 %collective-permute-start.4 = (bf16[96,4096]{1,0:T(8,128)(2,1)}, bf16[96,4096]{1,0:T(8,128)(2,1)}, u32[]{:S(2)}, u32[]{:S(2)}) collective-permute-start(bf16[96,4096]{1,0:T(8,128)(2,1)} %get-tuple-element.51), channel_id=1, source_target_pairs={{0,2},{2,0},{4,6},{6,4},{8,10},{10,8},{12,14},{14,12},{16,18},{18,... | collective-permute-start | bytes 2359304 | tf_op jit(solution)/shard_map/ppermute | solution.py:303
  24.3 35.8 %collective-permute-start.6 = (bf16[96,4096]{1,0:T(8,128)(2,1)}, bf16[96,4096]{1,0:T(8,128)(2,1)}, u32[]{:S(2)}, u32[]{:S(2)}) collective-permute-start(bf16[96,4096]{1,0:T(8,128)(2,1)} %get-tuple-element.53), channel_id=1, source_target_pairs={{0,6},{2,4},{4,2},{6,0},{8,14},{10,12},{12,10},{14,8},{16,22},{18,... | collective-permute-start | bytes 2359304 | tf_op jit(solution)/shard_map/ppermute | solution.py:303
  55.3 23.8 %collective-permute-start.1 = (bf16[4,64,2048]{2,1,0:T(8,128)(2,1)}, bf16[4,64,2048]{2,1,0:T(8,128)(2,1)}, u32[]{:S(2)}, u32[]{:S(2)}) collective-permute-start(bf16[4,64,2048]{2,1,0:T(8,128)(2,1)} %refs_2_.1), channel_id=1, source_target_pairs={{0,8},{2,10},{4,12},{6,14},{8,0},{10,2},{12,4},{14,6},{16,24},{18,... | collective-permute-start | bytes 3145736 | tf_op jit(solution)/shard_map/ppermute | solution.py:303
  55.4 25.0 %collective-permute-start.3 = (bf16[4,64,2048]{2,1,0:T(8,128)(2,1)}, bf16[4,64,2048]{2,1,0:T(8,128)(2,1)}, u32[]{:S(2)}, u32[]{:S(2)}) collective-permute-start(bf16[4,64,2048]{2,1,0:T(8,128)(2,1)} %refs_2_.1), channel_id=1, source_target_pairs={{8,16},{10,18},{12,20},{14,22},{16,8},{18,10},{20,12},{22,14},{9,1... | collective-permute-start | bytes 3145736 | tf_op jit(solution)/shard_map/ppermute | solution.py:303
  57.0 3.0 %copy-start = (bf16[96,4096]{1,0:T(8,128)(2,1)}, bf16[96,4096]{1,0:T(8,128)(2,1)S(1)}, u32[]{:S(2)}) copy-start(bf16[96,4096]{1,0:T(8,128)(2,1)S(1)} %collective-permute-done.5.refs_2_) | copy-start | bytes 2359300
  57.0 33.8 %collective-permute-start.10 = (bf16[160,4096]{1,0:T(8,128)(2,1)}, bf16[160,4096]{1,0:T(8,128)(2,1)}, u32[]{:S(2)}, u32[]{:S(2)}) collective-permute-start(bf16[160,4096]{1,0:T(8,128)(2,1)} %get-tuple-element.60), channel_id=1, source_target_pairs={{0,4},{2,6},{4,0},{6,2},{8,12},{10,14},{12,8},{14,10},{16,20},{18,... | collective-permute-start | bytes 3932168 | tf_op jit(solution)/shard_map/ppermute | solution.py:303
  58.5 32.3 %collective-permute-start.9 = (bf16[160,4096]{1,0:T(8,128)(2,1)}, bf16[160,4096]{1,0:T(8,128)(2,1)}, u32[]{:S(2)}, u32[]{:S(2)}) collective-permute-start(bf16[160,4096]{1,0:T(8,128)(2,1)} %get-tuple-element.58), channel_id=1, source_target_pairs={{0,2},{2,0},{4,6},{6,4},{8,10},{10,8},{12,14},{14,12},{16,18},{18,... | collective-permute-start | bytes 3932168 | tf_op jit(solution)/shard_map/ppermute | solution.py:303
  79.1 25.3 %collective-permute-start.8 = (bf16[2,64,4096]{2,1,0:T(8,128)(2,1)}, bf16[2,64,4096]{2,1,0:T(8,128)(2,1)}, u32[]{:S(2)}, u32[]{:S(2)}) collective-permute-start(bf16[2,64,4096]{2,1,0:T(8,128)(2,1)} %slice.18), channel_id=1, source_target_pairs={{8,0},{10,2},{12,4},{14,6},{16,24},{18,26},{20,28},{22,30},{9,1},{... | collective-permute-start | bytes 3145736 | tf_op jit(solution)/shard_map/ppermute | solution.py:303
  80.4 25.3 %collective-permute-start.7 = (bf16[4,64,2048]{2,1,0:T(8,128)(2,1)}, bf16[4,64,2048]{2,1,0:T(8,128)(2,1)}, u32[]{:S(2)}, u32[]{:S(2)}) collective-permute-start(bf16[4,64,2048]{2,1,0:T(8,128)(2,1)} %collective-permute-done.1.refs_3_), channel_id=1, source_target_pairs={{8,16},{10,18},{12,20},{14,22},{16,8},{18,10},{20,12},{22,14},{9,1... | collective-permute-start | bytes 3145736 | tf_op jit(solution)/shard_map/ppermute | solution.py:303
  82.1 72.1 %collective-permute-start.17 = (bf16[384,4096]{1,0:T(8,128)(2,1)}, bf16[384,4096]{1,0:T(8,128)(2,1)}, u32[]{:S(2)}, u32[]{:S(2)}) collective-permute-start(bf16[384,4096]{1,0:T(8,128)(2,1)} %join_rows.1), channel_id=1, source_target_pairs={{0,8},{2,10},{4,12},{6,14},{24,16},{26,18},{28,20},{30,22},{1,9},{... | collective-permute-start | bytes 9437192 | tf_op jit(solution)/shard_map/ppermute | solution.py:303
  90.8 28.8 %collective-permute-start.12 = (bf16[160,4096]{1,0:T(8,128)(2,1)}, bf16[160,4096]{1,0:T(8,128)(2,1)}, u32[]{:S(2)}, u32[]{:S(2)}) collective-permute-start(bf16[160,4096]{1,0:T(8,128)(2,1)} %get-tuple-element.65), channel_id=1, source_target_pairs={{0,6},{2,4},{4,2},{6,0},{8,14},{10,12},{12,10},{14,8},{16,22},{18,... | collective-permute-start | bytes 3932168 | tf_op jit(solution)/shard_map/ppermute | solution.py:303
  104.4 23.7 %collective-permute-start.11 = (bf16[4,64,2048]{2,1,0:T(8,128)(2,1)}, bf16[4,64,2048]{2,1,0:T(8,128)(2,1)}, u32[]{:S(2)}, u32[]{:S(2)}) collective-permute-start(bf16[4,64,2048]{2,1,0:T(8,128)(2,1)} %collective-permute-done.3.refs_4_.refs_2_), channel_id=1, source_target_pairs={{8,0},{10,2},{12,4},{14,6},{16,24},{18,26},{20,28},{22,30},{9,1},{... | collective-permute-start | bytes 3145736 | tf_op jit(solution)/shard_map/ppermute | solution.py:303
  105.7 48.3 %collective-permute-start.18 = (bf16[4,64,4096]{2,1,0:T(8,128)(2,1)}, bf16[4,64,4096]{2,1,0:T(8,128)(2,1)}, u32[]{:S(2)}, u32[]{:S(2)}) collective-permute-start(bf16[4,64,4096]{2,1,0:T(8,128)(2,1)} %collective-permute-done.refs_5_), channel_id=1, source_target_pairs={{8,16},{10,18},{12,20},{14,22},{16,8},{18,10},{20,12},{22,14},{9,1... | collective-permute-start | bytes 6291464 | tf_op jit(solution)/shard_map/ppermute | solution.py:303
  126.2 3.2 %collective-permute-start.14 = (f32[640,256]{1,0:T(8,128)}, f32[640,256]{1,0:T(8,128)S(1)}, u32[]{:S(2)}, u32[]{:S(2)}) collective-permute-start(f32[640,256]{1,0:T(8,128)} %down_rows.2.refs_0_), channel_id=1, source_target_pairs={{0,1},{1,0},{2,3},{3,2},{4,5},{5,4},{6,7},{7,6},{8,9},{9,8},{10,11... | collective-permute-start | bytes 1966088 | tf_op jit(solution)/shard_map/ppermute | solution.py:357
  128.1 25.9 %collective-permute-start.13 = (bf16[4,64,2048]{2,1,0:T(8,128)(2,1)}, bf16[4,64,2048]{2,1,0:T(8,128)(2,1)}, u32[]{:S(2)}, u32[]{:S(2)}) collective-permute-start(bf16[4,64,2048]{2,1,0:T(8,128)(2,1)} %collective-permute-done.7.refs_4_), channel_id=1, source_target_pairs={{8,0},{10,2},{12,4},{14,6},{16,24},{18,26},{20,28},{22,30},{9,1},{... | collective-permute-start | bytes 3145736 | tf_op jit(solution)/shard_map/ppermute | solution.py:303
  129.4 0.9 copy-start.2
  135.6 16.3 %collective-permute-start.15 = (bf16[160,2048]{1,0:T(8,128)(2,1)}, bf16[160,2048]{1,0:T(8,128)(2,1)}, u32[]{:S(2)}, u32[]{:S(2)}) collective-permute-start(bf16[160,2048]{1,0:T(8,128)(2,1)} %get-tuple-element.67), channel_id=1, source_target_pairs={{0,2},{2,0},{4,6},{6,4},{8,10},{10,8},{12,14},{14,12},{16,18},{18,... | collective-permute-start | bytes 1966088 | tf_op jit(solution)/shard_map/ppermute | solution.py:303
  136.8 15.3 %collective-permute-start.16 = (bf16[160,2048]{1,0:T(8,128)(2,1)}, bf16[160,2048]{1,0:T(8,128)(2,1)}, u32[]{:S(2)}, u32[]{:S(2)}) collective-permute-start(bf16[160,2048]{1,0:T(8,128)(2,1)} %get-tuple-element.68), channel_id=1, source_target_pairs={{0,4},{2,6},{4,0},{6,2},{8,12},{10,14},{12,8},{14,10},{16,20},{18,... | collective-permute-start | bytes 1966088 | tf_op jit(solution)/shard_map/ppermute | solution.py:303
  160.6 2.5 %collective-permute-start.19 = (f32[768,256]{1,0:T(8,128)}, f32[768,256]{1,0:T(8,128)S(1)}, u32[]{:S(2)}, u32[]{:S(2)}) collective-permute-start(f32[768,256]{1,0:T(8,128)} %down_rows.3), channel_id=1, source_target_pairs={{0,1},{1,0},{2,3},{3,2},{4,5},{5,4},{6,7},{7,6},{8,9},{9,8},{10,11... | collective-permute-start | bytes 2359304 | tf_op jit(solution)/shard_map/ppermute | solution.py:357
  163.1 22.9 %collective-permute-start.21 = (bf16[1024,2048]{1,0:T(8,128)(2,1)}, bf16[1024,2048]{1,0:T(8,128)(2,1)}, u32[]{:S(2)}, u32[]{:S(2)}) collective-permute-start(bf16[1024,2048]{1,0:T(8,128)(2,1)} %get-tuple-element.74), channel_id=1, source_target_pairs={{0,1},{1,0},{2,3},{3,2},{4,5},{5,4},{6,7},{7,6},{8,9},{9,8},{10,11... | collective-permute-start | bytes 12582920 | tf_op jit(solution)/shard_map/ppermute | solution.py:357
  163.2 22.8 %collective-permute-start.22 = (bf16[160,2048]{1,0:T(8,128)(2,1)}, bf16[160,2048]{1,0:T(8,128)(2,1)}, u32[]{:S(2)}, u32[]{:S(2)}) collective-permute-start(bf16[160,2048]{1,0:T(8,128)(2,1)} %get-tuple-element.77), channel_id=1, source_target_pairs={{0,6},{2,4},{4,2},{6,0},{8,14},{10,12},{12,10},{14,8},{16,22},{18,... | collective-permute-start | bytes 1966088 | tf_op jit(solution)/shard_map/ppermute | solution.py:303
  165.8 8.9 %copy-start.1 = (bf16[768,256]{1,0:T(8,128)(2,1)}, bf16[768,256]{1,0:T(8,128)(2,1)S(1)}, u32[]{:S(2)}) copy-start(bf16[768,256]{1,0:T(8,128)(2,1)S(1)} %add_convert_fusion.refs_0_) | copy-start | bytes 1179652
  165.8 8.9 %collective-permute-start.20 = (bf16[384,256]{1,0:T(8,128)(2,1)S(1)}, bf16[384,256]{1,0:T(8,128)(2,1)S(1)}, u32[]{:S(2)}, u32[]{:S(2)}) collective-permute-start(bf16[384,256]{1,0:T(8,128)(2,1)S(1)} %slice.19), channel_id=1, source_target_pairs={{8,0},{10,2},{12,4},{14,6},{16,24},{18,26},{20,28},{22,30},{9,1},{... | collective-permute-start | bytes 589832 | tf_op jit(solution)/shard_map/ppermute | solution.py:303
  174.7 0.7 copy-start.5
  179.9 17.7 %collective-permute-start.23 = (bf16[96,2048]{1,0:T(8,128)(2,1)}, bf16[96,2048]{1,0:T(8,128)(2,1)S(1)}, u32[]{:S(2)}, u32[]{:S(2)}) collective-permute-start(bf16[96,2048]{1,0:T(8,128)(2,1)} %get-tuple-element.78), channel_id=1, source_target_pairs={{0,2},{2,0},{4,6},{6,4},{8,10},{10,8},{12,14},{14,12},{16,18},{18,... | collective-permute-start | bytes 1179656 | tf_op jit(solution)/shard_map/ppermute | solution.py:303
  180.6 18.9 %collective-permute-start.24 = (bf16[96,2048]{1,0:T(8,128)(2,1)}, bf16[96,2048]{1,0:T(8,128)(2,1)S(1)}, u32[]{:S(2)}, u32[]{:S(2)}) collective-permute-start(bf16[96,2048]{1,0:T(8,128)(2,1)} %get-tuple-element.79), channel_id=1, source_target_pairs={{0,4},{2,6},{4,0},{6,2},{8,12},{10,14},{12,8},{14,10},{16,20},{18,... | collective-permute-start | bytes 1179656 | tf_op jit(solution)/shard_map/ppermute | solution.py:303
  182.1 17.3 %collective-permute-start.25 = (bf16[96,2048]{1,0:T(8,128)(2,1)}, bf16[96,2048]{1,0:T(8,128)(2,1)}, u32[]{:S(2)}, u32[]{:S(2)}) collective-permute-start(bf16[96,2048]{1,0:T(8,128)(2,1)} %get-tuple-element.80), channel_id=1, source_target_pairs={{0,6},{2,4},{4,2},{6,0},{8,14},{10,12},{12,10},{14,8},{16,22},{18,... | collective-permute-start | bytes 1179656 | tf_op jit(solution)/shard_map/ppermute | solution.py:303
  197.6 1.9 copy-start.3
  199.5 0.8 copy-start.4

commit v7 on v6

--- a/solution.py
+++ b/solution.py
@@ -128,26 +128,41 @@
     return [(len(arrays), count) for arrays, _, count in groups]
 
 
+def owned_by(shape, count):
+    owner = lax.broadcasted_iota(jnp.int32, shape, 0) // MOST % count
+    return owner == lax.broadcasted_iota(jnp.int32, shape, 1) // (shape[1] // count)
+
+
 def down_kernel(groups, sources, *refs):
-    xs, ws, o_ref = refs[:sources], refs[sources:-1], refs[-1]
+    xs, ws, o_ref, total = refs[:sources], refs[sources:-2], refs[-2], refs[-1]
     step = pl.program_id(0)
+    rank = o_ref.shape[1]
     sides = sources // COLUMNS
     side_rows = o_ref.shape[0] // sides
 
     @pl.when(step == 0)
     def _():
-        o_ref[...] = jnp.zeros_like(o_ref)
+        total[...] = jnp.zeros_like(total)
 
     for start, count, w in factors(ws, groups):
-        rank = w.shape[0] // count
         rows = jnp.concatenate([x[start * MOST : (start + count) * MOST] for x in xs], axis=0)
-        y = lax.dot_general(rows, w, NT, preferred_element_type=jnp.float32)
-        owner = lax.broadcasted_iota(jnp.int32, y.shape, 0) // MOST % count
-        y = jnp.where(owner == lax.broadcasted_iota(jnp.int32, y.shape, 1) // rank, y, 0.0)
-        part = COLUMNS * count * MOST
-        for side in range(sides):
-            at = side * side_rows + start * COLUMNS * MOST
-            o_ref[at : at + part, : w.shape[0]] += y[side * part : (side + 1) * part]
+        at = start * sources * MOST
+        total[at : at + rows.shape[0], : w.shape[0]] += lax.dot_general(
+            rows, w, NT, preferred_element_type=jnp.float32
+        )
+
+    @pl.when(step == pl.num_programs(0) - 1)
+    def _():
+        start = 0
+        for _, count in groups:
+            at, part = start * sources * MOST, COLUMNS * count * MOST
+            y = total[at : at + sides * part, : count * rank]
+            y = jnp.where(owned_by(y.shape, count), y, 0.0)
+            y = functools.reduce(jnp.add, [y[:, k * rank : (k + 1) * rank] for k in range(count)])
+            for side in range(sides):
+                to = side * side_rows + start * COLUMNS * MOST
+                o_ref[to : to + part] = y[side * part : (side + 1) * part]
+            start += count
 
 
 def down(xs, groups):
@@ -164,8 +179,9 @@
         functools.partial(down_kernel, shape_of(groups), len(xs)),
         grid=(width // tile,),
         in_specs=[block(section) for _, section in xs] + factor_specs(groups, rank, tile),
-        out_specs=pl.BlockSpec((rows, wide), lambda k: (0, 0)),
-        out_shape=jax.ShapeDtypeStruct((rows, wide), jnp.float32),
+        out_specs=pl.BlockSpec((rows, rank), lambda k: (0, 0)),
+        out_shape=jax.ShapeDtypeStruct((rows, rank), jnp.float32),
+        scratch_shapes=[pltpu.VMEM((rows, wide), jnp.float32)],
         compiler_params=params(),
         cost_estimate=cost(2 * rows * wide * width, 2 * width * (served * rank + rows)),
         name="down_rows",
@@ -178,7 +194,14 @@
 
     @pl.when(pl.program_id(0) == 0)
     def _():
-        y[...] = functools.reduce(jnp.add, [ref[...] for ref in ys]).astype(jnp.bfloat16)
+        low = functools.reduce(jnp.add, [ref[...] for ref in ys]).astype(jnp.float32)
+        at = 0
+        for _, count in groups:
+            part = COLUMNS * count * MOST
+            wide = jnp.concatenate([low[at : at + part]] * count, axis=1)
+            wide = jnp.where(owned_by(wide.shape, count), wide, 0.0)
+            y[at : at + part, : wide.shape[1]] = wide.astype(jnp.bfloat16)
+            at += part
 
     for start, count, u in factors(us, groups):
         part = count * MOST
@@ -193,11 +216,11 @@
     served = sum(count for _, _, count in groups)
     _, rank, columns = groups[0][0][0].shape
     tile = 512
-    rows, wide = served * COLUMNS * MOST, ys[0].shape[1]
+    rows, wide = served * COLUMNS * MOST, max(count for _, _, count in groups) * rank
     return pl.pallas_call(
         functools.partial(lift_kernel, shape_of(groups), len(ys)),
         grid=(columns // tile,),
-        in_specs=[pl.BlockSpec((rows, wide), lambda k: (0, 0))] * len(ys) + factor_specs(groups, rank, tile),
+        in_specs=[pl.BlockSpec((rows, rank), lambda k: (0, 0))] * len(ys) + factor_specs(groups, rank, tile),
         out_specs=[pl.BlockSpec((served * MOST, tile), lambda k: (0, k))] * COLUMNS,
         out_shape=[jax.ShapeDtypeStruct((served * MOST, columns), jnp.bfloat16)] * COLUMNS,
         scratch_shapes=[pltpu.VMEM((rows, wide), jnp.bfloat16)],
@@ -382,7 +405,7 @@
     )
     lifted_away = [rows[0]] + [send(rows[d], turn[d]) for d in range(1, COLUMNS)]
     base_own[0] = after(base_own[0], rows[0])
-    part = finish(back_home, [base_own, [base_other]], lifted_home, TILE, jnp.float32)
+    part = finish(back_home, [base_own, [base_other]], lifted_home, TILE, jnp.bfloat16)
     return finish(back_away, [[part]], lifted_away, 2 * TILE, jnp.bfloat16)
 
 

time: 209 us -> 208 us (level)
  transfers between devices with their start and end apart: 26 -> 26, of which waited for: 10 -> 9; matrix products, arithmetic and copies ran while one was open for 4% -> 4% of each run, Pallas kernels for 48% -> 47%
where the time goes in v7:
time: 208 us; the launch traced here: 207 us
  Pallas kernels  111 us (53%)
  waiting for transfers between devices  42.2 us (20%)
  starting transfers between devices  42.1 us (20%)
  local copies, waits for them, and re-layouts  6.79 us (3%)
  other arithmetic  3.6 us (2%)
    pallas_call x3, Pallas kernels, project(): pl.pallas_call(functools.partial(project_kernel, counts), grid_spec=pltpu...  54.1 us
    ppermute x23, starting transfers between devices, send(): return lax.ppermute(after(x, *earlier) if earlier else x, 'rep', pairs)  41.8 us
    ppermute x23, waiting for transfers between devices, send(): return lax.ppermute(after(x, *earlier) if earlier else x, 'rep', pairs)  38.5 us
    pallas_call x2, Pallas kernels, finish(): pl.pallas_call(functools.partial(finish_kernel, starts), grid=(columns //...  17.6 us
    pallas_call x2, Pallas kernels, down(): pl.pallas_call(functools.partial(down_kernel, shape_of(groups), len(xs)),...  13.1 us
    pallas_call x1, Pallas kernels, pack(): pl.pallas_call(pack_kernel, grid=(width // tile,), in_specs=[pl.BlockSpec...  12.5 us
    pallas_call x2, Pallas kernels, lift(): pl.pallas_call(functools.partial(lift_kernel, shape_of(groups), len(ys)),...  9.71 us
    pallas_call x1, Pallas kernels, join(): pl.pallas_call(join_kernel, grid=(width // tile,), in_specs=[pl.BlockSpec...  4.39 us
  transfers between devices with their start and end apart: 26, of which 9 were waited for; matrix products, arithmetic and copies ran while one was open for 4% of the time, Pallas kernels for 47%

profile of v7, /device:TPU:0, one launch (start us, length us, event | category | flops | bytes accessed | tf_op | source)
XLA Modules:
  0.0 206.8 jit_solution(16878381493597362362)
XLA Ops:
  0.0 2.1 collective-permute-start.2
  2.1 4.5 %collective-permute-start = (bf16[4,64,4096]{2,1,0:T(8,128)(2,1)}, bf16[4,64,4096]{2,1,0:T(8,128)(2,1)}, u32[]{:S(2)}, u32[]{:S(2)}) collective-permute-start(bf16[4,64,4096]{2,1,0:T(8,128)(2,1)} %bitcast.9), channel_id=1, source_target_pairs={{0,8},{2,10},{4,12},{6,14},{8,0},{10,2},{12,4},{14,6},{16,24},{18,... | collective-permute-start | bytes 6291464 | tf_op jit(solution)/shard_map/ppermute | solution.py:326
  6.6 0.8 select_reduce_fusion
  8.0 0.7 fusion.14.target_ref
  8.7 12.5 %pack_rows.1 = (bf16[96,4096]{1,0:T(8,128)(2,1)}, bf16[96,4096]{1,0:T(8,128)(2,1)}, bf16[96,4096]{1,0:T(8,128)(2,1)}, bf16[96,4096]{1,0:T(8,128)(2,1)}, bf16[160...) custom-call(s32[1,1024]{1,0:T(1,128)} %fusion.14.target_ref, ...), custom_call_target="tpu_custom_call" | custom-call | flops 8589934592 | bytes 16777216 | tf_op jit(solution)/shard_map/pack_rows/pallas_call | solution.py:45
  21.2 1.5 collective-permute-start.5
  22.8 1.5 collective-permute-start.4
  25.3 30.0 %project_half.3 = (bf16[1024,2048]{1,0:T(8,128)(2,1)}, bf16[1024,512]{1,0:T(8,128)(2,1)}) custom-call(s32[2]{0:T(128)} %pad_add_fusion.place_ref, bf16[1024,4096]{1,0:T(8,128)(2,1)} %x_ref.4, bf16[4096,4096]{1,0:T(8,128)(2,1)} %w_ref.5), custom_call_target="tpu_custom_call" | custom-call | flops 21474836480 | bytes 34603008 | tf_op jit(solution)/shard_map/project_half/pallas_call | solution.py:88
  55.4 1.6 collective-permute-start.3
  57.0 1.5 collective-permute-start.10
  58.5 1.5 collective-permute-start.9
  60.0 4.4 %join_rows.1 = bf16[384,4096]{1,0:T(8,128)(2,1)} custom-call(bf16[96,4096]{1,0:T(8,128)(2,1)} %get-tuple-element.69.refs_0_, bf16[96,4096]{1,0:T(8,128)(2,1)} %collective-permute-done.4.refs_1_, bf16[96,4096]{1,0:T(8,128)(2,1)} %copy-done, bf16[96,4096]{1,0:T(8,128)(2,1)} %collective-permute-done.6.refs_3_), custom_call_target="tpu_custom_call" | custom-call | bytes 6291456 | tf_op jit(solution)/shard_map/join_rows/pallas_call | solution.py:284
  64.4 2.3 %slice.18 = bf16[2,64,4096]{2,1,0:T(8,128)(2,1)} slice(bf16[4,64,4096]{2,1,0:T(8,128)(2,1)} %collective-permute-done.2.refs_6_.refs_8_), slice={[0:2], [0:64], [0:4096]} | slice | bytes 2097152 | tf_op jit(solution)/shard_map/slice | solution.py:366
  66.7 12.0 %project_half.4.rest_1_ = bf16[1024,768]{1,0:T(8,128)(2,1)} custom-call(s32[1]{0:T(128)} %bitcast.6.place_ref, bf16[1024,4096]{1,0:T(8,128)(2,1)} %x_ref.4, bf16[4096,4096]{1,0:T(8,128)(2,1)} %w_ref.5), custom_call_target="tpu_custom_call" | custom-call | flops 6442450944 | bytes 16252928 | tf_op jit(solution)/shard_map/project_half/pallas_call | solution.py:88
  79.1 1.3 collective-permute-start.8
  80.4 1.7 collective-permute-start.7
  82.1 8.7 %collective-permute-start.17 = (bf16[384,4096]{1,0:T(8,128)(2,1)}, bf16[384,4096]{1,0:T(8,128)(2,1)}, u32[]{:S(2)}, u32[]{:S(2)}) collective-permute-start(bf16[384,4096]{1,0:T(8,128)(2,1)} %join_rows.1), channel_id=1, source_target_pairs={{0,8},{2,10},{4,12},{6,14},{24,16},{26,18},{28,20},{30,22},{1,9},{... | collective-permute-start | bytes 9437192 | tf_op jit(solution)/shard_map/ppermute | solution.py:326
  90.8 1.5 collective-permute-start.12
  92.4 12.0 %project_half.5.rest_2_ = bf16[1024,768]{1,0:T(8,128)(2,1)} custom-call(s32[1]{0:T(128)} %bitcast.7.place_ref, bf16[1024,4096]{1,0:T(8,128)(2,1)} %x_ref.4, bf16[4096,4096]{1,0:T(8,128)(2,1)} %w_ref.5), custom_call_target="tpu_custom_call" | custom-call | flops 6442450944 | bytes 16252928 | tf_op jit(solution)/shard_map/project_half/pallas_call | solution.py:88
  104.4 1.3 collective-permute-start.11
  105.7 2.0 collective-permute-start.18
  107.8 11.9 %collective-permute-done.12.refs_3_ = bf16[160,4096]{1,0:T(8,128)(2,1)} collective-permute-done((bf16[160,4096]{1,0:T(8,128)(2,1)}, bf16[160,4096]{1,0:T(8,128)(2,1)}, u32[]{:S(2)}, u32[]{:S(2)}) %collective-permute-start.12) | collective-permute-done | bytes 1310752 | tf_op jit(solution)/shard_map/ppermute | solution.py:326
  119.7 6.7 %down_rows.2.refs_0_ = f32[640,64]{1,0:T(8,128)} custom-call(bf16[160,4096]{1,0:T(8,128)(2,1)} %get-tuple-element.63.refs_0_, bf16[160,4096]{1,0:T(8,128)(2,1)} %collective-permute-done.9.refs_1_, bf16[160,4096]{1,0:T(8,128)(2,1)} %collective-permute-done.10.refs_2_, bf16[160,4096]{1,0:T(8,128)(2,1)} %collective-permute-done.12.refs_3_, ...), custom_call_target="tpu_custom_call" | custom-call | flops 1342177280 | bytes 10485760 | tf_op jit(solution)/shard_map/down_rows/pallas_call | solution.py:178
  126.3 1.8 collective-permute-done.11.refs_5_.refs_3_
  128.1 1.3 collective-permute-start.13
  129.4 1.8 collective-permute-done.14.refs_1_
  131.3 0.7 copy-done.4
  132.0 5.2 %lift_rows.2 = (bf16[160,2048]{1,0:T(8,128)(2,1)}, bf16[160,2048]{1,0:T(8,128)(2,1)}, bf16[160,2048]{1,0:T(8,128)(2,1)}, bf16[160,2048]{1,0:T(8,128)(2,1)}) custom-call(f32[640,64]{1,0:T(8,128)} %down_rows.2.refs_0_, f32[640,64]{1,0:T(8,128)} %copy-done.4, bf16[4,64,2048]{2,1,0:T(8,128)(2,1)} %refs_2_.1, ...), custom_call_target="tpu_custom_call" | custom-call | flops 671088640 | bytes 5242880 | tf_op jit(solution)/shard_map/lift_rows/pallas_call | solution.py:220
  137.2 1.2 collective-permute-start.15
  138.3 1.5 collective-permute-start.16
  139.9 14.3 %collective-permute-done.15.rest_5_ = bf16[160,2048]{1,0:T(8,128)(2,1)S(1)} collective-permute-done((bf16[160,2048]{1,0:T(8,128)(2,1)}, bf16[160,2048]{1,0:T(8,128)(2,1)S(1)}, u32[]{:S(2)}, u32[]{:S(2)}) %collective-permute-start.15) | collective-permute-done | bytes 655392 | tf_op jit(solution)/shard_map/ppermute | solution.py:326
  154.2 1.0 collective-permute-done.16.rest_6_
  155.2 6.4 %down_rows.3 = f32[768,64]{1,0:T(8,128)} custom-call(bf16[96,4096]{1,0:T(8,128)(2,1)} %get-tuple-element.69.refs_0_, bf16[96,4096]{1,0:T(8,128)(2,1)} %collective-permute-done.4.refs_1_, bf16[96,4096]{1,0:T(8,128)(2,1)} %copy-done, bf16[96,4096]{1,0:T(8,128)(2,1)} %collective-permute-done.6.refs_3_, ...), custom_call_target="tpu_custom_call" | custom-call | flops 1610612736 | bytes 9437184 | tf_op jit(solution)/shard_map/down_rows/pallas_call | solution.py:178
  161.7 1.9 collective-permute-done.19
  163.7 1.5 collective-permute-start.22
  165.3 1.1 add_convert_fusion.refs_0_
  166.3 1.5 collective-permute-start.20
  167.9 6.4 %collective-permute-done.20.refs_1_ = bf16[384,64]{1,0:T(8,128)(2,1)S(1)} collective-permute-done((bf16[384,64]{1,0:T(8,128)(2,1)S(1)}, bf16[384,64]{1,0:T(8,128)(2,1)S(1)}, u32[]{:S(2)}, u32[]{:S(2)}) %collective-permute-start.20) | collective-permute-done | bytes 49184 | tf_op jit(solution)/shard_map/ppermute | solution.py:326
  174.2 0.6 copy-done.5
  174.9 4.5 %lift_rows.3 = (bf16[96,2048]{1,0:T(8,128)(2,1)}, bf16[96,2048]{1,0:T(8,128)(2,1)}, bf16[96,2048]{1,0:T(8,128)(2,1)}, bf16[96,2048]{1,0:T(8,128)(2,1)}) custom-call(bf16[768,64]{1,0:T(8,128)(2,1)} %copy-done.1, bf16[384,64]{1,0:T(8,128)(2,1)} %copy-done.5, bf16[4,64,2048]{2,1,0:T(8,128)(2,1)} %collective-permute-done.3.refs_4_.refs_2_, ...), custom_call_target="tpu_custom_call" | custom-call | flops 402653184 | bytes 3145728 | tf_op jit(solution)/shard_map/lift_rows/pallas_call | solution.py:220
  179.4 1.5 collective-permute-start.23
  181.5 1.5 collective-permute-start.25
  183.4 1.3 slice.17.onehot_ref
  184.6 1.0 slice.16.onehot_ref
  185.6 0.9 copy-done.3
  186.5 10.8 %finish_rows.2.rest_0_ = bf16[1024,2048]{1,0:T(8,128)(2,1)} custom-call(bf16[1024,640]{1,0:T(8,128)(2,1)} %slice.17.onehot_ref, bf16[1024,512]{1,0:T(8,128)(2,1)} %get-tuple-element.73.rest_0_, bf16[1024,768]{1,0:T(8,128)(2,1)} %project_half.4.rest_1_, bf16[1024,768]{1,0:T(8,128)(2,1)} %project_half.5.rest_2_, ...), custom_call_target="tpu_custom_call" | custom-call | flops 2684354560 | bytes 16777216 | tf_op jit(solution)/shard_map/finish_rows/pallas_call | solution.py:261
  197.3 2.7 %collective-permute-done.24.rest_3_ = bf16[96,2048]{1,0:T(8,128)(2,1)} collective-permute-done((bf16[96,2048]{1,0:T(8,128)(2,1)}, bf16[96,2048]{1,0:T(8,128)(2,1)}, u32[]{:S(2)}, u32[]{:S(2)}) %collective-permute-start.24) | collective-permute-done | bytes 393248 | tf_op jit(solution)/shard_map/ppermute | solution.py:326
  200.0 6.8 %finish_rows.3 = bf16[1024,2048]{1,0:T(8,128)(2,1)} custom-call(bf16[1024,384]{1,0:T(8,128)(2,1)} %slice.16.onehot_ref, bf16[1024,2048]{1,0:T(8,128)(2,1)} %finish_rows.2.rest_0_, bf16[96,2048]{1,0:T(8,128)(2,1)} %get-tuple-element.72.rest_1_, bf16[96,2048]{1,0:T(8,128)(2,1)} %collective-permute-done.23.rest_2_, ...), custom_call_target="tpu_custom_call" | custom-call | flops 1610612736 | bytes 16777216 | tf_op jit(solution)/shard_map/finish_rows/pallas_call | solution.py:261
  (39 shorter events, 3.4 us)
Async XLA Ops:
  0.0 55.4 %collective-permute-start.2 = (bf16[4,64,4096]{2,1,0:T(8,128)(2,1)}, bf16[4,64,4096]{2,1,0:T(8,128)(2,1)}, u32[]{:S(2)}, u32[]{:S(2)}) collective-permute-start(bf16[4,64,4096]{2,1,0:T(8,128)(2,1)} %bitcast.8), channel_id=1, source_target_pairs={{8,16},{10,18},{12,20},{14,22},{16,8},{18,10},{20,12},{22,14},{9,1... | collective-permute-start | bytes 6291464 | tf_op jit(solution)/shard_map/ppermute | solution.py:326
  2.1 53.3 %collective-permute-start = (bf16[4,64,4096]{2,1,0:T(8,128)(2,1)}, bf16[4,64,4096]{2,1,0:T(8,128)(2,1)}, u32[]{:S(2)}, u32[]{:S(2)}) collective-permute-start(bf16[4,64,4096]{2,1,0:T(8,128)(2,1)} %bitcast.9), channel_id=1, source_target_pairs={{0,8},{2,10},{4,12},{6,14},{8,0},{10,2},{12,4},{14,6},{16,24},{18,... | collective-permute-start | bytes 6291464 | tf_op jit(solution)/shard_map/ppermute | solution.py:326
  21.2 35.8 %collective-permute-start.5 = (bf16[96,4096]{1,0:T(8,128)(2,1)}, bf16[96,4096]{1,0:T(8,128)(2,1)S(1)}, u32[]{:S(2)}, u32[]{:S(2)}) collective-permute-start(bf16[96,4096]{1,0:T(8,128)(2,1)} %get-tuple-element.52), channel_id=1, source_target_pairs={{0,4},{2,6},{4,0},{6,2},{8,12},{10,14},{12,8},{14,10},{16,20},{18,... | collective-permute-start | bytes 2359304 | tf_op jit(solution)/shard_map/ppermute | solution.py:326
  22.8 35.8 %collective-permute-start.4 = (bf16[96,4096]{1,0:T(8,128)(2,1)}, bf16[96,4096]{1,0:T(8,128)(2,1)}, u32[]{:S(2)}, u32[]{:S(2)}) collective-permute-start(bf16[96,4096]{1,0:T(8,128)(2,1)} %get-tuple-element.51), channel_id=1, source_target_pairs={{0,2},{2,0},{4,6},{6,4},{8,10},{10,8},{12,14},{14,12},{16,18},{18,... | collective-permute-start | bytes 2359304 | tf_op jit(solution)/shard_map/ppermute | solution.py:326
  24.3 35.8 %collective-permute-start.6 = (bf16[96,4096]{1,0:T(8,128)(2,1)}, bf16[96,4096]{1,0:T(8,128)(2,1)}, u32[]{:S(2)}, u32[]{:S(2)}) collective-permute-start(bf16[96,4096]{1,0:T(8,128)(2,1)} %get-tuple-element.53), channel_id=1, source_target_pairs={{0,6},{2,4},{4,2},{6,0},{8,14},{10,12},{12,10},{14,8},{16,22},{18,... | collective-permute-start | bytes 2359304 | tf_op jit(solution)/shard_map/ppermute | solution.py:326
  55.3 23.8 %collective-permute-start.1 = (bf16[4,64,2048]{2,1,0:T(8,128)(2,1)}, bf16[4,64,2048]{2,1,0:T(8,128)(2,1)}, u32[]{:S(2)}, u32[]{:S(2)}) collective-permute-start(bf16[4,64,2048]{2,1,0:T(8,128)(2,1)} %refs_2_.1), channel_id=1, source_target_pairs={{0,8},{2,10},{4,12},{6,14},{8,0},{10,2},{12,4},{14,6},{16,24},{18,... | collective-permute-start | bytes 3145736 | tf_op jit(solution)/shard_map/ppermute | solution.py:326
  55.4 25.0 %collective-permute-start.3 = (bf16[4,64,2048]{2,1,0:T(8,128)(2,1)}, bf16[4,64,2048]{2,1,0:T(8,128)(2,1)}, u32[]{:S(2)}, u32[]{:S(2)}) collective-permute-start(bf16[4,64,2048]{2,1,0:T(8,128)(2,1)} %refs_2_.1), channel_id=1, source_target_pairs={{8,16},{10,18},{12,20},{14,22},{16,8},{18,10},{20,12},{22,14},{9,1... | collective-permute-start | bytes 3145736 | tf_op jit(solution)/shard_map/ppermute | solution.py:326
  57.0 3.0 %copy-start = (bf16[96,4096]{1,0:T(8,128)(2,1)}, bf16[96,4096]{1,0:T(8,128)(2,1)S(1)}, u32[]{:S(2)}) copy-start(bf16[96,4096]{1,0:T(8,128)(2,1)S(1)} %collective-permute-done.5.refs_2_) | copy-start | bytes 2359300
  57.0 33.8 %collective-permute-start.10 = (bf16[160,4096]{1,0:T(8,128)(2,1)}, bf16[160,4096]{1,0:T(8,128)(2,1)}, u32[]{:S(2)}, u32[]{:S(2)}) collective-permute-start(bf16[160,4096]{1,0:T(8,128)(2,1)} %get-tuple-element.60), channel_id=1, source_target_pairs={{0,4},{2,6},{4,0},{6,2},{8,12},{10,14},{12,8},{14,10},{16,20},{18,... | collective-permute-start | bytes 3932168 | tf_op jit(solution)/shard_map/ppermute | solution.py:326
  58.5 32.3 %collective-permute-start.9 = (bf16[160,4096]{1,0:T(8,128)(2,1)}, bf16[160,4096]{1,0:T(8,128)(2,1)}, u32[]{:S(2)}, u32[]{:S(2)}) collective-permute-start(bf16[160,4096]{1,0:T(8,128)(2,1)} %get-tuple-element.58), channel_id=1, source_target_pairs={{0,2},{2,0},{4,6},{6,4},{8,10},{10,8},{12,14},{14,12},{16,18},{18,... | collective-permute-start | bytes 3932168 | tf_op jit(solution)/shard_map/ppermute | solution.py:326
  79.1 25.3 %collective-permute-start.8 = (bf16[2,64,4096]{2,1,0:T(8,128)(2,1)}, bf16[2,64,4096]{2,1,0:T(8,128)(2,1)}, u32[]{:S(2)}, u32[]{:S(2)}) collective-permute-start(bf16[2,64,4096]{2,1,0:T(8,128)(2,1)} %slice.18), channel_id=1, source_target_pairs={{8,0},{10,2},{12,4},{14,6},{16,24},{18,26},{20,28},{22,30},{9,1},{... | collective-permute-start | bytes 3145736 | tf_op jit(solution)/shard_map/ppermute | solution.py:326
  80.4 25.3 %collective-permute-start.7 = (bf16[4,64,2048]{2,1,0:T(8,128)(2,1)}, bf16[4,64,2048]{2,1,0:T(8,128)(2,1)}, u32[]{:S(2)}, u32[]{:S(2)}) collective-permute-start(bf16[4,64,2048]{2,1,0:T(8,128)(2,1)} %collective-permute-done.1.refs_3_), channel_id=1, source_target_pairs={{8,16},{10,18},{12,20},{14,22},{16,8},{18,10},{20,12},{22,14},{9,1... | collective-permute-start | bytes 3145736 | tf_op jit(solution)/shard_map/ppermute | solution.py:326
  82.1 73.0 %collective-permute-start.17 = (bf16[384,4096]{1,0:T(8,128)(2,1)}, bf16[384,4096]{1,0:T(8,128)(2,1)}, u32[]{:S(2)}, u32[]{:S(2)}) collective-permute-start(bf16[384,4096]{1,0:T(8,128)(2,1)} %join_rows.1), channel_id=1, source_target_pairs={{0,8},{2,10},{4,12},{6,14},{24,16},{26,18},{28,20},{30,22},{1,9},{... | collective-permute-start | bytes 9437192 | tf_op jit(solution)/shard_map/ppermute | solution.py:326
  90.8 28.8 %collective-permute-start.12 = (bf16[160,4096]{1,0:T(8,128)(2,1)}, bf16[160,4096]{1,0:T(8,128)(2,1)}, u32[]{:S(2)}, u32[]{:S(2)}) collective-permute-start(bf16[160,4096]{1,0:T(8,128)(2,1)} %get-tuple-element.65), channel_id=1, source_target_pairs={{0,6},{2,4},{4,2},{6,0},{8,14},{10,12},{12,10},{14,8},{16,22},{18,... | collective-permute-start | bytes 3932168 | tf_op jit(solution)/shard_map/ppermute | solution.py:326
  104.4 23.7 %collective-permute-start.11 = (bf16[4,64,2048]{2,1,0:T(8,128)(2,1)}, bf16[4,64,2048]{2,1,0:T(8,128)(2,1)}, u32[]{:S(2)}, u32[]{:S(2)}) collective-permute-start(bf16[4,64,2048]{2,1,0:T(8,128)(2,1)} %collective-permute-done.3.refs_4_.refs_2_), channel_id=1, source_target_pairs={{8,0},{10,2},{12,4},{14,6},{16,24},{18,26},{20,28},{22,30},{9,1},{... | collective-permute-start | bytes 3145736 | tf_op jit(solution)/shard_map/ppermute | solution.py:326
  105.7 49.4 %collective-permute-start.18 = (bf16[4,64,4096]{2,1,0:T(8,128)(2,1)}, bf16[4,64,4096]{2,1,0:T(8,128)(2,1)}, u32[]{:S(2)}, u32[]{:S(2)}) collective-permute-start(bf16[4,64,4096]{2,1,0:T(8,128)(2,1)} %collective-permute-done.refs_5_), channel_id=1, source_target_pairs={{8,16},{10,18},{12,20},{14,22},{16,8},{18,10},{20,12},{22,14},{9,1... | collective-permute-start | bytes 6291464 | tf_op jit(solution)/shard_map/ppermute | solution.py:326
  128.1 27.1 %collective-permute-start.13 = (bf16[4,64,2048]{2,1,0:T(8,128)(2,1)}, bf16[4,64,2048]{2,1,0:T(8,128)(2,1)}, u32[]{:S(2)}, u32[]{:S(2)}) collective-permute-start(bf16[4,64,2048]{2,1,0:T(8,128)(2,1)} %collective-permute-done.7.refs_4_), channel_id=1, source_target_pairs={{8,0},{10,2},{12,4},{14,6},{16,24},{18,26},{20,28},{22,30},{9,1},{... | collective-permute-start | bytes 3145736 | tf_op jit(solution)/shard_map/ppermute | solution.py:326
  129.4 1.9 collective-permute-start.14
  131.3 0.7 copy-start.4
  137.2 17.0 %collective-permute-start.15 = (bf16[160,2048]{1,0:T(8,128)(2,1)}, bf16[160,2048]{1,0:T(8,128)(2,1)S(1)}, u32[]{:S(2)}, u32[]{:S(2)}) collective-permute-start(bf16[160,2048]{1,0:T(8,128)(2,1)} %get-tuple-element.67), channel_id=1, source_target_pairs={{0,2},{2,0},{4,6},{6,4},{8,10},{10,8},{12,14},{14,12},{16,18},{18,... | collective-permute-start | bytes 1966088 | tf_op jit(solution)/shard_map/ppermute | solution.py:326
  138.3 16.8 %collective-permute-start.16 = (bf16[160,2048]{1,0:T(8,128)(2,1)}, bf16[160,2048]{1,0:T(8,128)(2,1)}, u32[]{:S(2)}, u32[]{:S(2)}) collective-permute-start(bf16[160,2048]{1,0:T(8,128)(2,1)} %get-tuple-element.68), channel_id=1, source_target_pairs={{0,4},{2,6},{4,0},{6,2},{8,12},{10,14},{12,8},{14,10},{16,20},{18,... | collective-permute-start | bytes 1966088 | tf_op jit(solution)/shard_map/ppermute | solution.py:326
  154.2 7.4 %copy-start.2 = (bf16[160,2048]{1,0:T(8,128)(2,1)}, bf16[160,2048]{1,0:T(8,128)(2,1)S(1)}, u32[]{:S(2)}) copy-start(bf16[160,2048]{1,0:T(8,128)(2,1)S(1)} %collective-permute-done.15.rest_5_) | copy-start | bytes 1966084
  161.6 2.0 collective-permute-start.19
  163.6 22.0 %collective-permute-start.21 = (bf16[1024,2048]{1,0:T(8,128)(2,1)}, bf16[1024,2048]{1,0:T(8,128)(2,1)}, u32[]{:S(2)}, u32[]{:S(2)}) collective-permute-start(bf16[1024,2048]{1,0:T(8,128)(2,1)} %get-tuple-element.74), channel_id=1, source_target_pairs={{0,1},{1,0},{2,3},{3,2},{4,5},{5,4},{6,7},{7,6},{8,9},{9,8},{10,11... | collective-permute-start | bytes 12582920 | tf_op jit(solution)/shard_map/ppermute | solution.py:380
  163.7 21.9 %collective-permute-start.22 = (bf16[160,2048]{1,0:T(8,128)(2,1)}, bf16[160,2048]{1,0:T(8,128)(2,1)S(1)}, u32[]{:S(2)}, u32[]{:S(2)}) collective-permute-start(bf16[160,2048]{1,0:T(8,128)(2,1)} %get-tuple-element.77), channel_id=1, source_target_pairs={{0,6},{2,4},{4,2},{6,0},{8,14},{10,12},{12,10},{14,8},{16,22},{18,... | collective-permute-start | bytes 1966088 | tf_op jit(solution)/shard_map/ppermute | solution.py:326
  166.3 7.9 %copy-start.1 = (bf16[768,64]{1,0:T(8,128)(2,1)}, bf16[768,64]{1,0:T(8,128)(2,1)S(1)}, u32[]{:S(2)}) copy-start(bf16[768,64]{1,0:T(8,128)(2,1)S(1)} %add_convert_fusion.refs_0_) | copy-start | bytes 294916
  166.3 7.9 %collective-permute-start.20 = (bf16[384,64]{1,0:T(8,128)(2,1)S(1)}, bf16[384,64]{1,0:T(8,128)(2,1)S(1)}, u32[]{:S(2)}, u32[]{:S(2)}) collective-permute-start(bf16[384,64]{1,0:T(8,128)(2,1)S(1)} %slice.19), channel_id=1, source_target_pairs={{8,0},{10,2},{12,4},{14,6},{16,24},{18,26},{20,28},{22,30},{9,1},{... | collective-permute-start | bytes 147464 | tf_op jit(solution)/shard_map/ppermute | solution.py:326
  174.2 0.6 copy-start.5
  179.4 17.9 %collective-permute-start.23 = (bf16[96,2048]{1,0:T(8,128)(2,1)}, bf16[96,2048]{1,0:T(8,128)(2,1)}, u32[]{:S(2)}, u32[]{:S(2)}) collective-permute-start(bf16[96,2048]{1,0:T(8,128)(2,1)} %get-tuple-element.78), channel_id=1, source_target_pairs={{0,2},{2,0},{4,6},{6,4},{8,10},{10,8},{12,14},{14,12},{16,18},{18,... | collective-permute-start | bytes 1179656 | tf_op jit(solution)/shard_map/ppermute | solution.py:326
  180.9 19.0 %collective-permute-start.24 = (bf16[96,2048]{1,0:T(8,128)(2,1)}, bf16[96,2048]{1,0:T(8,128)(2,1)}, u32[]{:S(2)}, u32[]{:S(2)}) collective-permute-start(bf16[96,2048]{1,0:T(8,128)(2,1)} %get-tuple-element.79), channel_id=1, source_target_pairs={{0,4},{2,6},{4,0},{6,2},{8,12},{10,14},{12,8},{14,10},{16,20},{18,... | collective-permute-start | bytes 1179656 | tf_op jit(solution)/shard_map/ppermute | solution.py:326
  181.5 18.5 %collective-permute-start.25 = (bf16[96,2048]{1,0:T(8,128)(2,1)}, bf16[96,2048]{1,0:T(8,128)(2,1)}, u32[]{:S(2)}, u32[]{:S(2)}) collective-permute-start(bf16[96,2048]{1,0:T(8,128)(2,1)} %get-tuple-element.80), channel_id=1, source_target_pairs={{0,6},{2,4},{4,2},{6,0},{8,14},{10,12},{12,10},{14,8},{16,22},{18,... | collective-permute-start | bytes 1179656 | tf_op jit(solution)/shard_map/ppermute | solution.py:326
  185.6 0.9 copy-start.3

commit v8 on v7

--- a/solution.py
+++ b/solution.py
@@ -168,7 +168,7 @@
 def down(xs, groups):
     served = sum(count for _, _, count in groups)
     _, rank, width = groups[0][0][0].shape
-    tile = 1024
+    tile = 512
     rows = len(xs) * served * MOST
     wide = max(count for _, _, count in groups) * rank
 

time: 208 us -> 210 us (level)
  Pallas kernels: 111 us -> 115 us
    pallas_call x2, Pallas kernels: 13.1 us -> 17 us  [down(): pl.pallas_call(functools.partial(down_kernel, shape_of(groups), len(xs)),...]
  transfers between devices with their start and end apart: 26 -> 26, of which waited for: 9 -> 8; matrix products, arithmetic and copies ran while one was open for 4% -> 4% of each run, Pallas kernels for 47% -> 48%
where the time goes in v8:
time: 210 us; the launch traced here: 209 us
  Pallas kernels  115 us (55%)
  starting transfers between devices  41.9 us (20%)
  waiting for transfers between devices  40.5 us (19%)
  local copies, waits for them, and re-layouts  6.79 us (3%)
  other arithmetic  3.6 us (2%)
    pallas_call x3, Pallas kernels, project(): pl.pallas_call(functools.partial(project_kernel, counts), grid_spec=pltpu...  54.1 us
    ppermute x23, starting transfers between devices, send(): return lax.ppermute(after(x, *earlier) if earlier else x, 'rep', pairs)  41.6 us
    ppermute x23, waiting for transfers between devices, send(): return lax.ppermute(after(x, *earlier) if earlier else x, 'rep', pairs)  36.7 us
    pallas_call x2, Pallas kernels, finish(): pl.pallas_call(functools.partial(finish_kernel, starts), grid=(columns //...  17.6 us
    pallas_call x2, Pallas kernels, down(): pl.pallas_call(functools.partial(down_kernel, shape_of(groups), len(xs)),...  17 us
    pallas_call x1, Pallas kernels, pack(): pl.pallas_call(pack_kernel, grid=(width // tile,), in_specs=[pl.BlockSpec...  12.5 us
    pallas_call x2, Pallas kernels, lift(): pl.pallas_call(functools.partial(lift_kernel, shape_of(groups), len(ys)),...  9.71 us
    pallas_call x1, Pallas kernels, join(): pl.pallas_call(join_kernel, grid=(width // tile,), in_specs=[pl.BlockSpec...  4.39 us
  transfers between devices with their start and end apart: 26, of which 8 were waited for; matrix products, arithmetic and copies ran while one was open for 4% of the time, Pallas kernels for 48%

profile of v8, /device:TPU:0, one launch (start us, length us, event | category | flops | bytes accessed | tf_op | source)
XLA Modules:
  0.0 208.8 jit_solution(10475069570553837639)
XLA Ops:
  0.0 2.1 collective-permute-start.2
  2.1 4.5 %collective-permute-start = (bf16[4,64,4096]{2,1,0:T(8,128)(2,1)}, bf16[4,64,4096]{2,1,0:T(8,128)(2,1)}, u32[]{:S(2)}, u32[]{:S(2)}) collective-permute-start(bf16[4,64,4096]{2,1,0:T(8,128)(2,1)} %bitcast.9), channel_id=1, source_target_pairs={{0,8},{2,10},{4,12},{6,14},{8,0},{10,2},{12,4},{14,6},{16,24},{18,... | collective-permute-start | bytes 6291464 | tf_op jit(solution)/shard_map/ppermute | solution.py:326
  6.6 0.8 select_reduce_fusion
  8.0 0.7 fusion.14.target_ref
  8.7 12.5 %pack_rows.1 = (bf16[96,4096]{1,0:T(8,128)(2,1)}, bf16[96,4096]{1,0:T(8,128)(2,1)}, bf16[96,4096]{1,0:T(8,128)(2,1)}, bf16[96,4096]{1,0:T(8,128)(2,1)}, bf16[160...) custom-call(s32[1,1024]{1,0:T(1,128)} %fusion.14.target_ref, ...), custom_call_target="tpu_custom_call" | custom-call | flops 8589934592 | bytes 16777216 | tf_op jit(solution)/shard_map/pack_rows/pallas_call | solution.py:45
  21.2 1.5 collective-permute-start.5
  22.8 1.5 collective-permute-start.4
  24.7 0.6 pad_add_fusion.place_ref
  25.3 30.0 %project_half.3 = (bf16[1024,2048]{1,0:T(8,128)(2,1)}, bf16[1024,512]{1,0:T(8,128)(2,1)}) custom-call(s32[2]{0:T(128)} %pad_add_fusion.place_ref, bf16[1024,4096]{1,0:T(8,128)(2,1)} %x_ref.4, bf16[4096,4096]{1,0:T(8,128)(2,1)} %w_ref.5), custom_call_target="tpu_custom_call" | custom-call | flops 21474836480 | bytes 34603008 | tf_op jit(solution)/shard_map/project_half/pallas_call | solution.py:88
  55.4 1.6 collective-permute-start.3
  57.0 1.5 collective-permute-start.10
  58.5 1.5 collective-permute-start.9
  60.0 4.4 %join_rows.1 = bf16[384,4096]{1,0:T(8,128)(2,1)} custom-call(bf16[96,4096]{1,0:T(8,128)(2,1)} %get-tuple-element.69.refs_0_, bf16[96,4096]{1,0:T(8,128)(2,1)} %collective-permute-done.4.refs_1_, bf16[96,4096]{1,0:T(8,128)(2,1)} %copy-done, bf16[96,4096]{1,0:T(8,128)(2,1)} %collective-permute-done.6.refs_3_), custom_call_target="tpu_custom_call" | custom-call | bytes 6291456 | tf_op jit(solution)/shard_map/join_rows/pallas_call | solution.py:284
  64.4 2.3 %slice.18 = bf16[2,64,4096]{2,1,0:T(8,128)(2,1)} slice(bf16[4,64,4096]{2,1,0:T(8,128)(2,1)} %collective-permute-done.2.refs_6_.refs_8_), slice={[0:2], [0:64], [0:4096]} | slice | bytes 2097152 | tf_op jit(solution)/shard_map/slice | solution.py:366
  66.7 12.0 %project_half.4.rest_1_ = bf16[1024,768]{1,0:T(8,128)(2,1)} custom-call(s32[1]{0:T(128)} %bitcast.6.place_ref, bf16[1024,4096]{1,0:T(8,128)(2,1)} %x_ref.4, bf16[4096,4096]{1,0:T(8,128)(2,1)} %w_ref.5), custom_call_target="tpu_custom_call" | custom-call | flops 6442450944 | bytes 16252928 | tf_op jit(solution)/shard_map/project_half/pallas_call | solution.py:88
  79.1 1.3 collective-permute-start.8
  80.4 1.7 collective-permute-start.7
  82.1 8.7 %collective-permute-start.17 = (bf16[384,4096]{1,0:T(8,128)(2,1)}, bf16[384,4096]{1,0:T(8,128)(2,1)}, u32[]{:S(2)}, u32[]{:S(2)}) collective-permute-start(bf16[384,4096]{1,0:T(8,128)(2,1)} %join_rows.1), channel_id=1, source_target_pairs={{0,8},{2,10},{4,12},{6,14},{24,16},{26,18},{28,20},{30,22},{1,9},{... | collective-permute-start | bytes 9437192 | tf_op jit(solution)/shard_map/ppermute | solution.py:326
  90.8 1.5 collective-permute-start.12
  92.4 12.0 %project_half.5.rest_2_ = bf16[1024,768]{1,0:T(8,128)(2,1)} custom-call(s32[1]{0:T(128)} %bitcast.7.place_ref, bf16[1024,4096]{1,0:T(8,128)(2,1)} %x_ref.4, bf16[4096,4096]{1,0:T(8,128)(2,1)} %w_ref.5), custom_call_target="tpu_custom_call" | custom-call | flops 6442450944 | bytes 16252928 | tf_op jit(solution)/shard_map/project_half/pallas_call | solution.py:88
  104.4 1.3 collective-permute-start.11
  105.7 2.0 collective-permute-start.18
  107.8 11.9 %collective-permute-done.12.refs_3_ = bf16[160,4096]{1,0:T(8,128)(2,1)} collective-permute-done((bf16[160,4096]{1,0:T(8,128)(2,1)}, bf16[160,4096]{1,0:T(8,128)(2,1)}, u32[]{:S(2)}, u32[]{:S(2)}) %collective-permute-start.12) | collective-permute-done | bytes 1310752 | tf_op jit(solution)/shard_map/ppermute | solution.py:326
  119.7 8.6 %down_rows.2.refs_0_ = f32[640,64]{1,0:T(8,128)} custom-call(bf16[160,4096]{1,0:T(8,128)(2,1)} %get-tuple-element.63.refs_0_, bf16[160,4096]{1,0:T(8,128)(2,1)} %collective-permute-done.9.refs_1_, bf16[160,4096]{1,0:T(8,128)(2,1)} %collective-permute-done.10.refs_2_, bf16[160,4096]{1,0:T(8,128)(2,1)} %collective-permute-done.12.refs_3_, ...), custom_call_target="tpu_custom_call" | custom-call | flops 1342177280 | bytes 10485760 | tf_op jit(solution)/shard_map/down_rows/pallas_call | solution.py:178
  128.3 1.3 collective-permute-start.13
  129.7 1.8 collective-permute-done.14.refs_1_
  131.5 0.7 copy-done.4
  132.2 5.2 %lift_rows.2 = (bf16[160,2048]{1,0:T(8,128)(2,1)}, bf16[160,2048]{1,0:T(8,128)(2,1)}, bf16[160,2048]{1,0:T(8,128)(2,1)}, bf16[160,2048]{1,0:T(8,128)(2,1)}) custom-call(f32[640,64]{1,0:T(8,128)} %down_rows.2.refs_0_, f32[640,64]{1,0:T(8,128)} %copy-done.4, bf16[4,64,2048]{2,1,0:T(8,128)(2,1)} %refs_2_.1, ...), custom_call_target="tpu_custom_call" | custom-call | flops 671088640 | bytes 5242880 | tf_op jit(solution)/shard_map/lift_rows/pallas_call | solution.py:220
  137.4 1.0 collective-permute-start.15
  138.3 1.5 collective-permute-start.16
  139.9 14.5 %collective-permute-done.15.rest_5_ = bf16[160,2048]{1,0:T(8,128)(2,1)S(1)} collective-permute-done((bf16[160,2048]{1,0:T(8,128)(2,1)}, bf16[160,2048]{1,0:T(8,128)(2,1)S(1)}, u32[]{:S(2)}, u32[]{:S(2)}) %collective-permute-start.15) | collective-permute-done | bytes 655392 | tf_op jit(solution)/shard_map/ppermute | solution.py:326
  154.4 0.8 collective-permute-done.16.rest_6_
  155.2 8.4 %down_rows.3 = f32[768,64]{1,0:T(8,128)} custom-call(bf16[96,4096]{1,0:T(8,128)(2,1)} %get-tuple-element.69.refs_0_, bf16[96,4096]{1,0:T(8,128)(2,1)} %collective-permute-done.4.refs_1_, bf16[96,4096]{1,0:T(8,128)(2,1)} %copy-done, bf16[96,4096]{1,0:T(8,128)(2,1)} %collective-permute-done.6.refs_3_, ...), custom_call_target="tpu_custom_call" | custom-call | flops 1610612736 | bytes 9437184 | tf_op jit(solution)/shard_map/down_rows/pallas_call | solution.py:178
  163.7 1.9 collective-permute-done.19
  165.7 1.5 collective-permute-start.22
  167.2 1.1 add_convert_fusion.refs_0_
  168.3 1.5 collective-permute-start.20
  169.8 6.4 %collective-permute-done.20.refs_1_ = bf16[384,64]{1,0:T(8,128)(2,1)S(1)} collective-permute-done((bf16[384,64]{1,0:T(8,128)(2,1)S(1)}, bf16[384,64]{1,0:T(8,128)(2,1)S(1)}, u32[]{:S(2)}, u32[]{:S(2)}) %collective-permute-start.20) | collective-permute-done | bytes 49184 | tf_op jit(solution)/shard_map/ppermute | solution.py:326
  176.2 0.6 copy-done.5
  176.8 4.5 %lift_rows.3 = (bf16[96,2048]{1,0:T(8,128)(2,1)}, bf16[96,2048]{1,0:T(8,128)(2,1)}, bf16[96,2048]{1,0:T(8,128)(2,1)}, bf16[96,2048]{1,0:T(8,128)(2,1)}) custom-call(bf16[768,64]{1,0:T(8,128)(2,1)} %copy-done.1, bf16[384,64]{1,0:T(8,128)(2,1)} %copy-done.5, bf16[4,64,2048]{2,1,0:T(8,128)(2,1)} %collective-permute-done.3.refs_4_.refs_2_, ...), custom_call_target="tpu_custom_call" | custom-call | flops 402653184 | bytes 3145728 | tf_op jit(solution)/shard_map/lift_rows/pallas_call | solution.py:220
  181.4 1.5 collective-permute-start.23
  183.4 1.5 collective-permute-start.25
  185.3 1.3 slice.17.onehot_ref
  186.6 1.0 slice.16.onehot_ref
  187.6 0.9 copy-done.3
  188.5 10.8 %finish_rows.2.rest_0_ = bf16[1024,2048]{1,0:T(8,128)(2,1)} custom-call(bf16[1024,640]{1,0:T(8,128)(2,1)} %slice.17.onehot_ref, bf16[1024,512]{1,0:T(8,128)(2,1)} %get-tuple-element.73.rest_0_, bf16[1024,768]{1,0:T(8,128)(2,1)} %project_half.4.rest_1_, bf16[1024,768]{1,0:T(8,128)(2,1)} %project_half.5.rest_2_, ...), custom_call_target="tpu_custom_call" | custom-call | flops 2684354560 | bytes 16777216 | tf_op jit(solution)/shard_map/finish_rows/pallas_call | solution.py:261
  199.2 2.7 %collective-permute-done.24.rest_3_ = bf16[96,2048]{1,0:T(8,128)(2,1)} collective-permute-done((bf16[96,2048]{1,0:T(8,128)(2,1)}, bf16[96,2048]{1,0:T(8,128)(2,1)}, u32[]{:S(2)}, u32[]{:S(2)}) %collective-permute-start.24) | collective-permute-done | bytes 393248 | tf_op jit(solution)/shard_map/ppermute | solution.py:326
  202.0 6.8 %finish_rows.3 = bf16[1024,2048]{1,0:T(8,128)(2,1)} custom-call(bf16[1024,384]{1,0:T(8,128)(2,1)} %slice.16.onehot_ref, bf16[1024,2048]{1,0:T(8,128)(2,1)} %finish_rows.2.rest_0_, bf16[96,2048]{1,0:T(8,128)(2,1)} %get-tuple-element.72.rest_1_, bf16[96,2048]{1,0:T(8,128)(2,1)} %collective-permute-done.23.rest_2_, ...), custom_call_target="tpu_custom_call" | custom-call | flops 1610612736 | bytes 16777216 | tf_op jit(solution)/shard_map/finish_rows/pallas_call | solution.py:261
  (39 shorter events, 2.8 us)
Async XLA Ops:
  0.0 55.4 %collective-permute-start.2 = (bf16[4,64,4096]{2,1,0:T(8,128)(2,1)}, bf16[4,64,4096]{2,1,0:T(8,128)(2,1)}, u32[]{:S(2)}, u32[]{:S(2)}) collective-permute-start(bf16[4,64,4096]{2,1,0:T(8,128)(2,1)} %bitcast.8), channel_id=1, source_target_pairs={{8,16},{10,18},{12,20},{14,22},{16,8},{18,10},{20,12},{22,14},{9,1... | collective-permute-start | bytes 6291464 | tf_op jit(solution)/shard_map/ppermute | solution.py:326
  2.1 53.3 %collective-permute-start = (bf16[4,64,4096]{2,1,0:T(8,128)(2,1)}, bf16[4,64,4096]{2,1,0:T(8,128)(2,1)}, u32[]{:S(2)}, u32[]{:S(2)}) collective-permute-start(bf16[4,64,4096]{2,1,0:T(8,128)(2,1)} %bitcast.9), channel_id=1, source_target_pairs={{0,8},{2,10},{4,12},{6,14},{8,0},{10,2},{12,4},{14,6},{16,24},{18,... | collective-permute-start | bytes 6291464 | tf_op jit(solution)/shard_map/ppermute | solution.py:326
  21.2 35.8 %collective-permute-start.5 = (bf16[96,4096]{1,0:T(8,128)(2,1)}, bf16[96,4096]{1,0:T(8,128)(2,1)S(1)}, u32[]{:S(2)}, u32[]{:S(2)}) collective-permute-start(bf16[96,4096]{1,0:T(8,128)(2,1)} %get-tuple-element.52), channel_id=1, source_target_pairs={{0,4},{2,6},{4,0},{6,2},{8,12},{10,14},{12,8},{14,10},{16,20},{18,... | collective-permute-start | bytes 2359304 | tf_op jit(solution)/shard_map/ppermute | solution.py:326
  22.8 35.8 %collective-permute-start.4 = (bf16[96,4096]{1,0:T(8,128)(2,1)}, bf16[96,4096]{1,0:T(8,128)(2,1)}, u32[]{:S(2)}, u32[]{:S(2)}) collective-permute-start(bf16[96,4096]{1,0:T(8,128)(2,1)} %get-tuple-element.51), channel_id=1, source_target_pairs={{0,2},{2,0},{4,6},{6,4},{8,10},{10,8},{12,14},{14,12},{16,18},{18,... | collective-permute-start | bytes 2359304 | tf_op jit(solution)/shard_map/ppermute | solution.py:326
  24.3 35.8 %collective-permute-start.6 = (bf16[96,4096]{1,0:T(8,128)(2,1)}, bf16[96,4096]{1,0:T(8,128)(2,1)}, u32[]{:S(2)}, u32[]{:S(2)}) collective-permute-start(bf16[96,4096]{1,0:T(8,128)(2,1)} %get-tuple-element.53), channel_id=1, source_target_pairs={{0,6},{2,4},{4,2},{6,0},{8,14},{10,12},{12,10},{14,8},{16,22},{18,... | collective-permute-start | bytes 2359304 | tf_op jit(solution)/shard_map/ppermute | solution.py:326
  55.3 23.8 %collective-permute-start.1 = (bf16[4,64,2048]{2,1,0:T(8,128)(2,1)}, bf16[4,64,2048]{2,1,0:T(8,128)(2,1)}, u32[]{:S(2)}, u32[]{:S(2)}) collective-permute-start(bf16[4,64,2048]{2,1,0:T(8,128)(2,1)} %refs_2_.1), channel_id=1, source_target_pairs={{0,8},{2,10},{4,12},{6,14},{8,0},{10,2},{12,4},{14,6},{16,24},{18,... | collective-permute-start | bytes 3145736 | tf_op jit(solution)/shard_map/ppermute | solution.py:326
  55.4 25.0 %collective-permute-start.3 = (bf16[4,64,2048]{2,1,0:T(8,128)(2,1)}, bf16[4,64,2048]{2,1,0:T(8,128)(2,1)}, u32[]{:S(2)}, u32[]{:S(2)}) collective-permute-start(bf16[4,64,2048]{2,1,0:T(8,128)(2,1)} %refs_2_.1), channel_id=1, source_target_pairs={{8,16},{10,18},{12,20},{14,22},{16,8},{18,10},{20,12},{22,14},{9,1... | collective-permute-start | bytes 3145736 | tf_op jit(solution)/shard_map/ppermute | solution.py:326
  57.0 3.0 %copy-start = (bf16[96,4096]{1,0:T(8,128)(2,1)}, bf16[96,4096]{1,0:T(8,128)(2,1)S(1)}, u32[]{:S(2)}) copy-start(bf16[96,4096]{1,0:T(8,128)(2,1)S(1)} %collective-permute-done.5.refs_2_) | copy-start | bytes 2359300
  57.0 33.8 %collective-permute-start.10 = (bf16[160,4096]{1,0:T(8,128)(2,1)}, bf16[160,4096]{1,0:T(8,128)(2,1)}, u32[]{:S(2)}, u32[]{:S(2)}) collective-permute-start(bf16[160,4096]{1,0:T(8,128)(2,1)} %get-tuple-element.60), channel_id=1, source_target_pairs={{0,4},{2,6},{4,0},{6,2},{8,12},{10,14},{12,8},{14,10},{16,20},{18,... | collective-permute-start | bytes 3932168 | tf_op jit(solution)/shard_map/ppermute | solution.py:326
  58.5 32.3 %collective-permute-start.9 = (bf16[160,4096]{1,0:T(8,128)(2,1)}, bf16[160,4096]{1,0:T(8,128)(2,1)}, u32[]{:S(2)}, u32[]{:S(2)}) collective-permute-start(bf16[160,4096]{1,0:T(8,128)(2,1)} %get-tuple-element.58), channel_id=1, source_target_pairs={{0,2},{2,0},{4,6},{6,4},{8,10},{10,8},{12,14},{14,12},{16,18},{18,... | collective-permute-start | bytes 3932168 | tf_op jit(solution)/shard_map/ppermute | solution.py:326
  79.1 25.3 %collective-permute-start.8 = (bf16[2,64,4096]{2,1,0:T(8,128)(2,1)}, bf16[2,64,4096]{2,1,0:T(8,128)(2,1)}, u32[]{:S(2)}, u32[]{:S(2)}) collective-permute-start(bf16[2,64,4096]{2,1,0:T(8,128)(2,1)} %slice.18), channel_id=1, source_target_pairs={{8,0},{10,2},{12,4},{14,6},{16,24},{18,26},{20,28},{22,30},{9,1},{... | collective-permute-start | bytes 3145736 | tf_op jit(solution)/shard_map/ppermute | solution.py:326
  80.4 25.3 %collective-permute-start.7 = (bf16[4,64,2048]{2,1,0:T(8,128)(2,1)}, bf16[4,64,2048]{2,1,0:T(8,128)(2,1)}, u32[]{:S(2)}, u32[]{:S(2)}) collective-permute-start(bf16[4,64,2048]{2,1,0:T(8,128)(2,1)} %collective-permute-done.1.refs_3_), channel_id=1, source_target_pairs={{8,16},{10,18},{12,20},{14,22},{16,8},{18,10},{20,12},{22,14},{9,1... | collective-permute-start | bytes 3145736 | tf_op jit(solution)/shard_map/ppermute | solution.py:326
  82.1 73.0 %collective-permute-start.17 = (bf16[384,4096]{1,0:T(8,128)(2,1)}, bf16[384,4096]{1,0:T(8,128)(2,1)}, u32[]{:S(2)}, u32[]{:S(2)}) collective-permute-start(bf16[384,4096]{1,0:T(8,128)(2,1)} %join_rows.1), channel_id=1, source_target_pairs={{0,8},{2,10},{4,12},{6,14},{24,16},{26,18},{28,20},{30,22},{1,9},{... | collective-permute-start | bytes 9437192 | tf_op jit(solution)/shard_map/ppermute | solution.py:326
  90.8 28.8 %collective-permute-start.12 = (bf16[160,4096]{1,0:T(8,128)(2,1)}, bf16[160,4096]{1,0:T(8,128)(2,1)}, u32[]{:S(2)}, u32[]{:S(2)}) collective-permute-start(bf16[160,4096]{1,0:T(8,128)(2,1)} %get-tuple-element.65), channel_id=1, source_target_pairs={{0,6},{2,4},{4,2},{6,0},{8,14},{10,12},{12,10},{14,8},{16,22},{18,... | collective-permute-start | bytes 3932168 | tf_op jit(solution)/shard_map/ppermute | solution.py:326
  104.4 23.9 %collective-permute-start.11 = (bf16[4,64,2048]{2,1,0:T(8,128)(2,1)}, bf16[4,64,2048]{2,1,0:T(8,128)(2,1)}, u32[]{:S(2)}, u32[]{:S(2)}) collective-permute-start(bf16[4,64,2048]{2,1,0:T(8,128)(2,1)} %collective-permute-done.3.refs_4_.refs_2_), channel_id=1, source_target_pairs={{8,0},{10,2},{12,4},{14,6},{16,24},{18,26},{20,28},{22,30},{9,1},{... | collective-permute-start | bytes 3145736 | tf_op jit(solution)/shard_map/ppermute | solution.py:326
  105.7 49.4 %collective-permute-start.18 = (bf16[4,64,4096]{2,1,0:T(8,128)(2,1)}, bf16[4,64,4096]{2,1,0:T(8,128)(2,1)}, u32[]{:S(2)}, u32[]{:S(2)}) collective-permute-start(bf16[4,64,4096]{2,1,0:T(8,128)(2,1)} %collective-permute-done.refs_5_), channel_id=1, source_target_pairs={{8,16},{10,18},{12,20},{14,22},{16,8},{18,10},{20,12},{22,14},{9,1... | collective-permute-start | bytes 6291464 | tf_op jit(solution)/shard_map/ppermute | solution.py:326
  128.3 26.9 %collective-permute-start.13 = (bf16[4,64,2048]{2,1,0:T(8,128)(2,1)}, bf16[4,64,2048]{2,1,0:T(8,128)(2,1)}, u32[]{:S(2)}, u32[]{:S(2)}) collective-permute-start(bf16[4,64,2048]{2,1,0:T(8,128)(2,1)} %collective-permute-done.7.refs_4_), channel_id=1, source_target_pairs={{8,0},{10,2},{12,4},{14,6},{16,24},{18,26},{20,28},{22,30},{9,1},{... | collective-permute-start | bytes 3145736 | tf_op jit(solution)/shard_map/ppermute | solution.py:326
  129.6 1.9 collective-permute-start.14
  131.5 0.7 copy-start.4
  137.4 17.0 %collective-permute-start.15 = (bf16[160,2048]{1,0:T(8,128)(2,1)}, bf16[160,2048]{1,0:T(8,128)(2,1)S(1)}, u32[]{:S(2)}, u32[]{:S(2)}) collective-permute-start(bf16[160,2048]{1,0:T(8,128)(2,1)} %get-tuple-element.67), channel_id=1, source_target_pairs={{0,2},{2,0},{4,6},{6,4},{8,10},{10,8},{12,14},{14,12},{16,18},{18,... | collective-permute-start | bytes 1966088 | tf_op jit(solution)/shard_map/ppermute | solution.py:326
  138.3 16.8 %collective-permute-start.16 = (bf16[160,2048]{1,0:T(8,128)(2,1)}, bf16[160,2048]{1,0:T(8,128)(2,1)}, u32[]{:S(2)}, u32[]{:S(2)}) collective-permute-start(bf16[160,2048]{1,0:T(8,128)(2,1)} %get-tuple-element.68), channel_id=1, source_target_pairs={{0,4},{2,6},{4,0},{6,2},{8,12},{10,14},{12,8},{14,10},{16,20},{18,... | collective-permute-start | bytes 1966088 | tf_op jit(solution)/shard_map/ppermute | solution.py:326
  154.4 9.2 %copy-start.2 = (bf16[160,2048]{1,0:T(8,128)(2,1)}, bf16[160,2048]{1,0:T(8,128)(2,1)S(1)}, u32[]{:S(2)}) copy-start(bf16[160,2048]{1,0:T(8,128)(2,1)S(1)} %collective-permute-done.15.rest_5_) | copy-start | bytes 1966084
  163.6 2.0 collective-permute-start.19
  165.6 22.0 %collective-permute-start.21 = (bf16[1024,2048]{1,0:T(8,128)(2,1)}, bf16[1024,2048]{1,0:T(8,128)(2,1)}, u32[]{:S(2)}, u32[]{:S(2)}) collective-permute-start(bf16[1024,2048]{1,0:T(8,128)(2,1)} %get-tuple-element.74), channel_id=1, source_target_pairs={{0,1},{1,0},{2,3},{3,2},{4,5},{5,4},{6,7},{7,6},{8,9},{9,8},{10,11... | collective-permute-start | bytes 12582920 | tf_op jit(solution)/shard_map/ppermute | solution.py:380
  165.7 21.9 %collective-permute-start.22 = (bf16[160,2048]{1,0:T(8,128)(2,1)}, bf16[160,2048]{1,0:T(8,128)(2,1)S(1)}, u32[]{:S(2)}, u32[]{:S(2)}) collective-permute-start(bf16[160,2048]{1,0:T(8,128)(2,1)} %get-tuple-element.77), channel_id=1, source_target_pairs={{0,6},{2,4},{4,2},{6,0},{8,14},{10,12},{12,10},{14,8},{16,22},{18,... | collective-permute-start | bytes 1966088 | tf_op jit(solution)/shard_map/ppermute | solution.py:326
  168.3 7.9 %copy-start.1 = (bf16[768,64]{1,0:T(8,128)(2,1)}, bf16[768,64]{1,0:T(8,128)(2,1)S(1)}, u32[]{:S(2)}) copy-start(bf16[768,64]{1,0:T(8,128)(2,1)S(1)} %add_convert_fusion.refs_0_) | copy-start | bytes 294916
  168.3 7.9 %collective-permute-start.20 = (bf16[384,64]{1,0:T(8,128)(2,1)S(1)}, bf16[384,64]{1,0:T(8,128)(2,1)S(1)}, u32[]{:S(2)}, u32[]{:S(2)}) collective-permute-start(bf16[384,64]{1,0:T(8,128)(2,1)S(1)} %slice.19), channel_id=1, source_target_pairs={{8,0},{10,2},{12,4},{14,6},{16,24},{18,26},{20,28},{22,30},{9,1},{... | collective-permute-start | bytes 147464 | tf_op jit(solution)/shard_map/ppermute | solution.py:326
  176.2 0.6 copy-start.5
  181.4 17.9 %collective-permute-start.23 = (bf16[96,2048]{1,0:T(8,128)(2,1)}, bf16[96,2048]{1,0:T(8,128)(2,1)}, u32[]{:S(2)}, u32[]{:S(2)}) collective-permute-start(bf16[96,2048]{1,0:T(8,128)(2,1)} %get-tuple-element.78), channel_id=1, source_target_pairs={{0,2},{2,0},{4,6},{6,4},{8,10},{10,8},{12,14},{14,12},{16,18},{18,... | collective-permute-start | bytes 1179656 | tf_op jit(solution)/shard_map/ppermute | solution.py:326
  182.9 19.0 %collective-permute-start.24 = (bf16[96,2048]{1,0:T(8,128)(2,1)}, bf16[96,2048]{1,0:T(8,128)(2,1)}, u32[]{:S(2)}, u32[]{:S(2)}) collective-permute-start(bf16[96,2048]{1,0:T(8,128)(2,1)} %get-tuple-element.79), channel_id=1, source_target_pairs={{0,4},{2,6},{4,0},{6,2},{8,12},{10,14},{12,8},{14,10},{16,20},{18,... | collective-permute-start | bytes 1179656 | tf_op jit(solution)/shard_map/ppermute | solution.py:326
  183.4 18.5 %collective-permute-start.25 = (bf16[96,2048]{1,0:T(8,128)(2,1)}, bf16[96,2048]{1,0:T(8,128)(2,1)}, u32[]{:S(2)}, u32[]{:S(2)}) collective-permute-start(bf16[96,2048]{1,0:T(8,128)(2,1)} %get-tuple-element.80), channel_id=1, source_target_pairs={{0,6},{2,4},{4,2},{6,0},{8,14},{10,12},{12,10},{14,8},{16,22},{18,... | collective-permute-start | bytes 1179656 | tf_op jit(solution)/shard_map/ppermute | solution.py:326
  187.6 0.9 copy-start.3
